TPU v7x, 256 devices: a whole 4x4x8 slice. The times are simulated.
256 devices in a mesh: mem: 8 (over y, z_hi), samp: 32 (over x, z_lo, core).
Axes of the slice: x: 4, y: 4, z: 8 (z_hi: 2, z_lo: 4; z = z_hi * 4 + z_lo), core: 2. Of those that a mesh axis runs over, the one named last changes fastest.
Arguments:
- first_plane: bfloat16 [65536, 16384], P('samp', 'mem')
- second_plane: bfloat16 [16384, 16384], P('samp', 'mem')
- panel_owner: int32 [2], replicated, may hold values from 0 to 31
Outputs:
- covariance: float32 [1024, 65536], P('mem', 'samp')
All inputs are finite; a program needn't handle non-finite values.
Results may differ from a plain program's by a relative error of at most 0.0004.
The roundings to bfloat16 on the way count: a program that leaves them out, or rounds other values in their place, can miss the bound.
Values may be sent and summed in bfloat16 or wider, within the bound.
No kernel may reach another device: no remote copies, remote signals or barrier semaphores. Data moves between devices by JAX's collectives and lax.ppermute only.
A program may use at most 64 MiB of HBM per device.

v0:
```python
import jax
import jax.numpy as jnp
from jax import lax
from jax.sharding import PartitionSpec as P

F32 = jnp.float32
BF16 = jnp.bfloat16
WIRE = jnp.float16
CHUNKS = 2


def swap(value, axis, bits):
    size = lax.axis_size(axis)
    return lax.ppermute(value, axis, [(i, i ^ bits) for i in range(size)])


def pick(index, options):
    result = options[-1]
    for i in range(len(options) - 2, -1, -1):
        result = jnp.where(index == i, options[i], result)
    return result


def row_stats(rows):
    wide = rows.astype(F32)
    return jnp.stack([jnp.sum(wide, -1), jnp.max(wide, -1), jnp.max(-wide, -1)])


def merge(parts):
    total = parts[0]
    for part in parts[1:]:
        total = jnp.concatenate([total[:1] + part[:1], jnp.maximum(total[1:], part[1:])])
    return total


def after(value, others):
    return lax.optimization_barrier((value, others))[0]


def per_device(first_plane, second_plane, panel_owner):
    samples, shard = first_plane.shape
    members = shard * lax.axis_size("mem")
    samp, mem = lax.axis_index("samp"), lax.axis_index("mem")
    my_x, my_z, my_core = samp >> 3, (samp >> 1) & 3, samp & 1
    my_y, my_zh = mem >> 1, mem & 1
    own_x, own_z, own_core = panel_owner >> 3, (panel_owner >> 1) & 3, panel_owner & 1

    by_x = second_plane.reshape(4, 128, shard)
    piece = lambda bits: lax.dynamic_index_in_dim(by_x, my_x ^ bits, 0, keepdims=False)
    from_x = [piece(0)] + [swap(piece(bits), "samp", 8 * bits) for bits in (1, 2, 3)]
    first_plane = after(first_plane, from_x[0])
    first_local = row_stats(first_plane)
    halves = [
        pick(my_x ^ own_x[p], from_x).reshape(CHUNKS, 2, 4, -1, shard) for p in range(2)
    ]
    half = lambda core: jnp.stack(
        [lax.dynamic_index_in_dim(h, core, 1, keepdims=False) for h in halves]
    )
    kept, got = half(my_core), swap(half(1 - my_core), "samp", 1)
    column = jnp.stack(
        [jnp.where(my_core == own_core[p], kept[p], got[p]) for p in range(2)]
    )
    eighth = column.shape[3]
    piece_z = lambda bits: lax.dynamic_index_in_dim(column, my_z ^ bits, 2, keepdims=False)
    from_z = [piece_z(0)] + [swap(piece_z(bits), "samp", 2 * bits) for bits in (1, 2, 3)]

    column_local = row_stats(column).reshape(3, -1)
    stats = jnp.concatenate([first_local, column_local], axis=1)
    stats = merge([stats] + [swap(stats, "mem", bits) for bits in (2, 4, 6)])
    stats = after(stats, from_z[1:])
    stats = merge([stats, swap(stats, "mem", 1)])
    mean, span = stats[0] / members, stats[1] + stats[2]
    first_mean = mean[:samples]
    facts = jnp.stack([mean[samples:], span[samples:]]).reshape((2,) + column.shape[:-1])

    mine = jnp.stack([pick(my_z ^ own_z[p], [f[p] for f in from_z]) for p in range(2)])
    parts = [mine] + [swap(mine, "samp", 2 * bits) for bits in (1, 2, 3)]
    facts = after(facts, parts[1])
    facts_z = [facts] + [swap(facts, "samp", 2 * bits) for bits in (1, 2, 3)]
    facts = jnp.stack([pick(my_z ^ own_z[p], [f[:, p] for f in facts_z]) for p in range(2)], 1)
    line = jnp.stack([pick(my_z ^ place, parts) for place in range(4)], 2)
    line = (line.astype(F32) - facts[0][..., None]).astype(BF16)
    tiles = 8
    bound = jnp.max(facts[1]) * 1.02
    mark = jnp.broadcast_to(bound, (1, eighth, shard)).astype(BF16)

    first_anom = (first_plane.astype(F32) - first_mean[:, None]).astype(BF16)
    rows = 4 * eighth
    gathered = []
    for chunk in range(CHUNKS):
        sent = line[:, chunk].reshape(tiles, eighth, shard)
        if chunk == 0:
            sent = jnp.concatenate([sent, mark])
        else:
            sent = after(sent, gathered[0][1])
        gathered.append([sent] + [swap(sent, "samp", 8 * bits) for bits in (1, 2, 3)])

    blocks, arrived = [], []
    for chunk in range(CHUNKS):
        if chunk > 0:
            gathered[chunk] = after(gathered[chunk], arrived[-1][0])
        near = jnp.stack(gathered[chunk])
        far = swap(near, "samp", 1)
        if chunk == 0:
            marks = jnp.stack([near[:, tiles, 0, :128], far[:, tiles, 0, :128]])
            shrink_first = 4.0 / jnp.maximum(jnp.max(span[:samples]), 1e-30)
            shrink_panel = 1.0 / jnp.maximum(jnp.max(marks.astype(F32)), 1e-30)
            grow_first, grow_panel = 1.0 / shrink_first, 1.0 / shrink_panel
        panel_anom = jnp.stack([near[:, :tiles], far[:, :tiles]])
        shares = lax.dot_general(
            panel_anom.reshape(16 * rows, shard),
            first_anom,
            (((1,), (1,)), ((), ())),
            preferred_element_type=F32,
        ).reshape(2, 2, 2, 2, rows, samples)

        def for_y(dest):
            start = (0, (dest & 1) ^ (my_x >> 1), 0, dest >> 1, 0, 0)
            block = lax.dynamic_slice(shares, start, (2, 1, 2, 1, rows, samples))
            return block.reshape(2, 2, rows, samples)

        sent = [
            (for_y(my_y ^ bits) * shrink_first * shrink_panel).astype(WIRE) for bits in (1, 2, 3)
        ]
        arrived.append([swap(sent[bits - 1], "mem", 2 * bits) for bits in (1, 2, 3)])
        blocks.append(for_y(my_y))

    results = []
    for chunk in range(CHUNKS):
        if chunk + 1 < CHUNKS:
            arrived[chunk] = after(arrived[chunk], sent)
        total = blocks[chunk]
        for value in arrived[chunk]:
            total += value.astype(F32) * grow_panel * grow_first
        for_z = lambda dest: lax.dynamic_index_in_dim(total, dest ^ (my_x & 1), 1, keepdims=False)
        other = (for_z(1 - my_zh) * shrink_first * shrink_panel).astype(WIRE)
        total = for_z(my_zh) + swap(other, "mem", 1).astype(F32) * grow_panel * grow_first
        results += [pick(my_core ^ core, [total[0], total[1]]) / (members - 1) for core in range(2)]
    return jnp.concatenate(results, axis=0)


def solution(mesh):
    in_specs = (P("samp", "mem"), P("samp", "mem"), P())
    out_specs = P("mem", "samp")
    return jax.shard_map(
        per_device, mesh=mesh, in_specs=in_specs, out_specs=out_specs, check_vma=False
    )
```

profile of v0, /device:TPU:32, one launch (start us, length us, event | category | flops | bytes accessed | tf_op | source)
XLA Modules:
  0.0 216.7 jit_solution(5598451506954405545)
XLA Ops:
  0.0 1.5 dynamic-slice_bitcast_fusion
  1.5 1.6 collective-permute-start
  3.0 2.7 %collective-permute-start.1 = (bf16[128,2048]{1,0:T(8,128)(2,1)S(1)}, bf16[128,2048]{1,0:T(8,128)(2,1)S(1)}, u32[]{:S(2)}, u32[]{:S(2)}) collective-permute-start(bf16[128,2048]{1,0:T(8,128)(2,1)S(1)} %get-tuple-element.42), channel_id=1, source_target_pairs={{0,16},{1,17},{2,18},{3,19},{4,20},{5,21},{6,22},{7,23},{8,24},{9,... | collective-permute-start | bytes 1572872 | tf_op jit(solution)/shard_map/ppermute | solution.py:14
  6.2 0.7 shift-right-arithmetic_and_fusion
  6.9 0.6 fusion.61
  8.9 0.7 fusion.59
  12.1 4.2 %collective-permute-done = bf16[128,2048]{1,0:T(8,128)(2,1)S(1)} collective-permute-done((bf16[128,2048]{1,0:T(8,128)(2,1)S(1)}, bf16[128,2048]{1,0:T(8,128)(2,1)S(1)}, u32[]{:S(2)}, u32[]{:S(2)}) %collective-permute-start) | collective-permute-done | bytes 524320 | tf_op jit(solution)/shard_map/ppermute | solution.py:14
  16.4 12.4 %collective-permute-done.1 = bf16[128,2048]{1,0:T(8,128)(2,1)S(1)} collective-permute-done((bf16[128,2048]{1,0:T(8,128)(2,1)S(1)}, bf16[128,2048]{1,0:T(8,128)(2,1)S(1)}, u32[]{:S(2)}, u32[]{:S(2)}) %collective-permute-start.1) | collective-permute-done | bytes 524320 | tf_op jit(solution)/shard_map/ppermute | solution.py:14
  28.7 2.6 %collective-permute-done.2 = bf16[128,2048]{1,0:T(8,128)(2,1)S(1)} collective-permute-done((bf16[128,2048]{1,0:T(8,128)(2,1)S(1)}, bf16[128,2048]{1,0:T(8,128)(2,1)S(1)}, u32[]{:S(2)}, u32[]{:S(2)}) %collective-permute-start.2) | collective-permute-done | bytes 524320 | tf_op jit(solution)/shard_map/ppermute | solution.py:14
  31.3 1.2 select_select_fusion.1
  32.8 4.6 %reduce_max.90 = bf16[2048]{0:T(1024)(128)(2,1)S(1)} reduce(bf16[2048,2048]{1,0:T(8,128)(2,1)} %param.3, bf16[]{:T(256)} %constant.77.clone.1), dimensions={1}, to_apply=%region_1.2 | reduce | flops 4192256 | bytes 8392706 | tf_op jit(solution)/shard_map/reduce_max | solution.py:26
  37.4 6.0 %convert_reduce_fusion = (f32[2048]{0:T(1024)S(1)}, f32[2048]{0:T(1024)S(1)}) fusion(bf16[2048,2048]{1,0:T(8,128)(2,1)} %param.3), kind=kLoop, calls=%fused_computation.2 | loop fusion | flops 16773120 | bytes 8404992 | tf_op jit(solution)/shard_map/reduce_sum | solution.py:26
  44.2 1.7 collective-permute-start.10
  45.9 2.9 %collective-permute-start.11 = (f32[3,2176]{1,0:T(4,128)S(1)}, f32[3,2176]{1,0:T(4,128)S(1)}, u32[]{:S(2)}, u32[]{:S(2)}) collective-permute-start(f32[3,2176]{1,0:T(4,128)S(1)} %maximum_maximum_fusion), channel_id=1, source_target_pairs={{0,128},{32,160},{64,192},{96,224},{128,0},{160,32},{192,64},{224,... | collective-permute-start | bytes 78344 | tf_op jit(solution)/shard_map/ppermute | solution.py:14
  49.3 3.3 %collective-permute-start.5 = (bf16[2,2,8,2048]{3,2,1,0:T(8,128)(2,1)S(1)}, bf16[2,2,8,2048]{3,2,1,0:T(8,128)(2,1)S(1)}, u32[]{:S(2)}, u32[]{:S(2)}) collective-permute-start(bf16[2,2,8,2048]{3,2,1,0:T(8,128)(2,1)S(1)} %get-tuple-element.55), channel_id=1, source_target_pairs={{0,4},{1,5},{2,6},{3,7},{4,0},{5,1},{6,2},{7,3},{8,12},{9,13},{10,... | collective-permute-start | bytes 393224 | tf_op jit(solution)/shard_map/ppermute | solution.py:14
  53.0 0.9 collective-permute-done.12
  54.3 7.7 %collective-permute-done.5 = bf16[2,2,8,2048]{3,2,1,0:T(8,128)(2,1)S(1)} collective-permute-done((bf16[2,2,8,2048]{3,2,1,0:T(8,128)(2,1)S(1)}, bf16[2,2,8,2048]{3,2,1,0:T(8,128)(2,1)S(1)}, u32[]{:S(2)}, u32[]{:S(2)}) %collective-permute-start.5) | collective-permute-done | bytes 131104 | tf_op jit(solution)/shard_map/ppermute | solution.py:14
  62.0 2.5 %collective-permute-done.6 = bf16[2,2,8,2048]{3,2,1,0:T(8,128)(2,1)S(1)} collective-permute-done((bf16[2,2,8,2048]{3,2,1,0:T(8,128)(2,1)S(1)}, bf16[2,2,8,2048]{3,2,1,0:T(8,128)(2,1)S(1)}, u32[]{:S(2)}, u32[]{:S(2)}) %collective-permute-start.6) | collective-permute-done | bytes 131104 | tf_op jit(solution)/shard_map/ppermute | solution.py:14
  64.5 6.0 %collective-permute-start.13 = (f32[3,2176]{1,0:T(4,128)S(1)}, f32[3,2176]{1,0:T(4,128)S(1)}, u32[]{:S(2)}, u32[]{:S(2)}) collective-permute-start(f32[3,2176]{1,0:T(4,128)S(1)} %pad_maximum_fusion.6), channel_id=1, source_target_pairs={{0,32},{32,0},{64,96},{96,64},{128,160},{160,128},{192,224},{224,1... | collective-permute-start | bytes 78344 | tf_op jit(solution)/shard_map/ppermute | solution.py:14
  70.7 2.5 %collective-permute-start.8 = (bf16[2,2,8,2048]{3,2,1,0:T(8,128)(2,1)S(1)}, bf16[2,2,8,2048]{3,2,1,0:T(8,128)(2,1)S(1)}, u32[]{:S(2)}, u32[]{:S(2)}) collective-permute-start(bf16[2,2,8,2048]{3,2,1,0:T(8,128)(2,1)S(1)} %pad_maximum_fusion.5), channel_id=1, source_target_pairs={{0,4},{1,5},{2,6},{3,7},{4,0},{5,1},{6,2},{7,3},{8,12},{9,13},{10,... | collective-permute-start | bytes 393224 | tf_op jit(solution)/shard_map/ppermute | solution.py:14
  73.2 1.0 collective-permute-start.9
  74.7 2.4 %collective-permute-done.7 = bf16[2,2,8,2048]{3,2,1,0:T(8,128)(2,1)S(1)} collective-permute-done((bf16[2,2,8,2048]{3,2,1,0:T(8,128)(2,1)S(1)}, bf16[2,2,8,2048]{3,2,1,0:T(8,128)(2,1)S(1)}, u32[]{:S(2)}, u32[]{:S(2)}) %collective-permute-start.7) | collective-permute-done | bytes 131104 | tf_op jit(solution)/shard_map/ppermute | solution.py:14
  77.1 0.7 collective-permute-start.14
  77.8 1.8 collective-permute-start.15
  79.6 1.0 collective-permute-start.16
  80.6 1.5 collective-permute-done.8
  82.1 3.2 %collective-permute-done.9 = bf16[2,2,8,2048]{3,2,1,0:T(8,128)(2,1)S(1)} collective-permute-done((bf16[2,2,8,2048]{3,2,1,0:T(8,128)(2,1)S(1)}, bf16[2,2,8,2048]{3,2,1,0:T(8,128)(2,1)S(1)}, u32[]{:S(2)}, u32[]{:S(2)}) %collective-permute-start.9) | collective-permute-done | bytes 131104 | tf_op jit(solution)/shard_map/ppermute | solution.py:14
  85.7 0.6 fusion.51
  87.3 1.9 collective-permute-start.18
  89.3 2.8 %collective-permute-start.19 = (bf16[9,8,2048]{2,1,0:T(8,128)(2,1)S(1)}, bf16[9,8,2048]{2,1,0:T(8,128)(2,1)S(1)}, u32[]{:S(2)}, u32[]{:S(2)}) collective-permute-start(bf16[9,8,2048]{2,1,0:T(8,128)(2,1)S(1)} %get-tuple-element.62), channel_id=1, source_target_pairs={{0,24},{1,25},{2,26},{3,27},{4,28},{5,29},{6,30},{7,31},{8,16},{9,... | collective-permute-start | bytes 884744 | tf_op jit(solution)/shard_map/ppermute | solution.py:14
  92.0 5.2 %collective-permute-done.17 = bf16[9,8,2048]{2,1,0:T(8,128)(2,1)S(1)} collective-permute-done((bf16[9,8,2048]{2,1,0:T(8,128)(2,1)S(1)}, bf16[9,8,2048]{2,1,0:T(8,128)(2,1)S(1)}, u32[]{:S(2)}, u32[]{:S(2)}) %collective-permute-start.17) | collective-permute-done | bytes 294944 | tf_op jit(solution)/shard_map/ppermute | solution.py:14
  97.3 3.6 %collective-permute-done.18 = bf16[9,8,2048]{2,1,0:T(8,128)(2,1)S(1)} collective-permute-done((bf16[9,8,2048]{2,1,0:T(8,128)(2,1)S(1)}, bf16[9,8,2048]{2,1,0:T(8,128)(2,1)S(1)}, u32[]{:S(2)}, u32[]{:S(2)}) %collective-permute-start.18) | collective-permute-done | bytes 294944 | tf_op jit(solution)/shard_map/ppermute | solution.py:14
  100.9 2.6 %collective-permute-done.19 = bf16[9,8,2048]{2,1,0:T(8,128)(2,1)S(1)} collective-permute-done((bf16[9,8,2048]{2,1,0:T(8,128)(2,1)S(1)}, bf16[9,8,2048]{2,1,0:T(8,128)(2,1)S(1)}, u32[]{:S(2)}, u32[]{:S(2)}) %collective-permute-start.19) | collective-permute-done | bytes 294944 | tf_op jit(solution)/shard_map/ppermute | solution.py:14
  103.7 0.6 slice_reduce_fusion
  105.2 0.6 slice_reduce_fusion.2
  105.8 0.9 collective-permute-done.20
  106.7 1.4 slice_reduce_fusion.1
  109.3 1.3 slice.273
  110.6 7.1 %fusion.5 = f32[2,2,2,2,32,2048]{5,4,3,2,1,0:T(8,128)S(1)} fusion(bf16[2048,2048]{1,0:T(8,128)(2,1)} %param.3, f32[2048]{0:T(1024)S(1)} %bitcast.151, bf16[1,2,2,2,32,2048]{5,4,3,2,1,0:T(8,128)(2,1)S(1)} %bitcast.136, bf16[1,2,2,2,32,2048]{5,4,3,2,1,0:T(8,128)(2,1)S(1)} %bitcast.135), kind=kOutput, calls=%fused_computation.7 | convolution fusion | flops 4308598784 | bytes 14688256 | tf_op jit(solution)/shard_map/dot_general | solution.py:110
  117.8 1.2 fusion.27
  119.3 4.2 %collective-permute-start.25 = (bf16[8,8,2048]{2,1,0:T(8,128)(2,1)S(1)}, bf16[8,8,2048]{2,1,0:T(8,128)(2,1)S(1)}, u32[]{:S(2)}, u32[]{:S(2)}) collective-permute-start(bf16[8,8,2048]{2,1,0:T(8,128)(2,1)S(1)} %bitcast.138), channel_id=1, source_target_pairs={{0,16},{1,17},{2,18},{3,19},{4,20},{5,21},{6,22},{7,23},{8,24},{9,... | collective-permute-start | bytes 786440 | tf_op jit(solution)/shard_map/ppermute | solution.py:14
  124.0 4.5 %collective-permute-done.24 = bf16[8,8,2048]{2,1,0:T(8,128)(2,1)S(1)} collective-permute-done((bf16[8,8,2048]{2,1,0:T(8,128)(2,1)S(1)}, bf16[8,8,2048]{2,1,0:T(8,128)(2,1)S(1)}, u32[]{:S(2)}, u32[]{:S(2)}) %collective-permute-start.24) | collective-permute-done | bytes 262176 | tf_op jit(solution)/shard_map/ppermute | solution.py:14
  128.5 7.1 %collective-permute-done.25 = bf16[8,8,2048]{2,1,0:T(8,128)(2,1)S(1)} collective-permute-done((bf16[8,8,2048]{2,1,0:T(8,128)(2,1)S(1)}, bf16[8,8,2048]{2,1,0:T(8,128)(2,1)S(1)}, u32[]{:S(2)}, u32[]{:S(2)}) %collective-permute-start.25) | collective-permute-done | bytes 262176 | tf_op jit(solution)/shard_map/ppermute | solution.py:14
  135.6 2.6 %collective-permute-done.26 = bf16[8,8,2048]{2,1,0:T(8,128)(2,1)S(1)} collective-permute-done((bf16[8,8,2048]{2,1,0:T(8,128)(2,1)S(1)}, bf16[8,8,2048]{2,1,0:T(8,128)(2,1)S(1)}, u32[]{:S(2)}, u32[]{:S(2)}) %collective-permute-start.26) | collective-permute-done | bytes 262176 | tf_op jit(solution)/shard_map/ppermute | solution.py:14
  138.2 0.8 copy-done
  139.4 3.7 %collective-permute-start.22 = (f16[2,2,32,2048]{3,2,0,1:T(8,128)(2,1)S(1)}, f16[2,2,32,2048]{3,2,0,1:T(8,128)(2,1)S(1)}, u32[]{:S(2)}, u32[]{:S(2)}) collective-permute-start(f16[2,2,32,2048]{3,2,0,1:T(8,128)(2,1)S(1)} %fusion.29), channel_id=1, source_target_pairs={{0,128},{32,160},{64,192},{96,224},{128,0},{160,32},{192,64},{224,... | collective-permute-start | bytes 1572872 | tf_op jit(solution)/shard_map/ppermute | solution.py:14
  143.1 0.8 collective-permute-start.23
  143.9 7.4 %fusion.3 = f32[2,2,2,2,32,2048]{5,4,3,2,1,0:T(8,128)S(1)} fusion(bf16[2048,2048]{1,0:T(8,128)(2,1)} %param.3, f32[2048]{0:T(1024)S(1)} %bitcast.152, bf16[1,2,2,2,32,2048]{5,4,3,2,1,0:T(8,128)(2,1)} %bitcast.51, bf16[1,2,2,2,32,2048]{5,4,3,2,1,0:T(8,128)(2,1)S(1)} %bitcast.134), kind=kOutput, calls=%fused_computation.6 | convolution fusion | flops 4308598784 | bytes 14688256 | tf_op jit(solution)/shard_map/dot_general | solution.py:110
  151.8 0.9 fusion.30
  152.7 0.9 fusion.31
  153.7 0.9 fusion.32
  154.6 1.2 collective-permute-done.22
  155.7 11.1 %collective-permute-done.23 = f16[2,2,32,2048]{3,2,1,0:T(8,128)(2,1)S(1)} collective-permute-done((f16[2,2,32,2048]{3,2,1,0:T(8,128)(2,1)}, f16[2,2,32,2048]{3,2,1,0:T(8,128)(2,1)S(1)}, u32[]{:S(2)}, u32[]{:S(2)}) %collective-permute-start.23) | collective-permute-done | bytes 524320 | tf_op jit(solution)/shard_map/ppermute | solution.py:14
  167.4 1.5 collective-permute-start.28
  168.9 0.8 collective-permute-start.29
  169.7 2.7 %collective-permute-start.30 = (f16[2,2,32,2048]{3,2,0,1:T(8,128)(2,1)}, f16[2,2,32,2048]{3,2,0,1:T(8,128)(2,1)}, u32[]{:S(2)}, u32[]{:S(2)}) collective-permute-start(f16[2,2,32,2048]{3,2,0,1:T(8,128)(2,1)} %fusion.31), channel_id=1, source_target_pairs={{0,128},{32,160},{64,192},{96,224},{128,0},{160,32},{192,64},{224,... | collective-permute-start | bytes 1572872 | tf_op jit(solution)/shard_map/ppermute | solution.py:14
  172.4 1.2 collective-permute-start.31
  173.6 11.0 %collective-permute-done.28 = f16[2,32,2048]{2,1,0:T(8,128)(2,1)S(1)} collective-permute-done((f16[2,32,2048]{2,1,0:T(8,128)(2,1)S(1)}, f16[2,32,2048]{2,1,0:T(8,128)(2,1)S(1)}, u32[]{:S(2)}, u32[]{:S(2)}) %collective-permute-start.28) | collective-permute-done | bytes 262176 | tf_op jit(solution)/shard_map/ppermute | solution.py:14
  184.7 11.0 %collective-permute-done.30 = f16[2,2,32,2048]{3,2,0,1:T(8,128)(2,1)} collective-permute-done((f16[2,2,32,2048]{3,2,0,1:T(8,128)(2,1)}, f16[2,2,32,2048]{3,2,0,1:T(8,128)(2,1)}, u32[]{:S(2)}, u32[]{:S(2)}) %collective-permute-start.30) | collective-permute-done | bytes 524320 | tf_op jit(solution)/shard_map/ppermute | solution.py:14
  195.7 2.6 %collective-permute-done.31 = f16[2,2,32,2048]{3,2,0,1:T(8,128)(2,1)} collective-permute-done((f16[2,2,32,2048]{3,2,0,1:T(8,128)(2,1)}, f16[2,2,32,2048]{3,2,0,1:T(8,128)(2,1)}, u32[]{:S(2)}, u32[]{:S(2)}) %collective-permute-start.31) | collective-permute-done | bytes 524320 | tf_op jit(solution)/shard_map/ppermute | solution.py:14
  198.2 1.6 fusion.25
  199.9 4.6 %collective-permute-start.32 = (f16[2,32,2048]{2,1,0:T(8,128)(2,1)S(1)}, f16[2,32,2048]{2,1,0:T(8,128)(2,1)S(1)}, u32[]{:S(2)}, u32[]{:S(2)}) collective-permute-start(f16[2,32,2048]{2,1,0:T(8,128)(2,1)S(1)} %fusion.34), channel_id=1, source_target_pairs={{0,32},{32,0},{64,96},{96,64},{128,160},{160,128},{192,224},{224,1... | collective-permute-start | bytes 786440 | tf_op jit(solution)/shard_map/ppermute | solution.py:14
  204.6 10.9 %collective-permute-done.32 = f16[2,32,2048]{2,1,0:T(8,128)(2,1)S(1)} collective-permute-done((f16[2,32,2048]{2,1,0:T(8,128)(2,1)S(1)}, f16[2,32,2048]{2,1,0:T(8,128)(2,1)S(1)}, u32[]{:S(2)}, u32[]{:S(2)}) %collective-permute-start.32) | collective-permute-done | bytes 262176 | tf_op jit(solution)/shard_map/ppermute | solution.py:14
  215.6 1.1 pad_maximum_fusion.2
  (74 shorter events, 7.0 us)
Async XLA Ops:
  1.5 14.9 %collective-permute-start = (bf16[128,2048]{1,0:T(8,128)(2,1)S(1)}, bf16[128,2048]{1,0:T(8,128)(2,1)S(1)}, u32[]{:S(2)}, u32[]{:S(2)}) collective-permute-start(bf16[128,2048]{1,0:T(8,128)(2,1)S(1)} %get-tuple-element.43), channel_id=1, source_target_pairs={{0,8},{1,9},{2,10},{3,11},{4,12},{5,13},{6,14},{7,15},{8,0},{9,1},... | collective-permute-start | bytes 1572872 | tf_op jit(solution)/shard_map/ppermute | solution.py:14
  3.0 25.7 %collective-permute-start.1 = (bf16[128,2048]{1,0:T(8,128)(2,1)S(1)}, bf16[128,2048]{1,0:T(8,128)(2,1)S(1)}, u32[]{:S(2)}, u32[]{:S(2)}) collective-permute-start(bf16[128,2048]{1,0:T(8,128)(2,1)S(1)} %get-tuple-element.42), channel_id=1, source_target_pairs={{0,16},{1,17},{2,18},{3,19},{4,20},{5,21},{6,22},{7,23},{8,24},{9,... | collective-permute-start | bytes 1572872 | tf_op jit(solution)/shard_map/ppermute | solution.py:14
  5.8 25.5 %collective-permute-start.2 = (bf16[128,2048]{1,0:T(8,128)(2,1)S(1)}, bf16[128,2048]{1,0:T(8,128)(2,1)S(1)}, u32[]{:S(2)}, u32[]{:S(2)}) collective-permute-start(bf16[128,2048]{1,0:T(8,128)(2,1)S(1)} %get-tuple-element.41), channel_id=1, source_target_pairs={{0,24},{1,25},{2,26},{3,27},{4,28},{5,29},{6,30},{7,31},{8,16},{9,... | collective-permute-start | bytes 1572872 | tf_op jit(solution)/shard_map/ppermute | solution.py:14
  32.7 10.7 %collective-permute-start.3 = (bf16[2,2,4,8,2048]{4,3,2,1,0:T(8,128)(2,1)S(1)}, bf16[2,2,4,8,2048]{4,3,2,1,0:T(8,128)(2,1)S(1)}, u32[]{:S(2)}, u32[]{:S(2)}) collective-permute-start(bf16[2,2,4,8,2048]{4,3,2,1,0:T(8,128)(2,1)S(1)} %pad_maximum_fusion.4), channel_id=1, source_target_pairs={{0,1},{1,0},{2,3},{3,2},{4,5},{5,4},{6,7},{7,6},{8,9},{9,8},{10,11... | collective-permute-start | bytes 1572872 | tf_op jit(solution)/shard_map/ppermute | solution.py:14
  44.2 8.3 %collective-permute-start.10 = (f32[3,2176]{1,0:T(4,128)S(1)}, f32[3,2176]{1,0:T(4,128)S(1)}, u32[]{:S(2)}, u32[]{:S(2)}) collective-permute-start(f32[3,2176]{1,0:T(4,128)S(1)} %maximum_maximum_fusion), channel_id=1, source_target_pairs={{0,64},{32,96},{64,0},{96,32},{128,192},{160,224},{192,128},{224,1... | collective-permute-start | bytes 78344 | tf_op jit(solution)/shard_map/ppermute | solution.py:14
  45.9 7.1 %collective-permute-start.11 = (f32[3,2176]{1,0:T(4,128)S(1)}, f32[3,2176]{1,0:T(4,128)S(1)}, u32[]{:S(2)}, u32[]{:S(2)}) collective-permute-start(f32[3,2176]{1,0:T(4,128)S(1)} %maximum_maximum_fusion), channel_id=1, source_target_pairs={{0,128},{32,160},{64,192},{96,224},{128,0},{160,32},{192,64},{224,... | collective-permute-start | bytes 78344 | tf_op jit(solution)/shard_map/ppermute | solution.py:14
  48.8 5.1 %collective-permute-start.12 = (f32[3,2176]{1,0:T(4,128)S(1)}, f32[3,2176]{1,0:T(4,128)S(1)}, u32[]{:S(2)}, u32[]{:S(2)}) collective-permute-start(f32[3,2176]{1,0:T(4,128)S(1)} %maximum_maximum_fusion), channel_id=1, source_target_pairs={{0,192},{32,224},{64,128},{96,160},{128,64},{160,96},{192,0},{224,... | collective-permute-start | bytes 78344 | tf_op jit(solution)/shard_map/ppermute | solution.py:14
  49.1 5.2 %collective-permute-start.4 = (bf16[2,2,8,2048]{3,2,1,0:T(8,128)(2,1)S(1)}, bf16[2,2,8,2048]{3,2,1,0:T(8,128)(2,1)S(1)}, u32[]{:S(2)}, u32[]{:S(2)}) collective-permute-start(bf16[2,2,8,2048]{3,2,1,0:T(8,128)(2,1)S(1)} %get-tuple-element.54), channel_id=1, source_target_pairs={{0,2},{1,3},{2,0},{3,1},{4,6},{5,7},{6,4},{7,5},{8,10},{9,11},{10,... | collective-permute-start | bytes 393224 | tf_op jit(solution)/shard_map/ppermute | solution.py:14
  49.3 12.7 %collective-permute-start.5 = (bf16[2,2,8,2048]{3,2,1,0:T(8,128)(2,1)S(1)}, bf16[2,2,8,2048]{3,2,1,0:T(8,128)(2,1)S(1)}, u32[]{:S(2)}, u32[]{:S(2)}) collective-permute-start(bf16[2,2,8,2048]{3,2,1,0:T(8,128)(2,1)S(1)} %get-tuple-element.55), channel_id=1, source_target_pairs={{0,4},{1,5},{2,6},{3,7},{4,0},{5,1},{6,2},{7,3},{8,12},{9,13},{10,... | collective-permute-start | bytes 393224 | tf_op jit(solution)/shard_map/ppermute | solution.py:14
  52.5 12.0 %collective-permute-start.6 = (bf16[2,2,8,2048]{3,2,1,0:T(8,128)(2,1)S(1)}, bf16[2,2,8,2048]{3,2,1,0:T(8,128)(2,1)S(1)}, u32[]{:S(2)}, u32[]{:S(2)}) collective-permute-start(bf16[2,2,8,2048]{3,2,1,0:T(8,128)(2,1)S(1)} %get-tuple-element.56), channel_id=1, source_target_pairs={{0,6},{1,7},{2,4},{3,5},{4,2},{5,3},{6,0},{7,1},{8,14},{9,15},{10,... | collective-permute-start | bytes 393224 | tf_op jit(solution)/shard_map/ppermute | solution.py:14
  64.5 9.9 %collective-permute-start.13 = (f32[3,2176]{1,0:T(4,128)S(1)}, f32[3,2176]{1,0:T(4,128)S(1)}, u32[]{:S(2)}, u32[]{:S(2)}) collective-permute-start(f32[3,2176]{1,0:T(4,128)S(1)} %pad_maximum_fusion.6), channel_id=1, source_target_pairs={{0,32},{32,0},{64,96},{96,64},{128,160},{160,128},{192,224},{224,1... | collective-permute-start | bytes 78344 | tf_op jit(solution)/shard_map/ppermute | solution.py:14
  70.6 6.5 %collective-permute-start.7 = (bf16[2,2,8,2048]{3,2,1,0:T(8,128)(2,1)S(1)}, bf16[2,2,8,2048]{3,2,1,0:T(8,128)(2,1)S(1)}, u32[]{:S(2)}, u32[]{:S(2)}) collective-permute-start(bf16[2,2,8,2048]{3,2,1,0:T(8,128)(2,1)S(1)} %pad_maximum_fusion.5), channel_id=1, source_target_pairs={{0,2},{1,3},{2,0},{3,1},{4,6},{5,7},{6,4},{7,5},{8,10},{9,11},{10,... | collective-permute-start | bytes 393224 | tf_op jit(solution)/shard_map/ppermute | solution.py:14
  70.7 11.4 %collective-permute-start.8 = (bf16[2,2,8,2048]{3,2,1,0:T(8,128)(2,1)S(1)}, bf16[2,2,8,2048]{3,2,1,0:T(8,128)(2,1)S(1)}, u32[]{:S(2)}, u32[]{:S(2)}) collective-permute-start(bf16[2,2,8,2048]{3,2,1,0:T(8,128)(2,1)S(1)} %pad_maximum_fusion.5), channel_id=1, source_target_pairs={{0,4},{1,5},{2,6},{3,7},{4,0},{5,1},{6,2},{7,3},{8,12},{9,13},{10,... | collective-permute-start | bytes 393224 | tf_op jit(solution)/shard_map/ppermute | solution.py:14
  73.2 12.1 %collective-permute-start.9 = (bf16[2,2,8,2048]{3,2,1,0:T(8,128)(2,1)S(1)}, bf16[2,2,8,2048]{3,2,1,0:T(8,128)(2,1)S(1)}, u32[]{:S(2)}, u32[]{:S(2)}) collective-permute-start(bf16[2,2,8,2048]{3,2,1,0:T(8,128)(2,1)S(1)} %pad_maximum_fusion.5), channel_id=1, source_target_pairs={{0,6},{1,7},{2,4},{3,5},{4,2},{5,3},{6,0},{7,1},{8,14},{9,15},{10,... | collective-permute-start | bytes 393224 | tf_op jit(solution)/shard_map/ppermute | solution.py:14
  77.1 8.3 %collective-permute-start.14 = (f32[2,2,2,4,8]{4,3,2,1,0:T(4,128)S(1)}, f32[2,2,2,4,8]{4,3,2,1,0:T(4,128)S(1)}, u32[]{:S(2)}, u32[]{:S(2)}) collective-permute-start(f32[2,2,2,4,8]{4,3,2,1,0:T(4,128)S(1)} %pad_maximum_fusion.7), channel_id=1, source_target_pairs={{0,2},{1,3},{2,0},{3,1},{4,6},{5,7},{6,4},{7,5},{8,10},{9,11},{10,... | collective-permute-start | bytes 3080 | tf_op jit(solution)/shard_map/ppermute | solution.py:14
  77.8 7.6 %collective-permute-start.15 = (f32[2,2,2,4,8]{4,3,2,1,0:T(4,128)S(1)}, f32[2,2,2,4,8]{4,3,2,1,0:T(4,128)S(1)}, u32[]{:S(2)}, u32[]{:S(2)}) collective-permute-start(f32[2,2,2,4,8]{4,3,2,1,0:T(4,128)S(1)} %pad_maximum_fusion.7), channel_id=1, source_target_pairs={{0,4},{1,5},{2,6},{3,7},{4,0},{5,1},{6,2},{7,3},{8,12},{9,13},{10,... | collective-permute-start | bytes 3080 | tf_op jit(solution)/shard_map/ppermute | solution.py:14
  79.6 6.1 %collective-permute-start.16 = (f32[2,2,2,4,8]{4,3,2,1,0:T(4,128)S(1)}, f32[2,2,2,4,8]{4,3,2,1,0:T(4,128)S(1)}, u32[]{:S(2)}, u32[]{:S(2)}) collective-permute-start(f32[2,2,2,4,8]{4,3,2,1,0:T(4,128)S(1)} %pad_maximum_fusion.7), channel_id=1, source_target_pairs={{0,6},{1,7},{2,4},{3,5},{4,2},{5,3},{6,0},{7,1},{8,14},{9,15},{10,... | collective-permute-start | bytes 3080 | tf_op jit(solution)/shard_map/ppermute | solution.py:14
  87.2 10.0 %collective-permute-start.17 = (bf16[9,8,2048]{2,1,0:T(8,128)(2,1)S(1)}, bf16[9,8,2048]{2,1,0:T(8,128)(2,1)S(1)}, u32[]{:S(2)}, u32[]{:S(2)}) collective-permute-start(bf16[9,8,2048]{2,1,0:T(8,128)(2,1)S(1)} %get-tuple-element.62), channel_id=1, source_target_pairs={{0,8},{1,9},{2,10},{3,11},{4,12},{5,13},{6,14},{7,15},{8,0},{9,1},... | collective-permute-start | bytes 884744 | tf_op jit(solution)/shard_map/ppermute | solution.py:14
  87.3 13.5 %collective-permute-start.18 = (bf16[9,8,2048]{2,1,0:T(8,128)(2,1)S(1)}, bf16[9,8,2048]{2,1,0:T(8,128)(2,1)S(1)}, u32[]{:S(2)}, u32[]{:S(2)}) collective-permute-start(bf16[9,8,2048]{2,1,0:T(8,128)(2,1)S(1)} %get-tuple-element.62), channel_id=1, source_target_pairs={{0,16},{1,17},{2,18},{3,19},{4,20},{5,21},{6,22},{7,23},{8,24},{9,... | collective-permute-start | bytes 884744 | tf_op jit(solution)/shard_map/ppermute | solution.py:14
  89.3 14.2 %collective-permute-start.19 = (bf16[9,8,2048]{2,1,0:T(8,128)(2,1)S(1)}, bf16[9,8,2048]{2,1,0:T(8,128)(2,1)S(1)}, u32[]{:S(2)}, u32[]{:S(2)}) collective-permute-start(bf16[9,8,2048]{2,1,0:T(8,128)(2,1)S(1)} %get-tuple-element.62), channel_id=1, source_target_pairs={{0,24},{1,25},{2,26},{3,27},{4,28},{5,29},{6,30},{7,31},{8,16},{9,... | collective-permute-start | bytes 884744 | tf_op jit(solution)/shard_map/ppermute | solution.py:14
  103.6 3.1 %collective-permute-start.20 = (bf16[4,9,8,2048]{3,2,1,0:T(8,128)(2,1)S(1)}, bf16[4,9,8,2048]{3,2,1,0:T(8,128)(2,1)}, u32[]{:S(2)}, u32[]{:S(2)}) collective-permute-start(bf16[4,9,8,2048]{3,2,1,0:T(8,128)(2,1)S(1)} %pad_maximum_fusion), channel_id=1, source_target_pairs={{0,1},{1,0},{2,3},{3,2},{4,5},{5,4},{6,7},{7,6},{8,9},{9,8},{10,11... | collective-permute-start | bytes 3538952 | tf_op jit(solution)/shard_map/ppermute | solution.py:14
  119.1 19.1 %collective-permute-start.21 = (f16[2,2,32,2048]{3,2,0,1:T(8,128)(2,1)S(1)}, f16[2,2,32,2048]{3,2,0,1:T(8,128)(2,1)S(1)}, u32[]{:S(2)}, u32[]{:S(2)}) collective-permute-start(f16[2,2,32,2048]{3,2,0,1:T(8,128)(2,1)S(1)} %fusion.28), channel_id=1, source_target_pairs={{0,64},{32,96},{64,0},{96,32},{128,192},{160,224},{192,128},{224,1... | collective-permute-start | bytes 1572872 | tf_op jit(solution)/shard_map/ppermute | solution.py:14
  119.2 9.2 %collective-permute-start.24 = (bf16[8,8,2048]{2,1,0:T(8,128)(2,1)S(1)}, bf16[8,8,2048]{2,1,0:T(8,128)(2,1)S(1)}, u32[]{:S(2)}, u32[]{:S(2)}) collective-permute-start(bf16[8,8,2048]{2,1,0:T(8,128)(2,1)S(1)} %bitcast.137), channel_id=1, source_target_pairs={{0,8},{1,9},{2,10},{3,11},{4,12},{5,13},{6,14},{7,15},{8,0},{9,1},... | collective-permute-start | bytes 786440 | tf_op jit(solution)/shard_map/ppermute | solution.py:14
  119.3 16.3 %collective-permute-start.25 = (bf16[8,8,2048]{2,1,0:T(8,128)(2,1)S(1)}, bf16[8,8,2048]{2,1,0:T(8,128)(2,1)S(1)}, u32[]{:S(2)}, u32[]{:S(2)}) collective-permute-start(bf16[8,8,2048]{2,1,0:T(8,128)(2,1)S(1)} %bitcast.138), channel_id=1, source_target_pairs={{0,16},{1,17},{2,18},{3,19},{4,20},{5,21},{6,22},{7,23},{8,24},{9,... | collective-permute-start | bytes 786440 | tf_op jit(solution)/shard_map/ppermute | solution.py:14
  123.6 14.6 %collective-permute-start.26 = (bf16[8,8,2048]{2,1,0:T(8,128)(2,1)S(1)}, bf16[8,8,2048]{2,1,0:T(8,128)(2,1)S(1)}, u32[]{:S(2)}, u32[]{:S(2)}) collective-permute-start(bf16[8,8,2048]{2,1,0:T(8,128)(2,1)S(1)} %bitcast.139), channel_id=1, source_target_pairs={{0,24},{1,25},{2,26},{3,27},{4,28},{5,29},{6,30},{7,31},{8,16},{9,... | collective-permute-start | bytes 786440 | tf_op jit(solution)/shard_map/ppermute | solution.py:14
  138.2 0.8 copy-start
  139.1 4.7 %collective-permute-start.27 = (bf16[4,8,8,2048]{3,2,1,0:T(8,128)(2,1)S(1)}, bf16[4,8,8,2048]{3,2,1,0:T(8,128)(2,1)}, u32[]{:S(2)}, u32[]{:S(2)}) collective-permute-start(bf16[4,8,8,2048]{3,2,1,0:T(8,128)(2,1)S(1)} %pad_maximum_fusion.1), channel_id=1, source_target_pairs={{0,1},{1,0},{2,3},{3,2},{4,5},{5,4},{6,7},{7,6},{8,9},{9,8},{10,11... | collective-permute-start | bytes 3145736 | tf_op jit(solution)/shard_map/ppermute | solution.py:14
  139.4 16.4 %collective-permute-start.22 = (f16[2,2,32,2048]{3,2,0,1:T(8,128)(2,1)S(1)}, f16[2,2,32,2048]{3,2,0,1:T(8,128)(2,1)S(1)}, u32[]{:S(2)}, u32[]{:S(2)}) collective-permute-start(f16[2,2,32,2048]{3,2,0,1:T(8,128)(2,1)S(1)} %fusion.29), channel_id=1, source_target_pairs={{0,128},{32,160},{64,192},{96,224},{128,0},{160,32},{192,64},{224,... | collective-permute-start | bytes 1572872 | tf_op jit(solution)/shard_map/ppermute | solution.py:14
  143.1 23.8 %collective-permute-start.23 = (f16[2,2,32,2048]{3,2,1,0:T(8,128)(2,1)}, f16[2,2,32,2048]{3,2,1,0:T(8,128)(2,1)S(1)}, u32[]{:S(2)}, u32[]{:S(2)}) collective-permute-start(f16[2,2,32,2048]{3,2,1,0:T(8,128)(2,1)} %get-tuple-element.33), channel_id=1, source_target_pairs={{0,192},{32,224},{64,128},{96,160},{128,64},{160,96},{192,0},{224,... | collective-permute-start | bytes 1572872 | tf_op jit(solution)/shard_map/ppermute | solution.py:14
  151.8 15.1 %copy-start.1 = (f16[2,2,32,2048]{3,2,0,1:T(8,128)(2,1)S(1)}, f16[2,2,32,2048]{3,2,0,1:T(8,128)(2,1)}, u32[]{:S(2)}) copy-start(f16[2,2,32,2048]{3,2,0,1:T(8,128)(2,1)} %copy-done) | copy-start | bytes 1572868
  167.4 17.1 %collective-permute-start.28 = (f16[2,32,2048]{2,1,0:T(8,128)(2,1)S(1)}, f16[2,32,2048]{2,1,0:T(8,128)(2,1)S(1)}, u32[]{:S(2)}, u32[]{:S(2)}) collective-permute-start(f16[2,32,2048]{2,1,0:T(8,128)(2,1)S(1)} %fusion.35), channel_id=1, source_target_pairs={{0,32},{32,0},{64,96},{96,64},{128,160},{160,128},{192,224},{224,1... | collective-permute-start | bytes 786440 | tf_op jit(solution)/shard_map/ppermute | solution.py:14
  168.9 15.7 %collective-permute-start.29 = (f16[2,2,32,2048]{3,2,0,1:T(8,128)(2,1)}, f16[2,2,32,2048]{3,2,0,1:T(8,128)(2,1)S(1)}, u32[]{:S(2)}, u32[]{:S(2)}) collective-permute-start(f16[2,2,32,2048]{3,2,0,1:T(8,128)(2,1)} %fusion.30), channel_id=1, source_target_pairs={{0,64},{32,96},{64,0},{96,32},{128,192},{160,224},{192,128},{224,1... | collective-permute-start | bytes 1572872 | tf_op jit(solution)/shard_map/ppermute | solution.py:14
  169.7 25.9 %collective-permute-start.30 = (f16[2,2,32,2048]{3,2,0,1:T(8,128)(2,1)}, f16[2,2,32,2048]{3,2,0,1:T(8,128)(2,1)}, u32[]{:S(2)}, u32[]{:S(2)}) collective-permute-start(f16[2,2,32,2048]{3,2,0,1:T(8,128)(2,1)} %fusion.31), channel_id=1, source_target_pairs={{0,128},{32,160},{64,192},{96,224},{128,0},{160,32},{192,64},{224,... | collective-permute-start | bytes 1572872 | tf_op jit(solution)/shard_map/ppermute | solution.py:14
  172.4 25.8 %collective-permute-start.31 = (f16[2,2,32,2048]{3,2,0,1:T(8,128)(2,1)}, f16[2,2,32,2048]{3,2,0,1:T(8,128)(2,1)}, u32[]{:S(2)}, u32[]{:S(2)}) collective-permute-start(f16[2,2,32,2048]{3,2,0,1:T(8,128)(2,1)} %fusion.32), channel_id=1, source_target_pairs={{0,192},{32,224},{64,128},{96,160},{128,64},{160,96},{192,0},{224,... | collective-permute-start | bytes 1572872 | tf_op jit(solution)/shard_map/ppermute | solution.py:14
  199.9 15.6 %collective-permute-start.32 = (f16[2,32,2048]{2,1,0:T(8,128)(2,1)S(1)}, f16[2,32,2048]{2,1,0:T(8,128)(2,1)S(1)}, u32[]{:S(2)}, u32[]{:S(2)}) collective-permute-start(f16[2,32,2048]{2,1,0:T(8,128)(2,1)S(1)} %fusion.34), channel_id=1, source_target_pairs={{0,32},{32,0},{64,96},{96,64},{128,160},{160,128},{192,224},{224,1... | collective-permute-start | bytes 786440 | tf_op jit(solution)/shard_map/ppermute | solution.py:14
where the time goes:
time: 218 us; the launch traced here: 217 us
  waiting for transfers between devices  112 us (51%)
  starting transfers between devices  51.8 us (24%)
  other arithmetic  24.8 us (11%)
  matrix products  14.5 us (7%)
  between operations  7.12 us (3%)
  local copies, waits for them, and re-layouts  6.11 us (3%)
    ppermute x33, waiting for transfers between devices, swap(): return lax.ppermute(value, axis, [(i, i ^ bits) for i in range(size)])  112 us
    ppermute x33, starting transfers between devices, swap(): return lax.ppermute(value, axis, [(i, i ^ bits) for i in range(size)])  51.8 us
    dot_general x2, matrix products, per_device(): lax.dot_general(panel_anom.reshape(16 * rows, shard), first_anom, (((1,),...  14.5 us
    reduce_sum x2, other arithmetic, row_stats(): return jnp.stack([jnp.sum(wide, -1), jnp.max(wide, -1), jnp.max(-wide, -1)])  6.27 us
    reduce_max x3, other arithmetic, row_stats(): return jnp.stack([jnp.sum(wide, -1), jnp.max(wide, -1), jnp.max(-wide, -1)])  4.74 us
  transfers between devices with their start and end apart: 33, of which 25 were waited for; matrix products, arithmetic and copies ran while one was open for 12% of the time, Pallas kernels for 0%

commit v1 on v0

--- a/solution.py
+++ b/solution.py
@@ -50,6 +50,7 @@
     from_x = [piece(0)] + [swap(piece(bits), "samp", 8 * bits) for bits in (1, 2, 3)]
     first_plane = after(first_plane, from_x[0])
     first_local = row_stats(first_plane)
+    from_x = after(from_x, first_local)
     halves = [
         pick(my_x ^ own_x[p], from_x).reshape(CHUNKS, 2, 4, -1, shard) for p in range(2)
     ]
@@ -98,7 +99,7 @@
     blocks, arrived = [], []
     for chunk in range(CHUNKS):
         if chunk > 0:
-            gathered[chunk] = after(gathered[chunk], arrived[-1][0])
+            gathered[chunk] = after(gathered[chunk], sent)
         near = jnp.stack(gathered[chunk])
         far = swap(near, "samp", 1)
         if chunk == 0:

time: 218 us -> 199 us (0.913)
  waiting for transfers between devices: 112 us -> 94 us
    ppermute x33, waiting for transfers between devices: 112 us -> 94 us  [swap(): return lax.ppermute(value, axis, [(i, i ^ bits) for i in range(size)])]
    convert_element_type x6 -> x5, other arithmetic: 4.23 us -> 4.65 us  [per_device(): (for_y(my_y ^ bits) * shrink_first * shrink_panel).astype(WIRE)]
  transfers between devices with their start and end apart: 33 -> 33, of which waited for: 25 -> 22; matrix products, arithmetic and copies ran while one was open for 12% -> 19% of each run, Pallas kernels for 0% -> 0%
where the time goes in v1:
time: 199 us; the launch traced here: 198 us
  waiting for transfers between devices  94 us (47%)
  starting transfers between devices  51.2 us (26%)
  other arithmetic  24.7 us (12%)
  matrix products  14.2 us (7%)
  between operations  7.17 us (4%)
  local copies, waits for them, and re-layouts  6.39 us (3%)
    ppermute x33, waiting for transfers between devices, swap(): return lax.ppermute(value, axis, [(i, i ^ bits) for i in range(size)])  94 us
    ppermute x33, starting transfers between devices, swap(): return lax.ppermute(value, axis, [(i, i ^ bits) for i in range(size)])  51.2 us
    dot_general x2, matrix products, per_device(): lax.dot_general(panel_anom.reshape(16 * rows, shard), first_anom, (((1,),...  14.2 us
    reduce_sum x2, other arithmetic, row_stats(): return jnp.stack([jnp.sum(wide, -1), jnp.max(wide, -1), jnp.max(-wide, -1)])  6.28 us
    reduce_max x3, other arithmetic, row_stats(): return jnp.stack([jnp.sum(wide, -1), jnp.max(wide, -1), jnp.max(-wide, -1)])  4.74 us
    convert_element_type x5, other arithmetic, per_device(): (for_y(my_y ^ bits) * shrink_first * shrink_panel).astype(WIRE)  4.65 us
  transfers between devices with their start and end apart: 33, of which 22 were waited for; matrix products, arithmetic and copies ran while one was open for 19% of the time, Pallas kernels for 0%

profile of v1, /device:TPU:32, one launch (start us, length us, event | category | flops | bytes accessed | tf_op | source)
XLA Modules:
  0.0 197.7 jit_solution(605855291911348147)
XLA Ops:
  0.0 2.5 %dynamic-slice_bitcast_fusion = (bf16[128,2048]{1,0:T(8,128)(2,1)S(1)}, bf16[128,2048]{1,0:T(8,128)(2,1)S(1)}, bf16[128,2048]{1,0:T(8,128)(2,1)}, bf16[128,2048]{1,0:T(8,128)(2,1)S(1)}) fusion(bf16[4,128,2048]{2,1,0:T(8,128)(2,1)} %bitcast.130, s32[]{:T(128)S(6)} %select_n.326, s32[]{:T(128)S(6)} %select_n.325, s32[]{:T(128)S(6)} %select_n.324, s32[]{:T(128)S(6)} %select_n.323), kind=kLoop, calls=%fused_computation.67 | loop fusion | bytes 4194320 | tf_op jit(solution)/shard_map/jit(dynamic_index_in_dim)/squeeze | solution.py:49
  2.5 1.5 collective-permute-start
  4.0 2.7 %collective-permute-start.1 = (bf16[128,2048]{1,0:T(8,128)(2,1)S(1)}, bf16[128,2048]{1,0:T(8,128)(2,1)S(1)}, u32[]{:S(2)}, u32[]{:S(2)}) collective-permute-start(bf16[128,2048]{1,0:T(8,128)(2,1)S(1)} %get-tuple-element.50), channel_id=1, source_target_pairs={{0,16},{1,17},{2,18},{3,19},{4,20},{5,21},{6,22},{7,23},{8,24},{9,... | collective-permute-start | bytes 1572872 | tf_op jit(solution)/shard_map/ppermute | solution.py:14
  6.7 0.5 collective-permute-start.2
  7.2 0.7 fusion.61
  9.3 0.7 fusion.59
  12.6 4.6 %reduce_max.90 = bf16[2048]{0:T(1024)(128)(2,1)S(1)} reduce(bf16[2048,2048]{1,0:T(8,128)(2,1)} %param.3, bf16[]{:T(256)} %constant.77.clone.1), dimensions={1}, to_apply=%region_1.2 | reduce | flops 4192256 | bytes 8392706 | tf_op jit(solution)/shard_map/reduce_max | solution.py:26
  17.2 0.4 collective-permute-done
  17.5 12.4 %collective-permute-done.1 = bf16[128,2048]{1,0:T(8,128)(2,1)S(1)} collective-permute-done((bf16[128,2048]{1,0:T(8,128)(2,1)S(1)}, bf16[128,2048]{1,0:T(8,128)(2,1)S(1)}, u32[]{:S(2)}, u32[]{:S(2)}) %collective-permute-start.1) | collective-permute-done | bytes 524320 | tf_op jit(solution)/shard_map/ppermute | solution.py:14
  29.9 2.4 %collective-permute-done.2 = bf16[128,2048]{1,0:T(8,128)(2,1)S(1)} collective-permute-done((bf16[128,2048]{1,0:T(8,128)(2,1)S(1)}, bf16[128,2048]{1,0:T(8,128)(2,1)S(1)}, u32[]{:S(2)}, u32[]{:S(2)}) %collective-permute-start.2) | collective-permute-done | bytes 524320 | tf_op jit(solution)/shard_map/ppermute | solution.py:14
  32.6 6.0 %convert_reduce_fusion = (f32[2048]{0:T(1024)S(1)}, f32[2048]{0:T(1024)S(1)}) fusion(bf16[2048,2048]{1,0:T(8,128)(2,1)} %param.3), kind=kLoop, calls=%fused_computation.2 | loop fusion | flops 16773120 | bytes 8404992 | tf_op jit(solution)/shard_map/reduce_sum | solution.py:26
  39.4 1.7 collective-permute-start.10
  41.1 2.9 %collective-permute-start.11 = (f32[3,2176]{1,0:T(4,128)S(1)}, f32[3,2176]{1,0:T(4,128)S(1)}, u32[]{:S(2)}, u32[]{:S(2)}) collective-permute-start(f32[3,2176]{1,0:T(4,128)S(1)} %maximum_maximum_fusion), channel_id=1, source_target_pairs={{0,128},{32,160},{64,192},{96,224},{128,0},{160,32},{192,64},{224,... | collective-permute-start | bytes 78344 | tf_op jit(solution)/shard_map/ppermute | solution.py:14
  44.5 3.3 %collective-permute-start.5 = (bf16[2,2,8,2048]{3,2,1,0:T(8,128)(2,1)S(1)}, bf16[2,2,8,2048]{3,2,1,0:T(8,128)(2,1)S(1)}, u32[]{:S(2)}, u32[]{:S(2)}) collective-permute-start(bf16[2,2,8,2048]{3,2,1,0:T(8,128)(2,1)S(1)} %get-tuple-element.64), channel_id=1, source_target_pairs={{0,4},{1,5},{2,6},{3,7},{4,0},{5,1},{6,2},{7,3},{8,12},{9,13},{10,... | collective-permute-start | bytes 393224 | tf_op jit(solution)/shard_map/ppermute | solution.py:14
  47.7 0.5 collective-permute-start.6
  48.2 0.9 collective-permute-done.12
  49.5 7.7 %collective-permute-done.5 = bf16[2,2,8,2048]{3,2,1,0:T(8,128)(2,1)S(1)} collective-permute-done((bf16[2,2,8,2048]{3,2,1,0:T(8,128)(2,1)S(1)}, bf16[2,2,8,2048]{3,2,1,0:T(8,128)(2,1)S(1)}, u32[]{:S(2)}, u32[]{:S(2)}) %collective-permute-start.5) | collective-permute-done | bytes 131104 | tf_op jit(solution)/shard_map/ppermute | solution.py:14
  57.2 2.5 %collective-permute-done.6 = bf16[2,2,8,2048]{3,2,1,0:T(8,128)(2,1)S(1)} collective-permute-done((bf16[2,2,8,2048]{3,2,1,0:T(8,128)(2,1)S(1)}, bf16[2,2,8,2048]{3,2,1,0:T(8,128)(2,1)S(1)}, u32[]{:S(2)}, u32[]{:S(2)}) %collective-permute-start.6) | collective-permute-done | bytes 131104 | tf_op jit(solution)/shard_map/ppermute | solution.py:14
  59.7 6.0 %collective-permute-start.13 = (f32[3,2176]{1,0:T(4,128)S(1)}, f32[3,2176]{1,0:T(4,128)S(1)}, u32[]{:S(2)}, u32[]{:S(2)}) collective-permute-start(f32[3,2176]{1,0:T(4,128)S(1)} %pad_maximum_fusion.6), channel_id=1, source_target_pairs={{0,32},{32,0},{64,96},{96,64},{128,160},{160,128},{192,224},{224,1... | collective-permute-start | bytes 78344 | tf_op jit(solution)/shard_map/ppermute | solution.py:14
  65.9 2.5 %collective-permute-start.8 = (bf16[2,2,8,2048]{3,2,1,0:T(8,128)(2,1)S(1)}, bf16[2,2,8,2048]{3,2,1,0:T(8,128)(2,1)S(1)}, u32[]{:S(2)}, u32[]{:S(2)}) collective-permute-start(bf16[2,2,8,2048]{3,2,1,0:T(8,128)(2,1)S(1)} %pad_maximum_fusion.5), channel_id=1, source_target_pairs={{0,4},{1,5},{2,6},{3,7},{4,0},{5,1},{6,2},{7,3},{8,12},{9,13},{10,... | collective-permute-start | bytes 393224 | tf_op jit(solution)/shard_map/ppermute | solution.py:14
  68.4 1.0 collective-permute-start.9
  70.0 2.4 %collective-permute-done.7 = bf16[2,2,8,2048]{3,2,1,0:T(8,128)(2,1)S(1)} collective-permute-done((bf16[2,2,8,2048]{3,2,1,0:T(8,128)(2,1)S(1)}, bf16[2,2,8,2048]{3,2,1,0:T(8,128)(2,1)S(1)}, u32[]{:S(2)}, u32[]{:S(2)}) %collective-permute-start.7) | collective-permute-done | bytes 131104 | tf_op jit(solution)/shard_map/ppermute | solution.py:14
  72.3 0.7 collective-permute-start.14
  73.0 1.8 collective-permute-start.15
  74.8 1.0 collective-permute-start.16
  75.8 1.5 collective-permute-done.8
  77.3 3.2 %collective-permute-done.9 = bf16[2,2,8,2048]{3,2,1,0:T(8,128)(2,1)S(1)} collective-permute-done((bf16[2,2,8,2048]{3,2,1,0:T(8,128)(2,1)S(1)}, bf16[2,2,8,2048]{3,2,1,0:T(8,128)(2,1)S(1)}, u32[]{:S(2)}, u32[]{:S(2)}) %collective-permute-start.9) | collective-permute-done | bytes 131104 | tf_op jit(solution)/shard_map/ppermute | solution.py:14
  80.9 0.6 fusion.51
  82.6 1.9 collective-permute-start.18
  84.5 2.8 %collective-permute-start.19 = (bf16[9,8,2048]{2,1,0:T(8,128)(2,1)S(1)}, bf16[9,8,2048]{2,1,0:T(8,128)(2,1)S(1)}, u32[]{:S(2)}, u32[]{:S(2)}) collective-permute-start(bf16[9,8,2048]{2,1,0:T(8,128)(2,1)S(1)} %get-tuple-element.71), channel_id=1, source_target_pairs={{0,24},{1,25},{2,26},{3,27},{4,28},{5,29},{6,30},{7,31},{8,16},{9,... | collective-permute-start | bytes 884744 | tf_op jit(solution)/shard_map/ppermute | solution.py:14
  87.2 5.2 %collective-permute-done.17 = bf16[9,8,2048]{2,1,0:T(8,128)(2,1)S(1)} collective-permute-done((bf16[9,8,2048]{2,1,0:T(8,128)(2,1)S(1)}, bf16[9,8,2048]{2,1,0:T(8,128)(2,1)S(1)}, u32[]{:S(2)}, u32[]{:S(2)}) %collective-permute-start.17) | collective-permute-done | bytes 294944 | tf_op jit(solution)/shard_map/ppermute | solution.py:14
  92.5 3.6 %collective-permute-done.18 = bf16[9,8,2048]{2,1,0:T(8,128)(2,1)S(1)} collective-permute-done((bf16[9,8,2048]{2,1,0:T(8,128)(2,1)S(1)}, bf16[9,8,2048]{2,1,0:T(8,128)(2,1)S(1)}, u32[]{:S(2)}, u32[]{:S(2)}) %collective-permute-start.18) | collective-permute-done | bytes 294944 | tf_op jit(solution)/shard_map/ppermute | solution.py:14
  96.1 2.6 %collective-permute-done.19 = bf16[9,8,2048]{2,1,0:T(8,128)(2,1)S(1)} collective-permute-done((bf16[9,8,2048]{2,1,0:T(8,128)(2,1)S(1)}, bf16[9,8,2048]{2,1,0:T(8,128)(2,1)S(1)}, u32[]{:S(2)}, u32[]{:S(2)}) %collective-permute-start.19) | collective-permute-done | bytes 294944 | tf_op jit(solution)/shard_map/ppermute | solution.py:14
  99.0 0.6 slice_reduce_fusion
  100.5 4.2 %collective-permute-start.25 = (bf16[8,8,2048]{2,1,0:T(8,128)(2,1)S(1)}, bf16[8,8,2048]{2,1,0:T(8,128)(2,1)S(1)}, u32[]{:S(2)}, u32[]{:S(2)}) collective-permute-start(bf16[8,8,2048]{2,1,0:T(8,128)(2,1)S(1)} %bitcast.136), channel_id=1, source_target_pairs={{0,16},{1,17},{2,18},{3,19},{4,20},{5,21},{6,22},{7,23},{8,24},{9,... | collective-permute-start | bytes 786440 | tf_op jit(solution)/shard_map/ppermute | solution.py:14
  104.7 0.5 collective-permute-start.26
  105.2 0.6 slice_reduce_fusion.2
  105.8 1.4 slice_reduce_fusion.1
  108.5 1.3 slice.273
  109.8 7.1 %fusion.5 = f32[2,2,2,2,32,2048]{5,4,3,2,1,0:T(8,128)S(1)} fusion(bf16[2048,2048]{1,0:T(8,128)(2,1)} %param.3, f32[2048]{0:T(1024)S(1)} %bitcast.149, bf16[1,2,2,2,32,2048]{5,4,3,2,1,0:T(8,128)(2,1)S(1)} %bitcast.134, bf16[1,2,2,2,32,2048]{5,4,3,2,1,0:T(8,128)(2,1)S(1)} %bitcast.133), kind=kOutput, calls=%fused_computation.7 | convolution fusion | flops 4308598784 | bytes 14688256 | tf_op jit(solution)/shard_map/dot_general | solution.py:111
  116.9 1.3 constant_dynamic-slice_fusion.6
  118.2 0.9 fusion.29
  119.2 0.9 fusion.28
  120.4 1.5 collective-permute-start.22
  121.9 1.9 collective-permute-start.21
  123.8 0.8 collective-permute-start.23
  124.6 7.1 %fusion.3 = f32[2,2,2,2,32,2048]{5,4,3,2,1,0:T(8,128)S(1)} fusion(bf16[2048,2048]{1,0:T(8,128)(2,1)} %param.3, f32[2048]{0:T(1024)S(1)} %bitcast.150, bf16[1,2,2,2,32,2048]{5,4,3,2,1,0:T(8,128)(2,1)S(1)} %bitcast.151, bf16[1,2,2,2,32,2048]{5,4,3,2,1,0:T(8,128)(2,1)S(1)} %bitcast.132), kind=kOutput, calls=%fused_computation.6 | convolution fusion | flops 4308598784 | bytes 14688256 | tf_op jit(solution)/shard_map/dot_general | solution.py:111
  131.7 0.5 constant_dynamic-slice_fusion.3
  132.2 0.9 fusion.30
  133.1 0.9 fusion.31
  134.1 0.9 fusion.32
  135.0 2.0 %collective-permute-done.22 = f16[2,2,32,2048]{3,2,0,1:T(8,128)(2,1)S(1)} collective-permute-done((f16[2,2,32,2048]{3,2,0,1:T(8,128)(2,1)}, f16[2,2,32,2048]{3,2,0,1:T(8,128)(2,1)S(1)}, u32[]{:S(2)}, u32[]{:S(2)}) %collective-permute-start.22) | collective-permute-done | bytes 524320 | tf_op jit(solution)/shard_map/ppermute | solution.py:14
  137.0 10.4 %collective-permute-done.21 = f16[2,2,32,2048]{3,2,0,1:T(8,128)(2,1)S(1)} collective-permute-done((f16[2,2,32,2048]{3,2,0,1:T(8,128)(2,1)}, f16[2,2,32,2048]{3,2,0,1:T(8,128)(2,1)S(1)}, u32[]{:S(2)}, u32[]{:S(2)}) %collective-permute-start.21) | collective-permute-done | bytes 524320 | tf_op jit(solution)/shard_map/ppermute | solution.py:14
  147.6 0.5 copy_add_fusion
  148.2 1.3 collective-permute-start.28
  149.7 3.9 %collective-permute-start.30 = (f16[2,2,32,2048]{3,2,0,1:T(8,128)(2,1)}, f16[2,2,32,2048]{3,2,0,1:T(8,128)(2,1)}, u32[]{:S(2)}, u32[]{:S(2)}) collective-permute-start(f16[2,2,32,2048]{3,2,0,1:T(8,128)(2,1)} %fusion.31), channel_id=1, source_target_pairs={{0,128},{32,160},{64,192},{96,224},{128,0},{160,32},{192,64},{224,... | collective-permute-start | bytes 1572872 | tf_op jit(solution)/shard_map/ppermute | solution.py:14
  153.5 0.6 collective-permute-start.31
  154.1 11.9 %collective-permute-done.28 = f16[2,32,2048]{2,1,0:T(8,128)(2,1)S(1)} collective-permute-done((f16[2,32,2048]{2,1,0:T(8,128)(2,1)S(1)}, f16[2,32,2048]{2,1,0:T(8,128)(2,1)S(1)}, u32[]{:S(2)}, u32[]{:S(2)}) %collective-permute-start.28) | collective-permute-done | bytes 262176 | tf_op jit(solution)/shard_map/ppermute | solution.py:14
  166.1 10.6 %collective-permute-done.30 = f16[2,2,32,2048]{3,2,0,1:T(8,128)(2,1)} collective-permute-done((f16[2,2,32,2048]{3,2,0,1:T(8,128)(2,1)}, f16[2,2,32,2048]{3,2,0,1:T(8,128)(2,1)}, u32[]{:S(2)}, u32[]{:S(2)}) %collective-permute-start.30) | collective-permute-done | bytes 524320 | tf_op jit(solution)/shard_map/ppermute | solution.py:14
  176.7 2.6 %collective-permute-done.31 = f16[2,2,32,2048]{3,2,0,1:T(8,128)(2,1)} collective-permute-done((f16[2,2,32,2048]{3,2,0,1:T(8,128)(2,1)}, f16[2,2,32,2048]{3,2,0,1:T(8,128)(2,1)}, u32[]{:S(2)}, u32[]{:S(2)}) %collective-permute-start.31) | collective-permute-done | bytes 524320 | tf_op jit(solution)/shard_map/ppermute | solution.py:14
  179.3 1.6 fusion.25
  181.0 4.6 %collective-permute-start.32 = (f16[2,32,2048]{2,1,0:T(8,128)(2,1)S(1)}, f16[2,32,2048]{2,1,0:T(8,128)(2,1)S(1)}, u32[]{:S(2)}, u32[]{:S(2)}) collective-permute-start(f16[2,32,2048]{2,1,0:T(8,128)(2,1)S(1)} %fusion.34), channel_id=1, source_target_pairs={{0,32},{32,0},{64,96},{96,64},{128,160},{160,128},{192,224},{224,1... | collective-permute-start | bytes 786440 | tf_op jit(solution)/shard_map/ppermute | solution.py:14
  185.7 10.8 %collective-permute-done.32 = f16[2,32,2048]{2,1,0:T(8,128)(2,1)S(1)} collective-permute-done((f16[2,32,2048]{2,1,0:T(8,128)(2,1)S(1)}, f16[2,32,2048]{2,1,0:T(8,128)(2,1)S(1)}, u32[]{:S(2)}, u32[]{:S(2)}) %collective-permute-start.32) | collective-permute-done | bytes 262176 | tf_op jit(solution)/shard_map/ppermute | solution.py:14
  196.6 1.1 pad_maximum_fusion.2
  (71 shorter events, 4.8 us)
Async XLA Ops:
  0.0 7.2 %copy-start = (s32[2]{0:T(128)S(1)}, s32[2]{0:T(128)}, u32[]{:S(2)}) copy-start(s32[2]{0:T(128)} %param.5) | copy-start | bytes 28
  2.5 15.0 %collective-permute-start = (bf16[128,2048]{1,0:T(8,128)(2,1)}, bf16[128,2048]{1,0:T(8,128)(2,1)S(1)}, u32[]{:S(2)}, u32[]{:S(2)}) collective-permute-start(bf16[128,2048]{1,0:T(8,128)(2,1)} %get-tuple-element.51), channel_id=1, source_target_pairs={{0,8},{1,9},{2,10},{3,11},{4,12},{5,13},{6,14},{7,15},{8,0},{9,1},... | collective-permute-start | bytes 1572872 | tf_op jit(solution)/shard_map/ppermute | solution.py:14
  4.0 25.9 %collective-permute-start.1 = (bf16[128,2048]{1,0:T(8,128)(2,1)S(1)}, bf16[128,2048]{1,0:T(8,128)(2,1)S(1)}, u32[]{:S(2)}, u32[]{:S(2)}) collective-permute-start(bf16[128,2048]{1,0:T(8,128)(2,1)S(1)} %get-tuple-element.50), channel_id=1, source_target_pairs={{0,16},{1,17},{2,18},{3,19},{4,20},{5,21},{6,22},{7,23},{8,24},{9,... | collective-permute-start | bytes 1572872 | tf_op jit(solution)/shard_map/ppermute | solution.py:14
  6.7 25.5 %collective-permute-start.2 = (bf16[128,2048]{1,0:T(8,128)(2,1)S(1)}, bf16[128,2048]{1,0:T(8,128)(2,1)S(1)}, u32[]{:S(2)}, u32[]{:S(2)}) collective-permute-start(bf16[128,2048]{1,0:T(8,128)(2,1)S(1)} %get-tuple-element.49), channel_id=1, source_target_pairs={{0,24},{1,25},{2,26},{3,27},{4,28},{5,29},{6,30},{7,31},{8,16},{9,... | collective-permute-start | bytes 1572872 | tf_op jit(solution)/shard_map/ppermute | solution.py:14
  32.5 6.1 %collective-permute-start.3 = (bf16[2,2,4,8,2048]{4,3,2,1,0:T(8,128)(2,1)S(1)}, bf16[2,2,4,8,2048]{4,3,2,1,0:T(8,128)(2,1)S(1)}, u32[]{:S(2)}, u32[]{:S(2)}) collective-permute-start(bf16[2,2,4,8,2048]{4,3,2,1,0:T(8,128)(2,1)S(1)} %pad_maximum_fusion.4), channel_id=1, source_target_pairs={{0,1},{1,0},{2,3},{3,2},{4,5},{5,4},{6,7},{7,6},{8,9},{9,8},{10,11... | collective-permute-start | bytes 1572872 | tf_op jit(solution)/shard_map/ppermute | solution.py:14
  39.4 8.3 %collective-permute-start.10 = (f32[3,2176]{1,0:T(4,128)S(1)}, f32[3,2176]{1,0:T(4,128)S(1)}, u32[]{:S(2)}, u32[]{:S(2)}) collective-permute-start(f32[3,2176]{1,0:T(4,128)S(1)} %maximum_maximum_fusion), channel_id=1, source_target_pairs={{0,64},{32,96},{64,0},{96,32},{128,192},{160,224},{192,128},{224,1... | collective-permute-start | bytes 78344 | tf_op jit(solution)/shard_map/ppermute | solution.py:14
  41.1 7.1 %collective-permute-start.11 = (f32[3,2176]{1,0:T(4,128)S(1)}, f32[3,2176]{1,0:T(4,128)S(1)}, u32[]{:S(2)}, u32[]{:S(2)}) collective-permute-start(f32[3,2176]{1,0:T(4,128)S(1)} %maximum_maximum_fusion), channel_id=1, source_target_pairs={{0,128},{32,160},{64,192},{96,224},{128,0},{160,32},{192,64},{224,... | collective-permute-start | bytes 78344 | tf_op jit(solution)/shard_map/ppermute | solution.py:14
  44.0 5.1 %collective-permute-start.12 = (f32[3,2176]{1,0:T(4,128)S(1)}, f32[3,2176]{1,0:T(4,128)S(1)}, u32[]{:S(2)}, u32[]{:S(2)}) collective-permute-start(f32[3,2176]{1,0:T(4,128)S(1)} %maximum_maximum_fusion), channel_id=1, source_target_pairs={{0,192},{32,224},{64,128},{96,160},{128,64},{160,96},{192,0},{224,... | collective-permute-start | bytes 78344 | tf_op jit(solution)/shard_map/ppermute | solution.py:14
  44.3 5.2 %collective-permute-start.4 = (bf16[2,2,8,2048]{3,2,1,0:T(8,128)(2,1)S(1)}, bf16[2,2,8,2048]{3,2,1,0:T(8,128)(2,1)S(1)}, u32[]{:S(2)}, u32[]{:S(2)}) collective-permute-start(bf16[2,2,8,2048]{3,2,1,0:T(8,128)(2,1)S(1)} %get-tuple-element.63), channel_id=1, source_target_pairs={{0,2},{1,3},{2,0},{3,1},{4,6},{5,7},{6,4},{7,5},{8,10},{9,11},{10,... | collective-permute-start | bytes 393224 | tf_op jit(solution)/shard_map/ppermute | solution.py:14
  44.5 12.7 %collective-permute-start.5 = (bf16[2,2,8,2048]{3,2,1,0:T(8,128)(2,1)S(1)}, bf16[2,2,8,2048]{3,2,1,0:T(8,128)(2,1)S(1)}, u32[]{:S(2)}, u32[]{:S(2)}) collective-permute-start(bf16[2,2,8,2048]{3,2,1,0:T(8,128)(2,1)S(1)} %get-tuple-element.64), channel_id=1, source_target_pairs={{0,4},{1,5},{2,6},{3,7},{4,0},{5,1},{6,2},{7,3},{8,12},{9,13},{10,... | collective-permute-start | bytes 393224 | tf_op jit(solution)/shard_map/ppermute | solution.py:14
  47.7 12.0 %collective-permute-start.6 = (bf16[2,2,8,2048]{3,2,1,0:T(8,128)(2,1)S(1)}, bf16[2,2,8,2048]{3,2,1,0:T(8,128)(2,1)S(1)}, u32[]{:S(2)}, u32[]{:S(2)}) collective-permute-start(bf16[2,2,8,2048]{3,2,1,0:T(8,128)(2,1)S(1)} %get-tuple-element.65), channel_id=1, source_target_pairs={{0,6},{1,7},{2,4},{3,5},{4,2},{5,3},{6,0},{7,1},{8,14},{9,15},{10,... | collective-permute-start | bytes 393224 | tf_op jit(solution)/shard_map/ppermute | solution.py:14
  59.7 9.9 %collective-permute-start.13 = (f32[3,2176]{1,0:T(4,128)S(1)}, f32[3,2176]{1,0:T(4,128)S(1)}, u32[]{:S(2)}, u32[]{:S(2)}) collective-permute-start(f32[3,2176]{1,0:T(4,128)S(1)} %pad_maximum_fusion.6), channel_id=1, source_target_pairs={{0,32},{32,0},{64,96},{96,64},{128,160},{160,128},{192,224},{224,1... | collective-permute-start | bytes 78344 | tf_op jit(solution)/shard_map/ppermute | solution.py:14
  65.8 6.5 %collective-permute-start.7 = (bf16[2,2,8,2048]{3,2,1,0:T(8,128)(2,1)S(1)}, bf16[2,2,8,2048]{3,2,1,0:T(8,128)(2,1)S(1)}, u32[]{:S(2)}, u32[]{:S(2)}) collective-permute-start(bf16[2,2,8,2048]{3,2,1,0:T(8,128)(2,1)S(1)} %pad_maximum_fusion.5), channel_id=1, source_target_pairs={{0,2},{1,3},{2,0},{3,1},{4,6},{5,7},{6,4},{7,5},{8,10},{9,11},{10,... | collective-permute-start | bytes 393224 | tf_op jit(solution)/shard_map/ppermute | solution.py:14
  65.9 11.4 %collective-permute-start.8 = (bf16[2,2,8,2048]{3,2,1,0:T(8,128)(2,1)S(1)}, bf16[2,2,8,2048]{3,2,1,0:T(8,128)(2,1)S(1)}, u32[]{:S(2)}, u32[]{:S(2)}) collective-permute-start(bf16[2,2,8,2048]{3,2,1,0:T(8,128)(2,1)S(1)} %pad_maximum_fusion.5), channel_id=1, source_target_pairs={{0,4},{1,5},{2,6},{3,7},{4,0},{5,1},{6,2},{7,3},{8,12},{9,13},{10,... | collective-permute-start | bytes 393224 | tf_op jit(solution)/shard_map/ppermute | solution.py:14
  68.4 12.1 %collective-permute-start.9 = (bf16[2,2,8,2048]{3,2,1,0:T(8,128)(2,1)S(1)}, bf16[2,2,8,2048]{3,2,1,0:T(8,128)(2,1)S(1)}, u32[]{:S(2)}, u32[]{:S(2)}) collective-permute-start(bf16[2,2,8,2048]{3,2,1,0:T(8,128)(2,1)S(1)} %pad_maximum_fusion.5), channel_id=1, source_target_pairs={{0,6},{1,7},{2,4},{3,5},{4,2},{5,3},{6,0},{7,1},{8,14},{9,15},{10,... | collective-permute-start | bytes 393224 | tf_op jit(solution)/shard_map/ppermute | solution.py:14
  72.3 8.3 %collective-permute-start.14 = (f32[2,2,2,4,8]{4,3,2,1,0:T(4,128)S(1)}, f32[2,2,2,4,8]{4,3,2,1,0:T(4,128)S(1)}, u32[]{:S(2)}, u32[]{:S(2)}) collective-permute-start(f32[2,2,2,4,8]{4,3,2,1,0:T(4,128)S(1)} %pad_maximum_fusion.7), channel_id=1, source_target_pairs={{0,2},{1,3},{2,0},{3,1},{4,6},{5,7},{6,4},{7,5},{8,10},{9,11},{10,... | collective-permute-start | bytes 3080 | tf_op jit(solution)/shard_map/ppermute | solution.py:14
  73.0 7.6 %collective-permute-start.15 = (f32[2,2,2,4,8]{4,3,2,1,0:T(4,128)S(1)}, f32[2,2,2,4,8]{4,3,2,1,0:T(4,128)S(1)}, u32[]{:S(2)}, u32[]{:S(2)}) collective-permute-start(f32[2,2,2,4,8]{4,3,2,1,0:T(4,128)S(1)} %pad_maximum_fusion.7), channel_id=1, source_target_pairs={{0,4},{1,5},{2,6},{3,7},{4,0},{5,1},{6,2},{7,3},{8,12},{9,13},{10,... | collective-permute-start | bytes 3080 | tf_op jit(solution)/shard_map/ppermute | solution.py:14
  74.8 6.1 %collective-permute-start.16 = (f32[2,2,2,4,8]{4,3,2,1,0:T(4,128)S(1)}, f32[2,2,2,4,8]{4,3,2,1,0:T(4,128)S(1)}, u32[]{:S(2)}, u32[]{:S(2)}) collective-permute-start(f32[2,2,2,4,8]{4,3,2,1,0:T(4,128)S(1)} %pad_maximum_fusion.7), channel_id=1, source_target_pairs={{0,6},{1,7},{2,4},{3,5},{4,2},{5,3},{6,0},{7,1},{8,14},{9,15},{10,... | collective-permute-start | bytes 3080 | tf_op jit(solution)/shard_map/ppermute | solution.py:14
  82.5 10.0 %collective-permute-start.17 = (bf16[9,8,2048]{2,1,0:T(8,128)(2,1)S(1)}, bf16[9,8,2048]{2,1,0:T(8,128)(2,1)S(1)}, u32[]{:S(2)}, u32[]{:S(2)}) collective-permute-start(bf16[9,8,2048]{2,1,0:T(8,128)(2,1)S(1)} %get-tuple-element.71), channel_id=1, source_target_pairs={{0,8},{1,9},{2,10},{3,11},{4,12},{5,13},{6,14},{7,15},{8,0},{9,1},... | collective-permute-start | bytes 884744 | tf_op jit(solution)/shard_map/ppermute | solution.py:14
  82.6 13.5 %collective-permute-start.18 = (bf16[9,8,2048]{2,1,0:T(8,128)(2,1)S(1)}, bf16[9,8,2048]{2,1,0:T(8,128)(2,1)S(1)}, u32[]{:S(2)}, u32[]{:S(2)}) collective-permute-start(bf16[9,8,2048]{2,1,0:T(8,128)(2,1)S(1)} %get-tuple-element.71), channel_id=1, source_target_pairs={{0,16},{1,17},{2,18},{3,19},{4,20},{5,21},{6,22},{7,23},{8,24},{9,... | collective-permute-start | bytes 884744 | tf_op jit(solution)/shard_map/ppermute | solution.py:14
  84.5 14.2 %collective-permute-start.19 = (bf16[9,8,2048]{2,1,0:T(8,128)(2,1)S(1)}, bf16[9,8,2048]{2,1,0:T(8,128)(2,1)S(1)}, u32[]{:S(2)}, u32[]{:S(2)}) collective-permute-start(bf16[9,8,2048]{2,1,0:T(8,128)(2,1)S(1)} %get-tuple-element.71), channel_id=1, source_target_pairs={{0,24},{1,25},{2,26},{3,27},{4,28},{5,29},{6,30},{7,31},{8,16},{9,... | collective-permute-start | bytes 884744 | tf_op jit(solution)/shard_map/ppermute | solution.py:14
  98.8 7.0 %collective-permute-start.20 = (bf16[4,9,8,2048]{3,2,1,0:T(8,128)(2,1)S(1)}, bf16[4,9,8,2048]{3,2,1,0:T(8,128)(2,1)}, u32[]{:S(2)}, u32[]{:S(2)}) collective-permute-start(bf16[4,9,8,2048]{3,2,1,0:T(8,128)(2,1)S(1)} %pad_maximum_fusion), channel_id=1, source_target_pairs={{0,1},{1,0},{2,3},{3,2},{4,5},{5,4},{6,7},{7,6},{8,9},{9,8},{10,11... | collective-permute-start | bytes 3538952 | tf_op jit(solution)/shard_map/ppermute | solution.py:14
  100.4 19.7 %collective-permute-start.24 = (bf16[8,8,2048]{2,1,0:T(8,128)(2,1)S(1)}, bf16[8,8,2048]{2,1,0:T(8,128)(2,1)S(1)}, u32[]{:S(2)}, u32[]{:S(2)}) collective-permute-start(bf16[8,8,2048]{2,1,0:T(8,128)(2,1)S(1)} %bitcast.135), channel_id=1, source_target_pairs={{0,8},{1,9},{2,10},{3,11},{4,12},{5,13},{6,14},{7,15},{8,0},{9,1},... | collective-permute-start | bytes 786440 | tf_op jit(solution)/shard_map/ppermute | solution.py:14
  100.5 19.6 %collective-permute-start.25 = (bf16[8,8,2048]{2,1,0:T(8,128)(2,1)S(1)}, bf16[8,8,2048]{2,1,0:T(8,128)(2,1)S(1)}, u32[]{:S(2)}, u32[]{:S(2)}) collective-permute-start(bf16[8,8,2048]{2,1,0:T(8,128)(2,1)S(1)} %bitcast.136), channel_id=1, source_target_pairs={{0,16},{1,17},{2,18},{3,19},{4,20},{5,21},{6,22},{7,23},{8,24},{9,... | collective-permute-start | bytes 786440 | tf_op jit(solution)/shard_map/ppermute | solution.py:14
  104.7 15.4 %collective-permute-start.26 = (bf16[8,8,2048]{2,1,0:T(8,128)(2,1)S(1)}, bf16[8,8,2048]{2,1,0:T(8,128)(2,1)S(1)}, u32[]{:S(2)}, u32[]{:S(2)}) collective-permute-start(bf16[8,8,2048]{2,1,0:T(8,128)(2,1)S(1)} %bitcast.137), channel_id=1, source_target_pairs={{0,24},{1,25},{2,26},{3,27},{4,28},{5,29},{6,30},{7,31},{8,16},{9,... | collective-permute-start | bytes 786440 | tf_op jit(solution)/shard_map/ppermute | solution.py:14
  120.2 4.3 %collective-permute-start.27 = (bf16[4,8,8,2048]{3,2,1,0:T(8,128)(2,1)S(1)}, bf16[4,8,8,2048]{3,2,1,0:T(8,128)(2,1)S(1)}, u32[]{:S(2)}, u32[]{:S(2)}) collective-permute-start(bf16[4,8,8,2048]{3,2,1,0:T(8,128)(2,1)S(1)} %pad_maximum_fusion.1), channel_id=1, source_target_pairs={{0,1},{1,0},{2,3},{3,2},{4,5},{5,4},{6,7},{7,6},{8,9},{9,8},{10,11... | collective-permute-start | bytes 3145736 | tf_op jit(solution)/shard_map/ppermute | solution.py:14
  120.4 16.6 %collective-permute-start.22 = (f16[2,2,32,2048]{3,2,0,1:T(8,128)(2,1)}, f16[2,2,32,2048]{3,2,0,1:T(8,128)(2,1)S(1)}, u32[]{:S(2)}, u32[]{:S(2)}) collective-permute-start(f16[2,2,32,2048]{3,2,0,1:T(8,128)(2,1)} %fusion.29), channel_id=1, source_target_pairs={{0,128},{32,160},{64,192},{96,224},{128,0},{160,32},{192,64},{224,... | collective-permute-start | bytes 1572872 | tf_op jit(solution)/shard_map/ppermute | solution.py:14
  121.9 25.5 %collective-permute-start.21 = (f16[2,2,32,2048]{3,2,0,1:T(8,128)(2,1)}, f16[2,2,32,2048]{3,2,0,1:T(8,128)(2,1)S(1)}, u32[]{:S(2)}, u32[]{:S(2)}) collective-permute-start(f16[2,2,32,2048]{3,2,0,1:T(8,128)(2,1)} %fusion.28), channel_id=1, source_target_pairs={{0,64},{32,96},{64,0},{96,32},{128,192},{160,224},{192,128},{224,1... | collective-permute-start | bytes 1572872 | tf_op jit(solution)/shard_map/ppermute | solution.py:14
  123.8 23.8 %collective-permute-start.23 = (f16[2,2,32,2048]{3,2,1,0:T(8,128)(2,1)}, f16[2,2,32,2048]{3,2,1,0:T(8,128)(2,1)S(1)}, u32[]{:S(2)}, u32[]{:S(2)}) collective-permute-start(f16[2,2,32,2048]{3,2,1,0:T(8,128)(2,1)} %get-tuple-element.41), channel_id=1, source_target_pairs={{0,192},{32,224},{64,128},{96,160},{128,64},{160,96},{192,0},{224,... | collective-permute-start | bytes 1572872 | tf_op jit(solution)/shard_map/ppermute | solution.py:14
  148.2 17.9 %collective-permute-start.28 = (f16[2,32,2048]{2,1,0:T(8,128)(2,1)S(1)}, f16[2,32,2048]{2,1,0:T(8,128)(2,1)S(1)}, u32[]{:S(2)}, u32[]{:S(2)}) collective-permute-start(f16[2,32,2048]{2,1,0:T(8,128)(2,1)S(1)} %fusion.35), channel_id=1, source_target_pairs={{0,32},{32,0},{64,96},{96,64},{128,160},{160,128},{192,224},{224,1... | collective-permute-start | bytes 786440 | tf_op jit(solution)/shard_map/ppermute | solution.py:14
  149.4 16.7 %collective-permute-start.29 = (f16[2,2,32,2048]{3,2,0,1:T(8,128)(2,1)}, f16[2,2,32,2048]{3,2,0,1:T(8,128)(2,1)S(1)}, u32[]{:S(2)}, u32[]{:S(2)}) collective-permute-start(f16[2,2,32,2048]{3,2,0,1:T(8,128)(2,1)} %fusion.30), channel_id=1, source_target_pairs={{0,64},{32,96},{64,0},{96,32},{128,192},{160,224},{192,128},{224,1... | collective-permute-start | bytes 1572872 | tf_op jit(solution)/shard_map/ppermute | solution.py:14
  149.7 27.0 %collective-permute-start.30 = (f16[2,2,32,2048]{3,2,0,1:T(8,128)(2,1)}, f16[2,2,32,2048]{3,2,0,1:T(8,128)(2,1)}, u32[]{:S(2)}, u32[]{:S(2)}) collective-permute-start(f16[2,2,32,2048]{3,2,0,1:T(8,128)(2,1)} %fusion.31), channel_id=1, source_target_pairs={{0,128},{32,160},{64,192},{96,224},{128,0},{160,32},{192,64},{224,... | collective-permute-start | bytes 1572872 | tf_op jit(solution)/shard_map/ppermute | solution.py:14
  153.5 25.8 %collective-permute-start.31 = (f16[2,2,32,2048]{3,2,0,1:T(8,128)(2,1)}, f16[2,2,32,2048]{3,2,0,1:T(8,128)(2,1)}, u32[]{:S(2)}, u32[]{:S(2)}) collective-permute-start(f16[2,2,32,2048]{3,2,0,1:T(8,128)(2,1)} %fusion.32), channel_id=1, source_target_pairs={{0,192},{32,224},{64,128},{96,160},{128,64},{160,96},{192,0},{224,... | collective-permute-start | bytes 1572872 | tf_op jit(solution)/shard_map/ppermute | solution.py:14
  181.0 15.5 %collective-permute-start.32 = (f16[2,32,2048]{2,1,0:T(8,128)(2,1)S(1)}, f16[2,32,2048]{2,1,0:T(8,128)(2,1)S(1)}, u32[]{:S(2)}, u32[]{:S(2)}) collective-permute-start(f16[2,32,2048]{2,1,0:T(8,128)(2,1)S(1)} %fusion.34), channel_id=1, source_target_pairs={{0,32},{32,0},{64,96},{96,64},{128,160},{160,128},{192,224},{224,1... | collective-permute-start | bytes 786440 | tf_op jit(solution)/shard_map/ppermute | solution.py:14

commit v2 on v0

--- a/solution.py
+++ b/solution.py
@@ -34,6 +34,11 @@
 
 
 def after(value, others):
+    token, others = lax.optimization_barrier((lax.create_token(), others))
+    return lax.optimization_barrier((token, value))[1], others
+
+
+def beside(value, others):
     return lax.optimization_barrier((value, others))[0]
 
 
@@ -48,8 +53,9 @@
     by_x = second_plane.reshape(4, 128, shard)
     piece = lambda bits: lax.dynamic_index_in_dim(by_x, my_x ^ bits, 0, keepdims=False)
     from_x = [piece(0)] + [swap(piece(bits), "samp", 8 * bits) for bits in (1, 2, 3)]
-    first_plane = after(first_plane, from_x[0])
+    first_plane, from_x[0] = after(first_plane, from_x[0])
     first_local = row_stats(first_plane)
+    from_x, first_local = after(from_x, first_local)
     halves = [
         pick(my_x ^ own_x[p], from_x).reshape(CHUNKS, 2, 4, -1, shard) for p in range(2)
     ]
@@ -67,7 +73,7 @@
     column_local = row_stats(column).reshape(3, -1)
     stats = jnp.concatenate([first_local, column_local], axis=1)
     stats = merge([stats] + [swap(stats, "mem", bits) for bits in (2, 4, 6)])
-    stats = after(stats, from_z[1:])
+    stats, from_z[1] = after(stats, from_z[1])
     stats = merge([stats, swap(stats, "mem", 1)])
     mean, span = stats[0] / members, stats[1] + stats[2]
     first_mean = mean[:samples]
@@ -75,7 +81,7 @@
 
     mine = jnp.stack([pick(my_z ^ own_z[p], [f[p] for f in from_z]) for p in range(2)])
     parts = [mine] + [swap(mine, "samp", 2 * bits) for bits in (1, 2, 3)]
-    facts = after(facts, parts[1])
+    facts, parts[1] = after(facts, parts[1])
     facts_z = [facts] + [swap(facts, "samp", 2 * bits) for bits in (1, 2, 3)]
     facts = jnp.stack([pick(my_z ^ own_z[p], [f[:, p] for f in facts_z]) for p in range(2)], 1)
     line = jnp.stack([pick(my_z ^ place, parts) for place in range(4)], 2)
@@ -85,39 +91,39 @@
     mark = jnp.broadcast_to(bound, (1, eighth, shard)).astype(BF16)
 
     first_anom = (first_plane.astype(F32) - first_mean[:, None]).astype(BF16)
-    rows = 4 * eighth
     gathered = []
     for chunk in range(CHUNKS):
         sent = line[:, chunk].reshape(tiles, eighth, shard)
         if chunk == 0:
             sent = jnp.concatenate([sent, mark])
         else:
-            sent = after(sent, gathered[0][1])
+            sent = beside(sent, gathered[0][1])
         gathered.append([sent] + [swap(sent, "samp", 8 * bits) for bits in (1, 2, 3)])
 
+    gathered[0], first_anom = after(gathered[0], first_anom)
     blocks, arrived = [], []
     for chunk in range(CHUNKS):
         if chunk > 0:
-            gathered[chunk] = after(gathered[chunk], arrived[-1][0])
+            gathered[chunk] = beside(gathered[chunk], sent)
         near = jnp.stack(gathered[chunk])
-        far = swap(near, "samp", 1)
+        panel_anom = jnp.stack([near, swap(near, "samp", 1)])
         if chunk == 0:
-            marks = jnp.stack([near[:, tiles, 0, :128], far[:, tiles, 0, :128]])
+            marks = panel_anom[:, :, tiles, 0, :128].astype(F32)
             shrink_first = 4.0 / jnp.maximum(jnp.max(span[:samples]), 1e-30)
-            shrink_panel = 1.0 / jnp.maximum(jnp.max(marks.astype(F32)), 1e-30)
+            shrink_panel = 1.0 / jnp.maximum(jnp.max(marks), 1e-30)
             grow_first, grow_panel = 1.0 / shrink_first, 1.0 / shrink_panel
-        panel_anom = jnp.stack([near[:, :tiles], far[:, :tiles]])
+        height = panel_anom.shape[2]
         shares = lax.dot_general(
-            panel_anom.reshape(16 * rows, shard),
+            panel_anom.reshape(-1, shard),
             first_anom,
             (((1,), (1,)), ((), ())),
             preferred_element_type=F32,
-        ).reshape(2, 2, 2, 2, rows, samples)
+        ).reshape(2, 2, 2, height, eighth, samples)
 
         def for_y(dest):
-            start = (0, (dest & 1) ^ (my_x >> 1), 0, dest >> 1, 0, 0)
-            block = lax.dynamic_slice(shares, start, (2, 1, 2, 1, rows, samples))
-            return block.reshape(2, 2, rows, samples)
+            start = (0, (dest & 1) ^ (my_x >> 1), 0, 4 * (dest >> 1), 0, 0)
+            block = lax.dynamic_slice(shares, start, (2, 1, 2, 4, eighth, samples))
+            return block.reshape(2, 2, 4, eighth, samples)
 
         sent = [
             (for_y(my_y ^ bits) * shrink_first * shrink_panel).astype(WIRE) for bits in (1, 2, 3)
@@ -128,15 +134,19 @@
     results = []
     for chunk in range(CHUNKS):
         if chunk + 1 < CHUNKS:
-            arrived[chunk] = after(arrived[chunk], sent)
-        total = blocks[chunk]
-        for value in arrived[chunk]:
-            total += value.astype(F32) * grow_panel * grow_first
-        for_z = lambda dest: lax.dynamic_index_in_dim(total, dest ^ (my_x & 1), 1, keepdims=False)
+            arrived[chunk] = beside(arrived[chunk], sent)
+
+        def for_z(dest):
+            part = lambda v: lax.dynamic_index_in_dim(v, dest ^ (my_x & 1), 1, keepdims=False)
+            total = part(blocks[chunk])
+            for value in arrived[chunk]:
+                total += part(value).astype(F32) * grow_panel * grow_first
+            return total
+
         other = (for_z(1 - my_zh) * shrink_first * shrink_panel).astype(WIRE)
         total = for_z(my_zh) + swap(other, "mem", 1).astype(F32) * grow_panel * grow_first
         results += [pick(my_core ^ core, [total[0], total[1]]) / (members - 1) for core in range(2)]
-    return jnp.concatenate(results, axis=0)
+    return jnp.stack(results).reshape(-1, samples)
 
 
 def solution(mesh):

time: 218 us -> 200 us (0.917)
  waiting for transfers between devices: 112 us -> 82.5 us
  other arithmetic: 24.8 us -> 31.3 us
  local copies, waits for them, and re-layouts: 6.11 us -> 10.2 us
  starting transfers between devices: 51.8 us -> 54.5 us
    ppermute x33, waiting for transfers between devices: 112 us -> 82.5 us  [swap(): return lax.ppermute(value, axis, [(i, i ^ bits) for i in range(size)])]
    convert_element_type x0 -> x1, other arithmetic: none -> 8.07 us  [per_device(): first_anom = (first_plane.astype(F32) - first_mean[:, None]).astype(BF16)]
    convert_element_type x6, other arithmetic: 4.23 us -> 0.87 us  [per_device(): (for_y(my_y ^ bits) * shrink_first * shrink_panel).astype(WIRE)]
    convert_element_type x2, other arithmetic: 0.15 us -> 3.03 us  [per_device(): other = (for_z(1 - my_zh) * shrink_first * shrink_panel).astype(WIRE)]
    add x2, other arithmetic: 0.16 us -> 2.95 us  [per_device(): for_z(my_zh) + swap(other, 'mem', 1).astype(F32) * grow_panel * grow_first]
    ppermute x33, starting transfers between devices: 51.8 us -> 54.5 us  [swap(): return lax.ppermute(value, axis, [(i, i ^ bits) for i in range(size)])]
    slice x3, local copies, waits for them, and re-layouts: 0.07 us -> 2.43 us  [per_device(): sent = line[:, chunk].reshape(tiles, eighth, shard)]
    unnamed x4 -> x12, local copies, waits for them, and re-layouts: 0.83 us -> 3.14 us
  transfers between devices with their start and end apart: 33 -> 33, of which waited for: 25 -> 21; matrix products, arithmetic and copies ran while one was open for 12% -> 21% of each run, Pallas kernels for 0% -> 0%
where the time goes in v2:
time: 200 us
  waiting for transfers between devices  82.5 us (41%)
  starting transfers between devices  54.5 us (27%)
  other arithmetic  31.3 us (16%)
  matrix products  14.7 us (7%)
  local copies, waits for them, and re-layouts  10.2 us (5%)
  between operations  6.44 us (3%)
    ppermute x33, waiting for transfers between devices, swap(): return lax.ppermute(value, axis, [(i, i ^ bits) for i in range(size)])  82.5 us
    ppermute x33, starting transfers between devices, swap(): return lax.ppermute(value, axis, [(i, i ^ bits) for i in range(size)])  54.5 us
    dot_general x2, matrix products, per_device(): lax.dot_general(panel_anom.reshape(-1, shard), first_anom, (((1,), (1,)),...  14.7 us
    convert_element_type x1, other arithmetic, per_device(): first_anom = (first_plane.astype(F32) - first_mean[:, None]).astype(BF16)  8.07 us
    reduce_sum x2, other arithmetic, row_stats(): return jnp.stack([jnp.sum(wide, -1), jnp.max(wide, -1), jnp.max(-wide, -1)])  6.29 us
    reduce_max x3, other arithmetic, row_stats(): return jnp.stack([jnp.sum(wide, -1), jnp.max(wide, -1), jnp.max(-wide, -1)])  4.74 us
  transfers between devices with their start and end apart: 33, of which 21 were waited for; matrix products, arithmetic and copies ran while one was open for 21% of the time, Pallas kernels for 0%

profile of v2, /device:TPU:32, one launch (start us, length us, event | category | flops | bytes accessed | tf_op | source)
XLA Modules:
  0.0 199.7 jit_solution(9905410829601320954)
XLA Ops:
  0.0 2.5 %dynamic-slice_bitcast_fusion = (bf16[128,2048]{1,0:T(8,128)(2,1)S(1)}, bf16[128,2048]{1,0:T(8,128)(2,1)S(1)}, bf16[128,2048]{1,0:T(8,128)(2,1)}, bf16[128,2048]{1,0:T(8,128)(2,1)S(1)}) fusion(bf16[4,128,2048]{2,1,0:T(8,128)(2,1)} %bitcast.167, s32[]{:T(128)S(6)} %select_n.355, s32[]{:T(128)S(6)} %select_n.354, s32[]{:T(128)S(6)} %select_n.353, s32[]{:T(128)S(6)} %select_n.350), kind=kLoop, calls=%fused_computation.78 | loop fusion | bytes 4194320 | tf_op jit(solution)/shard_map/jit(dynamic_index_in_dim)/squeeze | solution.py:54
  2.5 1.5 collective-permute-start
  4.0 2.7 %collective-permute-start.1 = (bf16[128,2048]{1,0:T(8,128)(2,1)S(1)}, bf16[128,2048]{1,0:T(8,128)(2,1)S(1)}, u32[]{:S(2)}, u32[]{:S(2)}) collective-permute-start(bf16[128,2048]{1,0:T(8,128)(2,1)S(1)} %get-tuple-element.76), channel_id=1, source_target_pairs={{0,16},{1,17},{2,18},{3,19},{4,20},{5,21},{6,22},{7,23},{8,24},{9,... | collective-permute-start | bytes 1572872 | tf_op jit(solution)/shard_map/ppermute | solution.py:14
  6.7 0.5 collective-permute-start.2
  7.2 6.0 %convert_reduce_fusion = (f32[2048]{0:T(1024)S(1)}, f32[2048]{0:T(1024)S(1)}) fusion(bf16[2048,2048]{1,0:T(8,128)(2,1)} %param.3), kind=kLoop, calls=%fused_computation.2 | loop fusion | flops 16773120 | bytes 8404992 | tf_op jit(solution)/shard_map/reduce_sum | solution.py:26
  13.3 0.6 fusion.64
  15.2 4.6 %reduce_max.82 = bf16[2048]{0:T(1024)(128)(2,1)S(1)} reduce(bf16[2048,2048]{1,0:T(8,128)(2,1)} %param.3, bf16[]{:T(256)} %constant.221.clone.1), dimensions={1}, to_apply=%region_1.2 | reduce | flops 4192256 | bytes 8392706 | tf_op jit(solution)/shard_map/reduce_max | solution.py:26
  19.8 10.1 %collective-permute-done.1 = bf16[128,2048]{1,0:T(8,128)(2,1)S(1)} collective-permute-done((bf16[128,2048]{1,0:T(8,128)(2,1)S(1)}, bf16[128,2048]{1,0:T(8,128)(2,1)S(1)}, u32[]{:S(2)}, u32[]{:S(2)}) %collective-permute-start.1) | collective-permute-done | bytes 524320 | tf_op jit(solution)/shard_map/ppermute | solution.py:14
  29.9 2.4 %collective-permute-done.2 = bf16[128,2048]{1,0:T(8,128)(2,1)S(1)} collective-permute-done((bf16[128,2048]{1,0:T(8,128)(2,1)S(1)}, bf16[128,2048]{1,0:T(8,128)(2,1)S(1)}, u32[]{:S(2)}, u32[]{:S(2)}) %collective-permute-start.2) | collective-permute-done | bytes 524320 | tf_op jit(solution)/shard_map/ppermute | solution.py:14
  32.6 0.7 fusion.62
  36.7 1.7 collective-permute-start.5
  38.4 2.9 %collective-permute-start.6 = (f32[3,2176]{1,0:T(4,128)S(1)}, f32[3,2176]{1,0:T(4,128)S(1)}, u32[]{:S(2)}, u32[]{:S(2)}) collective-permute-start(f32[3,2176]{1,0:T(4,128)S(1)} %maximum_maximum_fusion), channel_id=1, source_target_pairs={{0,128},{32,160},{64,192},{96,224},{128,0},{160,32},{192,64},{224,... | collective-permute-start | bytes 78344 | tf_op jit(solution)/shard_map/ppermute | solution.py:14
  41.7 3.7 %collective-permute-start.10 = (bf16[2,2,8,2048]{3,2,1,0:T(8,128)(2,1)S(1)}, bf16[2,2,8,2048]{3,2,1,0:T(8,128)(2,1)S(1)}, u32[]{:S(2)}, u32[]{:S(2)}) collective-permute-start(bf16[2,2,8,2048]{3,2,1,0:T(8,128)(2,1)S(1)} %get-tuple-element.93), channel_id=1, source_target_pairs={{0,6},{1,7},{2,4},{3,5},{4,2},{5,3},{6,0},{7,1},{8,14},{9,15},{10,... | collective-permute-start | bytes 393224 | tf_op jit(solution)/shard_map/ppermute | solution.py:14
  45.5 0.6 collective-permute-start.9
  46.0 0.4 collective-permute-done.7
  46.7 7.5 %collective-permute-start.8 = (f32[3,2176]{1,0:T(4,128)S(1)}, f32[3,2176]{1,0:T(4,128)S(1)}, u32[]{:S(2)}, u32[]{:S(2)}) collective-permute-start(f32[3,2176]{1,0:T(4,128)S(1)} %pad_maximum_fusion.6), channel_id=1, source_target_pairs={{0,32},{32,0},{64,96},{96,64},{128,160},{160,128},{192,224},{224,1... | collective-permute-start | bytes 78344 | tf_op jit(solution)/shard_map/ppermute | solution.py:14
  54.2 1.9 collective-permute-done.10
  56.1 1.6 collective-permute-done.9
  57.8 2.3 %collective-permute-start.11 = (bf16[2,2,8,2048]{3,2,1,0:T(8,128)(2,1)S(1)}, bf16[2,2,8,2048]{3,2,1,0:T(8,128)(2,1)S(1)}, u32[]{:S(2)}, u32[]{:S(2)}) collective-permute-start(bf16[2,2,8,2048]{3,2,1,0:T(8,128)(2,1)S(1)} %pad_maximum_fusion.5), channel_id=1, source_target_pairs={{0,2},{1,3},{2,0},{3,1},{4,6},{5,7},{6,4},{7,5},{8,10},{9,11},{10,... | collective-permute-start | bytes 393224 | tf_op jit(solution)/shard_map/ppermute | solution.py:14
  60.1 1.4 collective-permute-start.12
  62.2 1.9 collective-permute-done.11
  64.0 2.5 %collective-permute-start.14 = (f32[2,2,2,4,8]{4,3,2,1,0:T(4,128)S(1)}, f32[2,2,2,4,8]{4,3,2,1,0:T(4,128)S(1)}, u32[]{:S(2)}, u32[]{:S(2)}) collective-permute-start(f32[2,2,2,4,8]{4,3,2,1,0:T(4,128)S(1)} %pad_maximum_fusion.8), channel_id=1, source_target_pairs={{0,2},{1,3},{2,0},{3,1},{4,6},{5,7},{6,4},{7,5},{8,10},{9,11},{10,... | collective-permute-start | bytes 3080 | tf_op jit(solution)/shard_map/ppermute | solution.py:14
  66.5 1.1 collective-permute-start.15
  67.7 0.6 collective-permute-start.16
  68.3 2.6 %collective-permute-done.12 = bf16[2,2,8,2048]{3,2,1,0:T(8,128)(2,1)S(1)} collective-permute-done((bf16[2,2,8,2048]{3,2,1,0:T(8,128)(2,1)S(1)}, bf16[2,2,8,2048]{3,2,1,0:T(8,128)(2,1)S(1)}, u32[]{:S(2)}, u32[]{:S(2)}) %collective-permute-start.12) | collective-permute-done | bytes 131104 | tf_op jit(solution)/shard_map/ppermute | solution.py:14
  70.9 3.0 %collective-permute-done.13 = bf16[2,2,8,2048]{3,2,1,0:T(8,128)(2,1)S(1)} collective-permute-done((bf16[2,2,8,2048]{3,2,1,0:T(8,128)(2,1)S(1)}, bf16[2,2,8,2048]{3,2,1,0:T(8,128)(2,1)S(1)}, u32[]{:S(2)}, u32[]{:S(2)}) %collective-permute-start.13) | collective-permute-done | bytes 131104 | tf_op jit(solution)/shard_map/ppermute | solution.py:14
  74.3 0.6 fusion.52
  75.1 0.7 fusion.61
  76.6 1.9 collective-permute-start.18
  78.5 2.8 %collective-permute-start.19 = (bf16[9,8,2048]{2,1,0:T(8,128)(2,1)S(1)}, bf16[9,8,2048]{2,1,0:T(8,128)(2,1)S(1)}, u32[]{:S(2)}, u32[]{:S(2)}) collective-permute-start(bf16[9,8,2048]{2,1,0:T(8,128)(2,1)S(1)} %concatenate.15), channel_id=1, source_target_pairs={{0,24},{1,25},{2,26},{3,27},{4,28},{5,29},{6,30},{7,31},{8,16},{9,... | collective-permute-start | bytes 884744 | tf_op jit(solution)/shard_map/ppermute | solution.py:14
  81.3 8.1 %fusion.1 = bf16[2048,2048]{1,0:T(8,128)(2,1)} fusion(bf16[2048,2048]{1,0:T(8,128)(2,1)} %param.3, f32[2048]{0:T(1024)S(1)} %bitcast.178), kind=kLoop, calls=%fused_computation.4 | loop fusion | flops 12582912 | bytes 16785408 | tf_op jit(solution)/shard_map/convert_element_type | solution.py:93
  89.3 1.0 collective-permute-done.18
  90.3 2.6 %collective-permute-done.19 = bf16[9,8,2048]{2,1,0:T(8,128)(2,1)S(1)} collective-permute-done((bf16[9,8,2048]{2,1,0:T(8,128)(2,1)S(1)}, bf16[9,8,2048]{2,1,0:T(8,128)(2,1)S(1)}, u32[]{:S(2)}, u32[]{:S(2)}) %collective-permute-start.19) | collective-permute-done | bytes 294944 | tf_op jit(solution)/shard_map/ppermute | solution.py:14
  93.3 0.7 slice_reduce_fusion
  94.7 1.7 copy.37
  96.4 4.2 %collective-permute-start.25 = (bf16[8,8,2048]{2,1,0:T(8,128)(2,1)}, bf16[8,8,2048]{2,1,0:T(8,128)(2,1)}, u32[]{:S(2)}, u32[]{:S(2)}) collective-permute-start(bf16[8,8,2048]{2,1,0:T(8,128)(2,1)} %bitcast.47), channel_id=1, source_target_pairs={{0,16},{1,17},{2,18},{3,19},{4,20},{5,21},{6,22},{7,23},{8,24},{9,... | collective-permute-start | bytes 786440 | tf_op jit(solution)/shard_map/ppermute | solution.py:14
  100.6 0.5 collective-permute-start.26
  101.1 0.6 fusion.57
  102.4 7.5 %fusion.4 = f32[2,2,2,9,8,2048]{5,4,3,2,1,0:T(8,128)S(1)} fusion(bf16[2048,2048]{1,0:T(8,128)(2,1)} %fusion.1, bf16[1,2,2,9,8,2048]{5,4,3,2,1,0:T(8,128)(2,1)S(1)} %bitcast.171, bf16[1,2,2,9,8,2048]{5,4,3,2,1,0:T(8,128)(2,1)S(1)} %bitcast.169), kind=kOutput, calls=%fused_computation.7 | convolution fusion | flops 4833017856 | bytes 15466496 | tf_op jit(solution)/shard_map/dot_general | solution.py:116
  110.4 1.7 copy-done.1
  112.1 1.1 collective-permute-done.25
  113.2 2.6 %collective-permute-done.26 = bf16[8,8,2048]{2,1,0:T(8,128)(2,1)} collective-permute-done((bf16[8,8,2048]{2,1,0:T(8,128)(2,1)}, bf16[8,8,2048]{2,1,0:T(8,128)(2,1)}, u32[]{:S(2)}, u32[]{:S(2)}) %collective-permute-start.26) | collective-permute-done | bytes 262176 | tf_op jit(solution)/shard_map/ppermute | solution.py:14
  115.8 1.3 pad_maximum_fusion.1
  117.3 2.0 collective-permute-start.22
  119.3 1.9 collective-permute-start.21
  121.2 0.3 collective-permute-start.23
  121.5 7.2 %fusion.2 = f32[2,2,2,8,8,2048]{5,4,3,2,1,0:T(8,128)S(1)} fusion(bf16[2048,2048]{1,0:T(8,128)(2,1)} %fusion.1, bf16[1,2,2,8,8,2048]{5,4,3,2,1,0:T(8,128)(2,1)} %bitcast.53, bf16[1,2,2,8,8,2048]{5,4,3,2,1,0:T(8,128)(2,1)S(1)} %bitcast.173), kind=kOutput, calls=%fused_computation.5 | convolution fusion | flops 4296015872 | bytes 14680064 | tf_op jit(solution)/shard_map/dot_general | solution.py:116
  129.3 1.4 copy-done
  130.8 2.9 %collective-permute-done.22 = f16[2,2,4,8,2048]{4,3,2,0,1:T(8,128)(2,1)S(1)} collective-permute-done((f16[2,2,4,8,2048]{4,3,2,0,1:T(8,128)(2,1)S(1)}, f16[2,2,4,8,2048]{4,3,2,0,1:T(8,128)(2,1)S(1)}, u32[]{:S(2)}, u32[]{:S(2)}) %collective-permute-start.22) | collective-permute-done | bytes 524320 | tf_op jit(solution)/shard_map/ppermute | solution.py:14
  133.7 10.9 %collective-permute-done.21 = f16[2,2,4,8,2048]{4,3,2,0,1:T(8,128)(2,1)S(1)} collective-permute-done((f16[2,2,4,8,2048]{4,3,2,0,1:T(8,128)(2,1)S(1)}, f16[2,2,4,8,2048]{4,3,2,0,1:T(8,128)(2,1)S(1)}, u32[]{:S(2)}, u32[]{:S(2)}) %collective-permute-start.21) | collective-permute-done | bytes 524320 | tf_op jit(solution)/shard_map/ppermute | solution.py:14
  144.6 1.7 fusion.35
  146.3 4.8 %collective-permute-start.28 = (f16[2,4,8,2048]{3,2,1,0:T(8,128)(2,1)S(1)}, f16[2,4,8,2048]{3,2,1,0:T(8,128)(2,1)}, u32[]{:S(2)}, u32[]{:S(2)}) collective-permute-start(f16[2,4,8,2048]{3,2,1,0:T(8,128)(2,1)S(1)} %fusion.35), channel_id=1, source_target_pairs={{0,32},{32,0},{64,96},{96,64},{128,160},{160,128},{192,224},{224,1... | collective-permute-start | bytes 786440 | tf_op jit(solution)/shard_map/ppermute | solution.py:14
  151.2 3.8 %collective-permute-start.30 = (f16[2,2,4,8,2048]{4,3,2,0,1:T(8,128)(2,1)S(1)}, f16[2,2,4,8,2048]{4,3,2,0,1:T(8,128)(2,1)S(1)}, u32[]{:S(2)}, u32[]{:S(2)}) collective-permute-start(f16[2,2,4,8,2048]{4,3,2,0,1:T(8,128)(2,1)S(1)} %fusion.27), channel_id=1, source_target_pairs={{0,128},{32,160},{64,192},{96,224},{128,0},{160,32},{192,64},{224,... | collective-permute-start | bytes 1572872 | tf_op jit(solution)/shard_map/ppermute | solution.py:14
  155.0 0.9 collective-permute-start.31
  155.9 7.3 %collective-permute-done.28 = f16[2,4,8,2048]{3,2,1,0:T(8,128)(2,1)} collective-permute-done((f16[2,4,8,2048]{3,2,1,0:T(8,128)(2,1)S(1)}, f16[2,4,8,2048]{3,2,1,0:T(8,128)(2,1)}, u32[]{:S(2)}, u32[]{:S(2)}) %collective-permute-start.28) | collective-permute-done | bytes 262176 | tf_op jit(solution)/shard_map/ppermute | solution.py:14
  163.3 1.6 fusion.36
  164.9 1.1 collective-permute-done.29
  166.0 11.9 %collective-permute-done.30 = f16[2,2,4,8,2048]{4,3,2,0,1:T(8,128)(2,1)S(1)} collective-permute-done((f16[2,2,4,8,2048]{4,3,2,0,1:T(8,128)(2,1)S(1)}, f16[2,2,4,8,2048]{4,3,2,0,1:T(8,128)(2,1)S(1)}, u32[]{:S(2)}, u32[]{:S(2)}) %collective-permute-start.30) | collective-permute-done | bytes 524320 | tf_op jit(solution)/shard_map/ppermute | solution.py:14
  177.9 2.7 %collective-permute-done.31 = f16[2,2,4,8,2048]{4,3,2,0,1:T(8,128)(2,1)S(1)} collective-permute-done((f16[2,2,4,8,2048]{4,3,2,0,1:T(8,128)(2,1)S(1)}, f16[2,2,4,8,2048]{4,3,2,0,1:T(8,128)(2,1)S(1)}, u32[]{:S(2)}, u32[]{:S(2)}) %collective-permute-start.31) | collective-permute-done | bytes 524320 | tf_op jit(solution)/shard_map/ppermute | solution.py:14
  180.5 1.3 fusion.31
  181.9 1.3 collective-permute-start.32
  183.2 14.0 %collective-permute-done.32 = f16[2,4,8,2048]{3,2,1,0:T(8,128)(2,1)S(1)} collective-permute-done((f16[2,4,8,2048]{3,2,1,0:T(8,128)(2,1)S(1)}, f16[2,4,8,2048]{3,2,1,0:T(8,128)(2,1)S(1)}, u32[]{:S(2)}, u32[]{:S(2)}) %collective-permute-start.32) | collective-permute-done | bytes 262176 | tf_op jit(solution)/shard_map/ppermute | solution.py:14
  197.3 1.3 fusion.32
  198.6 1.1 pad_maximum_fusion.2
  (78 shorter events, 4.9 us)
Async XLA Ops:
  2.5 17.3 %collective-permute-start = (bf16[128,2048]{1,0:T(8,128)(2,1)}, bf16[128,2048]{1,0:T(8,128)(2,1)S(1)}, u32[]{:S(2)}, u32[]{:S(2)}) collective-permute-start(bf16[128,2048]{1,0:T(8,128)(2,1)} %get-tuple-element.77), channel_id=1, source_target_pairs={{0,8},{1,9},{2,10},{3,11},{4,12},{5,13},{6,14},{7,15},{8,0},{9,1},... | collective-permute-start | bytes 1572872 | tf_op jit(solution)/shard_map/ppermute | solution.py:14
  4.0 25.9 %collective-permute-start.1 = (bf16[128,2048]{1,0:T(8,128)(2,1)S(1)}, bf16[128,2048]{1,0:T(8,128)(2,1)S(1)}, u32[]{:S(2)}, u32[]{:S(2)}) collective-permute-start(bf16[128,2048]{1,0:T(8,128)(2,1)S(1)} %get-tuple-element.76), channel_id=1, source_target_pairs={{0,16},{1,17},{2,18},{3,19},{4,20},{5,21},{6,22},{7,23},{8,24},{9,... | collective-permute-start | bytes 1572872 | tf_op jit(solution)/shard_map/ppermute | solution.py:14
  6.7 25.5 %collective-permute-start.2 = (bf16[128,2048]{1,0:T(8,128)(2,1)S(1)}, bf16[128,2048]{1,0:T(8,128)(2,1)S(1)}, u32[]{:S(2)}, u32[]{:S(2)}) collective-permute-start(bf16[128,2048]{1,0:T(8,128)(2,1)S(1)} %get-tuple-element.75), channel_id=1, source_target_pairs={{0,24},{1,25},{2,26},{3,27},{4,28},{5,29},{6,30},{7,31},{8,16},{9,... | collective-permute-start | bytes 1572872 | tf_op jit(solution)/shard_map/ppermute | solution.py:14
  7.2 6.1 %copy-start.5 = (s32[2]{0:T(128)S(1)}, s32[2]{0:T(128)}, u32[]{:S(2)}) copy-start(s32[2]{0:T(128)} %param.5) | copy-start | bytes 28
  32.5 3.4 %collective-permute-start.3 = (bf16[2,2,4,8,2048]{4,3,2,1,0:T(8,128)(2,1)S(1)}, bf16[2,2,4,8,2048]{4,3,2,1,0:T(8,128)(2,1)S(1)}, u32[]{:S(2)}, u32[]{:S(2)}) collective-permute-start(bf16[2,2,4,8,2048]{4,3,2,1,0:T(8,128)(2,1)S(1)} %pad_maximum_fusion.4), channel_id=1, source_target_pairs={{0,1},{1,0},{2,3},{3,2},{4,5},{5,4},{6,7},{7,6},{8,9},{9,8},{10,11... | collective-permute-start | bytes 1572872 | tf_op jit(solution)/shard_map/ppermute | solution.py:14
  36.7 8.8 %collective-permute-start.5 = (f32[3,2176]{1,0:T(4,128)S(1)}, f32[3,2176]{1,0:T(4,128)S(1)}, u32[]{:S(2)}, u32[]{:S(2)}) collective-permute-start(f32[3,2176]{1,0:T(4,128)S(1)} %maximum_maximum_fusion), channel_id=1, source_target_pairs={{0,64},{32,96},{64,0},{96,32},{128,192},{160,224},{192,128},{224,1... | collective-permute-start | bytes 78344 | tf_op jit(solution)/shard_map/ppermute | solution.py:14
  38.4 7.7 %collective-permute-start.6 = (f32[3,2176]{1,0:T(4,128)S(1)}, f32[3,2176]{1,0:T(4,128)S(1)}, u32[]{:S(2)}, u32[]{:S(2)}) collective-permute-start(f32[3,2176]{1,0:T(4,128)S(1)} %maximum_maximum_fusion), channel_id=1, source_target_pairs={{0,128},{32,160},{64,192},{96,224},{128,0},{160,32},{192,64},{224,... | collective-permute-start | bytes 78344 | tf_op jit(solution)/shard_map/ppermute | solution.py:14
  41.3 5.1 %collective-permute-start.7 = (f32[3,2176]{1,0:T(4,128)S(1)}, f32[3,2176]{1,0:T(4,128)S(1)}, u32[]{:S(2)}, u32[]{:S(2)}) collective-permute-start(f32[3,2176]{1,0:T(4,128)S(1)} %maximum_maximum_fusion), channel_id=1, source_target_pairs={{0,192},{32,224},{64,128},{96,160},{128,64},{160,96},{192,0},{224,... | collective-permute-start | bytes 78344 | tf_op jit(solution)/shard_map/ppermute | solution.py:14
  41.6 5.2 %collective-permute-start.4 = (bf16[2,2,8,2048]{3,2,1,0:T(8,128)(2,1)S(1)}, bf16[2,2,8,2048]{3,2,1,0:T(8,128)(2,1)S(1)}, u32[]{:S(2)}, u32[]{:S(2)}) collective-permute-start(bf16[2,2,8,2048]{3,2,1,0:T(8,128)(2,1)S(1)} %get-tuple-element.91), channel_id=1, source_target_pairs={{0,2},{1,3},{2,0},{3,1},{4,6},{5,7},{6,4},{7,5},{8,10},{9,11},{10,... | collective-permute-start | bytes 393224 | tf_op jit(solution)/shard_map/ppermute | solution.py:14
  41.7 14.4 %collective-permute-start.10 = (bf16[2,2,8,2048]{3,2,1,0:T(8,128)(2,1)S(1)}, bf16[2,2,8,2048]{3,2,1,0:T(8,128)(2,1)S(1)}, u32[]{:S(2)}, u32[]{:S(2)}) collective-permute-start(bf16[2,2,8,2048]{3,2,1,0:T(8,128)(2,1)S(1)} %get-tuple-element.93), channel_id=1, source_target_pairs={{0,6},{1,7},{2,4},{3,5},{4,2},{5,3},{6,0},{7,1},{8,14},{9,15},{10,... | collective-permute-start | bytes 393224 | tf_op jit(solution)/shard_map/ppermute | solution.py:14
  45.5 12.3 %collective-permute-start.9 = (bf16[2,2,8,2048]{3,2,1,0:T(8,128)(2,1)S(1)}, bf16[2,2,8,2048]{3,2,1,0:T(8,128)(2,1)S(1)}, u32[]{:S(2)}, u32[]{:S(2)}) collective-permute-start(bf16[2,2,8,2048]{3,2,1,0:T(8,128)(2,1)S(1)} %get-tuple-element.92), channel_id=1, source_target_pairs={{0,4},{1,5},{2,6},{3,7},{4,0},{5,1},{6,2},{7,3},{8,12},{9,13},{10,... | collective-permute-start | bytes 393224 | tf_op jit(solution)/shard_map/ppermute | solution.py:14
  46.7 15.1 %collective-permute-start.8 = (f32[3,2176]{1,0:T(4,128)S(1)}, f32[3,2176]{1,0:T(4,128)S(1)}, u32[]{:S(2)}, u32[]{:S(2)}) collective-permute-start(f32[3,2176]{1,0:T(4,128)S(1)} %pad_maximum_fusion.6), channel_id=1, source_target_pairs={{0,32},{32,0},{64,96},{96,64},{128,160},{160,128},{192,224},{224,1... | collective-permute-start | bytes 78344 | tf_op jit(solution)/shard_map/ppermute | solution.py:14
  57.8 6.2 %collective-permute-start.11 = (bf16[2,2,8,2048]{3,2,1,0:T(8,128)(2,1)S(1)}, bf16[2,2,8,2048]{3,2,1,0:T(8,128)(2,1)S(1)}, u32[]{:S(2)}, u32[]{:S(2)}) collective-permute-start(bf16[2,2,8,2048]{3,2,1,0:T(8,128)(2,1)S(1)} %pad_maximum_fusion.5), channel_id=1, source_target_pairs={{0,2},{1,3},{2,0},{3,1},{4,6},{5,7},{6,4},{7,5},{8,10},{9,11},{10,... | collective-permute-start | bytes 393224 | tf_op jit(solution)/shard_map/ppermute | solution.py:14
  60.1 10.8 %collective-permute-start.12 = (bf16[2,2,8,2048]{3,2,1,0:T(8,128)(2,1)S(1)}, bf16[2,2,8,2048]{3,2,1,0:T(8,128)(2,1)S(1)}, u32[]{:S(2)}, u32[]{:S(2)}) collective-permute-start(bf16[2,2,8,2048]{3,2,1,0:T(8,128)(2,1)S(1)} %pad_maximum_fusion.5), channel_id=1, source_target_pairs={{0,4},{1,5},{2,6},{3,7},{4,0},{5,1},{6,2},{7,3},{8,12},{9,13},{10,... | collective-permute-start | bytes 393224 | tf_op jit(solution)/shard_map/ppermute | solution.py:14
  61.5 12.4 %collective-permute-start.13 = (bf16[2,2,8,2048]{3,2,1,0:T(8,128)(2,1)S(1)}, bf16[2,2,8,2048]{3,2,1,0:T(8,128)(2,1)S(1)}, u32[]{:S(2)}, u32[]{:S(2)}) collective-permute-start(bf16[2,2,8,2048]{3,2,1,0:T(8,128)(2,1)S(1)} %pad_maximum_fusion.5), channel_id=1, source_target_pairs={{0,6},{1,7},{2,4},{3,5},{4,2},{5,3},{6,0},{7,1},{8,14},{9,15},{10,... | collective-permute-start | bytes 393224 | tf_op jit(solution)/shard_map/ppermute | solution.py:14
  64.0 10.0 %collective-permute-start.14 = (f32[2,2,2,4,8]{4,3,2,1,0:T(4,128)S(1)}, f32[2,2,2,4,8]{4,3,2,1,0:T(4,128)S(1)}, u32[]{:S(2)}, u32[]{:S(2)}) collective-permute-start(f32[2,2,2,4,8]{4,3,2,1,0:T(4,128)S(1)} %pad_maximum_fusion.8), channel_id=1, source_target_pairs={{0,2},{1,3},{2,0},{3,1},{4,6},{5,7},{6,4},{7,5},{8,10},{9,11},{10,... | collective-permute-start | bytes 3080 | tf_op jit(solution)/shard_map/ppermute | solution.py:14
  66.5 7.5 %collective-permute-start.15 = (f32[2,2,2,4,8]{4,3,2,1,0:T(4,128)S(1)}, f32[2,2,2,4,8]{4,3,2,1,0:T(4,128)S(1)}, u32[]{:S(2)}, u32[]{:S(2)}) collective-permute-start(f32[2,2,2,4,8]{4,3,2,1,0:T(4,128)S(1)} %pad_maximum_fusion.8), channel_id=1, source_target_pairs={{0,4},{1,5},{2,6},{3,7},{4,0},{5,1},{6,2},{7,3},{8,12},{9,13},{10,... | collective-permute-start | bytes 3080 | tf_op jit(solution)/shard_map/ppermute | solution.py:14
  67.7 6.6 %collective-permute-start.16 = (f32[2,2,2,4,8]{4,3,2,1,0:T(4,128)S(1)}, f32[2,2,2,4,8]{4,3,2,1,0:T(4,128)S(1)}, u32[]{:S(2)}, u32[]{:S(2)}) collective-permute-start(f32[2,2,2,4,8]{4,3,2,1,0:T(4,128)S(1)} %pad_maximum_fusion.8), channel_id=1, source_target_pairs={{0,6},{1,7},{2,4},{3,5},{4,2},{5,3},{6,0},{7,1},{8,14},{9,15},{10,... | collective-permute-start | bytes 3080 | tf_op jit(solution)/shard_map/ppermute | solution.py:14
  76.5 12.9 %collective-permute-start.17 = (bf16[9,8,2048]{2,1,0:T(8,128)(2,1)S(1)}, bf16[9,8,2048]{2,1,0:T(8,128)(2,1)S(1)}, u32[]{:S(2)}, u32[]{:S(2)}) collective-permute-start(bf16[9,8,2048]{2,1,0:T(8,128)(2,1)S(1)} %concatenate.15), channel_id=1, source_target_pairs={{0,8},{1,9},{2,10},{3,11},{4,12},{5,13},{6,14},{7,15},{8,0},{9,1},... | collective-permute-start | bytes 884744 | tf_op jit(solution)/shard_map/ppermute | solution.py:14
  76.6 13.8 %collective-permute-start.18 = (bf16[9,8,2048]{2,1,0:T(8,128)(2,1)S(1)}, bf16[9,8,2048]{2,1,0:T(8,128)(2,1)S(1)}, u32[]{:S(2)}, u32[]{:S(2)}) collective-permute-start(bf16[9,8,2048]{2,1,0:T(8,128)(2,1)S(1)} %concatenate.15), channel_id=1, source_target_pairs={{0,16},{1,17},{2,18},{3,19},{4,20},{5,21},{6,22},{7,23},{8,24},{9,... | collective-permute-start | bytes 884744 | tf_op jit(solution)/shard_map/ppermute | solution.py:14
  78.5 14.4 %collective-permute-start.19 = (bf16[9,8,2048]{2,1,0:T(8,128)(2,1)S(1)}, bf16[9,8,2048]{2,1,0:T(8,128)(2,1)S(1)}, u32[]{:S(2)}, u32[]{:S(2)}) collective-permute-start(bf16[9,8,2048]{2,1,0:T(8,128)(2,1)S(1)} %concatenate.15), channel_id=1, source_target_pairs={{0,24},{1,25},{2,26},{3,27},{4,28},{5,29},{6,30},{7,31},{8,16},{9,... | collective-permute-start | bytes 884744 | tf_op jit(solution)/shard_map/ppermute | solution.py:14
  93.1 8.0 %collective-permute-start.20 = (bf16[4,9,8,2048]{3,2,1,0:T(8,128)(2,1)S(1)}, bf16[4,9,8,2048]{3,2,1,0:T(8,128)(2,1)S(1)}, u32[]{:S(2)}, u32[]{:S(2)}) collective-permute-start(bf16[4,9,8,2048]{3,2,1,0:T(8,128)(2,1)S(1)} %get-tuple-element.80), channel_id=1, source_target_pairs={{0,1},{1,0},{2,3},{3,2},{4,5},{5,4},{6,7},{7,6},{8,9},{9,8},{10,11... | collective-permute-start | bytes 3538952 | tf_op jit(solution)/shard_map/ppermute | solution.py:14
  96.4 15.7 %collective-permute-start.24 = (bf16[8,8,2048]{2,1,0:T(8,128)(2,1)}, bf16[8,8,2048]{2,1,0:T(8,128)(2,1)}, u32[]{:S(2)}, u32[]{:S(2)}) collective-permute-start(bf16[8,8,2048]{2,1,0:T(8,128)(2,1)} %bitcast.47), channel_id=1, source_target_pairs={{0,8},{1,9},{2,10},{3,11},{4,12},{5,13},{6,14},{7,15},{8,0},{9,1},... | collective-permute-start | bytes 786440 | tf_op jit(solution)/shard_map/ppermute | solution.py:14
  96.4 16.9 %collective-permute-start.25 = (bf16[8,8,2048]{2,1,0:T(8,128)(2,1)}, bf16[8,8,2048]{2,1,0:T(8,128)(2,1)}, u32[]{:S(2)}, u32[]{:S(2)}) collective-permute-start(bf16[8,8,2048]{2,1,0:T(8,128)(2,1)} %bitcast.47), channel_id=1, source_target_pairs={{0,16},{1,17},{2,18},{3,19},{4,20},{5,21},{6,22},{7,23},{8,24},{9,... | collective-permute-start | bytes 786440 | tf_op jit(solution)/shard_map/ppermute | solution.py:14
  100.6 15.2 %collective-permute-start.26 = (bf16[8,8,2048]{2,1,0:T(8,128)(2,1)}, bf16[8,8,2048]{2,1,0:T(8,128)(2,1)}, u32[]{:S(2)}, u32[]{:S(2)}) collective-permute-start(bf16[8,8,2048]{2,1,0:T(8,128)(2,1)} %bitcast.47), channel_id=1, source_target_pairs={{0,24},{1,25},{2,26},{3,27},{4,28},{5,29},{6,30},{7,31},{8,16},{9,... | collective-permute-start | bytes 786440 | tf_op jit(solution)/shard_map/ppermute | solution.py:14
  109.9 2.2 %copy-start.1 = (f32[2,2,2,9,8,2048]{5,4,3,2,1,0:T(8,128)}, f32[2,2,2,9,8,2048]{5,4,3,2,1,0:T(8,128)S(1)}, u32[]{:S(2)}) copy-start(f32[2,2,2,9,8,2048]{5,4,3,2,1,0:T(8,128)S(1)} %fusion.4) | copy-start | bytes 14155780
  117.1 4.4 %collective-permute-start.27 = (bf16[4,8,8,2048]{3,2,1,0:T(8,128)(2,1)S(1)}, bf16[4,8,8,2048]{3,2,1,0:T(8,128)(2,1)}, u32[]{:S(2)}, u32[]{:S(2)}) collective-permute-start(bf16[4,8,8,2048]{3,2,1,0:T(8,128)(2,1)S(1)} %pad_maximum_fusion.1), channel_id=1, source_target_pairs={{0,1},{1,0},{2,3},{3,2},{4,5},{5,4},{6,7},{7,6},{8,9},{9,8},{10,11... | collective-permute-start | bytes 3145736 | tf_op jit(solution)/shard_map/ppermute | solution.py:14
  117.3 16.4 %collective-permute-start.22 = (f16[2,2,4,8,2048]{4,3,2,0,1:T(8,128)(2,1)S(1)}, f16[2,2,4,8,2048]{4,3,2,0,1:T(8,128)(2,1)S(1)}, u32[]{:S(2)}, u32[]{:S(2)}) collective-permute-start(f16[2,2,4,8,2048]{4,3,2,0,1:T(8,128)(2,1)S(1)} %fusion.25), channel_id=1, source_target_pairs={{0,128},{32,160},{64,192},{96,224},{128,0},{160,32},{192,64},{224,... | collective-permute-start | bytes 1572872 | tf_op jit(solution)/shard_map/ppermute | solution.py:14
  119.3 25.3 %collective-permute-start.21 = (f16[2,2,4,8,2048]{4,3,2,0,1:T(8,128)(2,1)S(1)}, f16[2,2,4,8,2048]{4,3,2,0,1:T(8,128)(2,1)S(1)}, u32[]{:S(2)}, u32[]{:S(2)}) collective-permute-start(f16[2,2,4,8,2048]{4,3,2,0,1:T(8,128)(2,1)S(1)} %fusion.24), channel_id=1, source_target_pairs={{0,64},{32,96},{64,0},{96,32},{128,192},{160,224},{192,128},{224,1... | collective-permute-start | bytes 1572872 | tf_op jit(solution)/shard_map/ppermute | solution.py:14
  121.2 23.4 %collective-permute-start.23 = (f16[2,2,4,8,2048]{4,3,2,1,0:T(8,128)(2,1)S(1)}, f16[2,2,4,8,2048]{4,3,2,1,0:T(8,128)(2,1)S(1)}, u32[]{:S(2)}, u32[]{:S(2)}) collective-permute-start(f16[2,2,4,8,2048]{4,3,2,1,0:T(8,128)(2,1)S(1)} %get-tuple-element.67), channel_id=1, source_target_pairs={{0,192},{32,224},{64,128},{96,160},{128,64},{160,96},{192,0},{224,... | collective-permute-start | bytes 1572872 | tf_op jit(solution)/shard_map/ppermute | solution.py:14
  128.8 1.9 copy-start
  133.7 21.3 %copy-start.2 = (f16[2,2,4,8,2048]{4,3,2,0,1:T(8,128)(2,1)}, f16[2,2,4,8,2048]{4,3,2,0,1:T(8,128)(2,1)S(1)}, u32[]{:S(2)}) copy-start(f16[2,2,4,8,2048]{4,3,2,0,1:T(8,128)(2,1)S(1)} %collective-permute-done.22) | copy-start | bytes 1572868
  144.6 10.4 %copy-start.3 = (f16[2,2,4,8,2048]{4,3,2,0,1:T(8,128)(2,1)}, f16[2,2,4,8,2048]{4,3,2,0,1:T(8,128)(2,1)S(1)}, u32[]{:S(2)}) copy-start(f16[2,2,4,8,2048]{4,3,2,0,1:T(8,128)(2,1)S(1)} %collective-permute-done.21) | copy-start | bytes 1572868
  144.6 10.4 %copy-start.4 = (f16[2,2,4,8,2048]{4,3,2,1,0:T(8,128)(2,1)}, f16[2,2,4,8,2048]{4,3,2,1,0:T(8,128)(2,1)S(1)}, u32[]{:S(2)}) copy-start(f16[2,2,4,8,2048]{4,3,2,1,0:T(8,128)(2,1)S(1)} %collective-permute-done.23) | copy-start | bytes 1572868
  146.3 16.9 %collective-permute-start.28 = (f16[2,4,8,2048]{3,2,1,0:T(8,128)(2,1)S(1)}, f16[2,4,8,2048]{3,2,1,0:T(8,128)(2,1)}, u32[]{:S(2)}, u32[]{:S(2)}) collective-permute-start(f16[2,4,8,2048]{3,2,1,0:T(8,128)(2,1)S(1)} %fusion.35), channel_id=1, source_target_pairs={{0,32},{32,0},{64,96},{96,64},{128,160},{160,128},{192,224},{224,1... | collective-permute-start | bytes 786440 | tf_op jit(solution)/shard_map/ppermute | solution.py:14
  151.1 14.9 %collective-permute-start.29 = (f16[2,2,4,8,2048]{4,3,2,0,1:T(8,128)(2,1)S(1)}, f16[2,2,4,8,2048]{4,3,2,0,1:T(8,128)(2,1)S(1)}, u32[]{:S(2)}, u32[]{:S(2)}) collective-permute-start(f16[2,2,4,8,2048]{4,3,2,0,1:T(8,128)(2,1)S(1)} %fusion.26), channel_id=1, source_target_pairs={{0,64},{32,96},{64,0},{96,32},{128,192},{160,224},{192,128},{224,1... | collective-permute-start | bytes 1572872 | tf_op jit(solution)/shard_map/ppermute | solution.py:14
  151.2 26.6 %collective-permute-start.30 = (f16[2,2,4,8,2048]{4,3,2,0,1:T(8,128)(2,1)S(1)}, f16[2,2,4,8,2048]{4,3,2,0,1:T(8,128)(2,1)S(1)}, u32[]{:S(2)}, u32[]{:S(2)}) collective-permute-start(f16[2,2,4,8,2048]{4,3,2,0,1:T(8,128)(2,1)S(1)} %fusion.27), channel_id=1, source_target_pairs={{0,128},{32,160},{64,192},{96,224},{128,0},{160,32},{192,64},{224,... | collective-permute-start | bytes 1572872 | tf_op jit(solution)/shard_map/ppermute | solution.py:14
  155.0 25.5 %collective-permute-start.31 = (f16[2,2,4,8,2048]{4,3,2,0,1:T(8,128)(2,1)S(1)}, f16[2,2,4,8,2048]{4,3,2,0,1:T(8,128)(2,1)S(1)}, u32[]{:S(2)}, u32[]{:S(2)}) collective-permute-start(f16[2,2,4,8,2048]{4,3,2,0,1:T(8,128)(2,1)S(1)} %fusion.28), channel_id=1, source_target_pairs={{0,192},{32,224},{64,128},{96,160},{128,64},{160,96},{192,0},{224,... | collective-permute-start | bytes 1572872 | tf_op jit(solution)/shard_map/ppermute | solution.py:14
  181.9 15.4 %collective-permute-start.32 = (f16[2,4,8,2048]{3,2,1,0:T(8,128)(2,1)S(1)}, f16[2,4,8,2048]{3,2,1,0:T(8,128)(2,1)S(1)}, u32[]{:S(2)}, u32[]{:S(2)}) collective-permute-start(f16[2,4,8,2048]{3,2,1,0:T(8,128)(2,1)S(1)} %fusion.31), channel_id=1, source_target_pairs={{0,32},{32,0},{64,96},{96,64},{128,160},{160,128},{192,224},{224,1... | collective-permute-start | bytes 786440 | tf_op jit(solution)/shard_map/ppermute | solution.py:14

commit v3 on v2

v3 whole, which is shorter than its diff:
```python
import jax
import jax.numpy as jnp
from jax import lax
from jax.sharding import PartitionSpec as P

F32 = jnp.float32
BF16 = jnp.bfloat16
WIRE = jnp.float16


def swap(value, axis, bits):
    size = lax.axis_size(axis)
    return lax.ppermute(value, axis, [(i, i ^ bits) for i in range(size)])


def pick(index, options):
    result = options[-1]
    for i in range(len(options) - 2, -1, -1):
        result = jnp.where(index == i, options[i], result)
    return result


def row_stats(rows):
    wide = rows.astype(F32)
    return jnp.stack([jnp.sum(wide, -1), jnp.max(wide, -1), jnp.max(-wide, -1)])


def merge(parts):
    total = parts[0]
    for part in parts[1:]:
        total = jnp.concatenate([total[:1] + part[:1], jnp.maximum(total[1:], part[1:])])
    return total


def after(value, others):
    token, others = lax.optimization_barrier((lax.create_token(), others))
    return lax.optimization_barrier((token, value))[1], others


def per_device(first_plane, second_plane, panel_owner):
    samples, shard = first_plane.shape
    members = shard * lax.axis_size("mem")
    samp, mem = lax.axis_index("samp"), lax.axis_index("mem")
    my_x, my_z, my_core = samp >> 3, (samp >> 1) & 3, samp & 1
    my_y, my_zh = mem >> 1, mem & 1
    own_x, own_z, own_core = panel_owner >> 3, (panel_owner >> 1) & 3, panel_owner & 1

    by_x = second_plane.reshape(4, 128, shard)
    piece = lambda bits: lax.dynamic_index_in_dim(by_x, my_x ^ bits, 0, keepdims=False)
    from_x = [piece(0)] + [swap(piece(bits), "samp", 8 * bits) for bits in (1, 2, 3)]
    first_plane, from_x[0] = after(first_plane, from_x[0])
    first_local = row_stats(first_plane)
    from_x, first_local = after(from_x, first_local)
    halves = [
        pick(my_x ^ own_x[p], from_x).reshape(2, 4, 2, 8, shard) for p in range(2)
    ]
    half = lambda core: jnp.stack(
        [lax.dynamic_index_in_dim(h, core, 0, keepdims=False) for h in halves]
    )
    kept, got = half(my_core), swap(half(1 - my_core), "samp", 1)
    column = jnp.stack(
        [jnp.where(my_core == own_core[p], kept[p], got[p]) for p in range(2)]
    )
    piece_z = lambda bits: lax.dynamic_index_in_dim(column, my_z ^ bits, 1, keepdims=False)
    from_z = [piece_z(0)] + [swap(piece_z(bits), "samp", 2 * bits) for bits in (1, 2, 3)]

    column_local = row_stats(column).reshape(3, -1)
    stats = jnp.concatenate([first_local, column_local], axis=1)
    stats = merge([stats] + [swap(stats, "mem", bits) for bits in (2, 4, 6)])
    stats, from_z[1] = after(stats, from_z[1])
    stats = merge([stats, swap(stats, "mem", 1)])
    mean, span = stats[0] / members, stats[1] + stats[2]
    first_mean = mean[:samples]
    facts = jnp.stack([mean[samples:], span[samples:]]).reshape((2,) + column.shape[:-1])

    mine = jnp.stack([pick(my_z ^ own_z[p], [f[p] for f in from_z]) for p in range(2)])
    parts = [mine] + [swap(mine, "samp", 2 * bits) for bits in (1, 2, 3)]
    facts, parts[1] = after(facts, parts[1])
    facts_z = [facts] + [swap(facts, "samp", 2 * bits) for bits in (1, 2, 3)]
    facts = jnp.stack([pick(my_z ^ own_z[p], [f[:, p] for f in facts_z]) for p in range(2)], 1)
    line = jnp.stack([pick(my_z ^ place, parts) for place in range(4)], 1)
    line = (line.astype(F32) - facts[0][..., None]).astype(BF16)
    tiles = 16
    bound = jnp.max(facts[1]) * 1.02
    mark = jnp.broadcast_to(bound, (1, 8, shard)).astype(BF16)
    sent = jnp.concatenate([line.reshape(tiles, 8, shard), mark])
    near = jnp.stack([sent] + [swap(sent, "samp", 8 * bits) for bits in (1, 2, 3)])
    far = swap(near, "samp", 1)

    first_anom = (first_plane.astype(F32) - first_mean[:, None]).astype(BF16)
    shrink_first = 4.0 / jnp.maximum(jnp.max(span[:samples]), 1e-30)
    grow_first = 1.0 / shrink_first
    results = []
    for anom in (near, far):
        shrink_panel = 1.0 / jnp.maximum(jnp.max(anom[:, tiles, 0, :128].astype(F32)), 1e-30)
        grow_panel = 1.0 / shrink_panel
        shares = lax.dot_general(
            anom.reshape(-1, shard),
            first_anom,
            (((1,), (1,)), ((), ())),
            preferred_element_type=F32,
        ).reshape(2, 2, tiles + 1, 8, samples)

        def for_y(dest):
            start = ((dest & 1) ^ (my_x >> 1), 0, 8 * (dest >> 1), 0, 0)
            block = lax.dynamic_slice(shares, start, (1, 2, 8, 8, samples))
            return block.reshape(2, 8, 8, samples)

        blocks = [for_y(my_y)]
        for bits in (1, 2, 3):
            sent = (for_y(my_y ^ bits) * shrink_first * shrink_panel).astype(WIRE)
            blocks.append(swap(sent, "mem", 2 * bits))

        def for_z(dest):
            part = lambda v: lax.dynamic_index_in_dim(v, dest ^ (my_x & 1), 0, keepdims=False)
            total = part(blocks[0])
            for value in blocks[1:]:
                total += part(value).astype(F32) * grow_panel * grow_first
            return total

        other = (for_z(1 - my_zh) * shrink_first * shrink_panel).astype(WIRE)
        total = for_z(my_zh) + swap(other, "mem", 1).astype(F32) * grow_panel * grow_first
        results.append(total / (members - 1))
    return jnp.stack([pick(my_core ^ core, results) for core in range(2)]).reshape(-1, samples)


def solution(mesh):
    in_specs = (P("samp", "mem"), P("samp", "mem"), P())
    out_specs = P("mem", "samp")
    return jax.shard_map(
        per_device, mesh=mesh, in_specs=in_specs, out_specs=out_specs, check_vma=False
    )
```

time: 200 us -> 183 us (0.915)
  waiting for transfers between devices: 82.5 us -> 72.8 us
  local copies, waits for them, and re-layouts: 10.2 us -> 4.39 us
  other arithmetic: 31.3 us -> 26.8 us
  matrix products: 14.7 us -> 18.4 us
    ppermute x33 -> x29, waiting for transfers between devices: 82.5 us -> 72.8 us  [swap(): return lax.ppermute(value, axis, [(i, i ^ bits) for i in range(size)])]
    convert_element_type x7 -> x2, other arithmetic: 8.94 us -> 5.11 us  [per_device(): sent = (for_y(my_y ^ bits) * shrink_first * shrink_panel).astype(WIRE)]
    dot_general x2, matrix products: 14.7 us -> 18.4 us  [per_device(): lax.dot_general(anom.reshape(-1, shard), first_anom, (((1,), (1,)), ((),...]
    unnamed x12 -> x4, local copies, waits for them, and re-layouts: 3.14 us -> 0.01 us
    add x2 -> x0, other arithmetic: 2.95 us -> none  [per_device(): for_z(my_zh) + swap(other, 'mem', 1).astype(F32) * grow_panel * grow_first]
    slice x3 -> x0, local copies, waits for them, and re-layouts: 2.43 us -> none  [per_device(): sent = line[:, chunk].reshape(tiles, eighth, shard)]
    ppermute x33 -> x29, starting transfers between devices: 54.5 us -> 53.8 us  [swap(): return lax.ppermute(value, axis, [(i, i ^ bits) for i in range(size)])]
  transfers between devices with their start and end apart: 33 -> 29, of which waited for: 21 -> 17; matrix products, arithmetic and copies ran while one was open for 21% -> 23% of each run, Pallas kernels for 0% -> 0%
where the time goes in v3:
time: 183 us
  waiting for transfers between devices  72.8 us (40%)
  starting transfers between devices  53.8 us (29%)
  other arithmetic  26.8 us (15%)
  matrix products  18.4 us (10%)
  between operations  6.82 us (4%)
  local copies, waits for them, and re-layouts  4.39 us (2%)
    ppermute x29, waiting for transfers between devices, swap(): return lax.ppermute(value, axis, [(i, i ^ bits) for i in range(size)])  72.8 us
    ppermute x29, starting transfers between devices, swap(): return lax.ppermute(value, axis, [(i, i ^ bits) for i in range(size)])  53.8 us
    dot_general x2, matrix products, per_device(): lax.dot_general(anom.reshape(-1, shard), first_anom, (((1,), (1,)), ((),...  18.4 us
    reduce_sum x2, other arithmetic, row_stats(): return jnp.stack([jnp.sum(wide, -1), jnp.max(wide, -1), jnp.max(-wide, -1)])  6.27 us
    convert_element_type x2, other arithmetic, per_device(): sent = (for_y(my_y ^ bits) * shrink_first * shrink_panel).astype(WIRE)  5.11 us
    reduce_max x3, other arithmetic, row_stats(): return jnp.stack([jnp.sum(wide, -1), jnp.max(wide, -1), jnp.max(-wide, -1)])  4.75 us
  transfers between devices with their start and end apart: 29, of which 17 were waited for; matrix products, arithmetic and copies ran while one was open for 23% of the time, Pallas kernels for 0%

profile of v3, /device:TPU:32, one launch (start us, length us, event | category | flops | bytes accessed | tf_op | source)
XLA Modules:
  0.0 183.0 jit_solution(16417936932079660680)
XLA Ops:
  0.0 2.5 %dynamic-slice_bitcast_fusion = (bf16[128,2048]{1,0:T(8,128)(2,1)}, bf16[128,2048]{1,0:T(8,128)(2,1)S(1)}, bf16[128,2048]{1,0:T(8,128)(2,1)S(1)}, bf16[128,2048]{1,0:T(8,128)(2,1)S(1)}) fusion(bf16[4,128,2048]{2,1,0:T(8,128)(2,1)} %bitcast.166, s32[]{:T(128)S(6)} %select_n.335, s32[]{:T(128)S(6)} %select_n.334, s32[]{:T(128)S(6)} %select_n.333, s32[]{:T(128)S(6)} %select_n.332), kind=kLoop, calls=%fused_computation.64 | loop fusion | bytes 4194320 | tf_op jit(solution)/shard_map/jit(dynamic_index_in_dim)/squeeze | solution.py:49
  2.5 2.8 %collective-permute-start.2 = (bf16[128,2048]{1,0:T(8,128)(2,1)}, bf16[128,2048]{1,0:T(8,128)(2,1)S(1)}, u32[]{:S(2)}, u32[]{:S(2)}) collective-permute-start(bf16[128,2048]{1,0:T(8,128)(2,1)} %get-tuple-element.50), channel_id=1, source_target_pairs={{0,24},{1,25},{2,26},{3,27},{4,28},{5,29},{6,30},{7,31},{8,16},{9,... | collective-permute-start | bytes 1572872 | tf_op jit(solution)/shard_map/ppermute | solution.py:13
  5.2 0.8 collective-permute-start.1
  6.0 0.5 collective-permute-start
  6.6 6.0 %convert_reduce_fusion = (f32[2048]{0:T(1024)S(1)}, f32[2048]{0:T(1024)S(1)}) fusion(bf16[2048,2048]{1,0:T(8,128)(2,1)} %param.3), kind=kLoop, calls=%fused_computation.2 | loop fusion | flops 16773120 | bytes 8404992 | tf_op jit(solution)/shard_map/reduce_sum | solution.py:25
  12.6 0.6 fusion.48
  14.5 4.6 %reduce_max.96 = bf16[2048]{0:T(1024)(128)(2,1)S(1)} reduce(bf16[2048,2048]{1,0:T(8,128)(2,1)} %param.3, bf16[]{:T(256)} %constant.203.clone.1), dimensions={1}, to_apply=%region_1.2 | reduce | flops 4192256 | bytes 8392706 | tf_op jit(solution)/shard_map/reduce_max | solution.py:25
  19.1 9.7 %collective-permute-done.2 = bf16[128,2048]{1,0:T(8,128)(2,1)S(1)} collective-permute-done((bf16[128,2048]{1,0:T(8,128)(2,1)}, bf16[128,2048]{1,0:T(8,128)(2,1)S(1)}, u32[]{:S(2)}, u32[]{:S(2)}) %collective-permute-start.2) | collective-permute-done | bytes 524320 | tf_op jit(solution)/shard_map/ppermute | solution.py:13
  28.8 0.4 collective-permute-done
  29.2 0.1 select_select_fusion.1
  29.6 0.7 fusion.46
  32.8 0.2 fusion.25
  33.0 0.2 convert_reduce_fusion.1
  33.3 0.1 stack.95
  33.5 3.1 %collective-permute-start.12 = (f32[3,2176]{1,0:T(4,128)S(1)}, f32[3,2176]{1,0:T(4,128)S(1)}, u32[]{:S(2)}, u32[]{:S(2)}) collective-permute-start(f32[3,2176]{1,0:T(4,128)S(1)} %maximum_maximum_fusion), channel_id=1, source_target_pairs={{0,192},{32,224},{64,128},{96,160},{128,64},{160,96},{192,0},{224,... | collective-permute-start | bytes 78344 | tf_op jit(solution)/shard_map/ppermute | solution.py:13
  36.6 0.6 collective-permute-start.11
  37.3 0.5 collective-permute-start.10
  37.9 3.4 %collective-permute-start.5 = (bf16[2,2,8,2048]{3,2,1,0:T(8,128)(2,1)S(1)}, bf16[2,2,8,2048]{3,2,1,0:T(8,128)(2,1)S(1)}, u32[]{:S(2)}, u32[]{:S(2)}) collective-permute-start(bf16[2,2,8,2048]{3,2,1,0:T(8,128)(2,1)S(1)} %get-tuple-element.63), channel_id=1, source_target_pairs={{0,4},{1,5},{2,6},{3,7},{4,0},{5,1},{6,2},{7,3},{8,12},{9,13},{10,... | collective-permute-start | bytes 393224 | tf_op jit(solution)/shard_map/ppermute | solution.py:13
  41.2 0.5 collective-permute-start.6
  41.7 0.4 collective-permute-done.11
  42.2 0.8 collective-permute-done.4
  43.0 7.5 %collective-permute-start.13 = (f32[3,2176]{1,0:T(4,128)S(1)}, f32[3,2176]{1,0:T(4,128)S(1)}, u32[]{:S(2)}, u32[]{:S(2)}) collective-permute-start(f32[3,2176]{1,0:T(4,128)S(1)} %pad_maximum_fusion.6), channel_id=1, source_target_pairs={{0,32},{32,0},{64,96},{96,64},{128,160},{160,128},{192,224},{224,1... | collective-permute-start | bytes 78344 | tf_op jit(solution)/shard_map/ppermute | solution.py:13
  50.6 0.8 collective-permute-done.5
  51.4 4.9 %collective-permute-done.6 = bf16[2,2,8,2048]{3,2,1,0:T(8,128)(2,1)S(1)} collective-permute-done((bf16[2,2,8,2048]{3,2,1,0:T(8,128)(2,1)S(1)}, bf16[2,2,8,2048]{3,2,1,0:T(8,128)(2,1)S(1)}, u32[]{:S(2)}, u32[]{:S(2)}) %collective-permute-start.6) | collective-permute-done | bytes 131104 | tf_op jit(solution)/shard_map/ppermute | solution.py:13
  56.3 1.6 collective-permute-start.9
  57.9 1.9 %collective-permute-start.7 = (bf16[2,2,8,2048]{3,2,1,0:T(8,128)(2,1)S(1)}, bf16[2,2,8,2048]{3,2,1,0:T(8,128)(2,1)S(1)}, u32[]{:S(2)}, u32[]{:S(2)}) collective-permute-start(bf16[2,2,8,2048]{3,2,1,0:T(8,128)(2,1)S(1)} %pad_maximum_fusion.5), channel_id=1, source_target_pairs={{0,2},{1,3},{2,0},{3,1},{4,6},{5,7},{6,4},{7,5},{8,10},{9,11},{10,... | collective-permute-start | bytes 393224 | tf_op jit(solution)/shard_map/ppermute | solution.py:13
  60.2 4.4 %collective-permute-done.7 = bf16[2,2,8,2048]{3,2,1,0:T(8,128)(2,1)S(1)} collective-permute-done((bf16[2,2,8,2048]{3,2,1,0:T(8,128)(2,1)S(1)}, bf16[2,2,8,2048]{3,2,1,0:T(8,128)(2,1)S(1)}, u32[]{:S(2)}, u32[]{:S(2)}) %collective-permute-start.7) | collective-permute-done | bytes 131104 | tf_op jit(solution)/shard_map/ppermute | solution.py:13
  64.6 1.4 collective-permute-start.16
  66.0 1.4 collective-permute-start.15
  67.4 0.7 collective-permute-start.14
  68.3 2.3 %collective-permute-done.15 = f32[2,2,4,2,8]{4,3,2,1,0:T(2,128)S(1)} collective-permute-done((f32[2,2,4,2,8]{4,3,2,1,0:T(2,128)S(1)}, f32[2,2,4,2,8]{4,3,2,1,0:T(2,128)S(1)}, u32[]{:S(2)}, u32[]{:S(2)}) %collective-permute-start.15) | collective-permute-done | bytes 1056 | tf_op jit(solution)/shard_map/ppermute | solution.py:13
  70.6 0.5 collective-permute-done.14
  71.1 0.6 fusion.39
  72.4 0.2 fusion.8
  72.7 3.1 %collective-permute-start.18 = (bf16[17,8,2048]{2,1,0:T(8,128)(2,1)S(1)}, bf16[17,8,2048]{2,1,0:T(8,128)(2,1)S(1)}, u32[]{:S(2)}, u32[]{:S(2)}) collective-permute-start(bf16[17,8,2048]{2,1,0:T(8,128)(2,1)S(1)} %get-tuple-element.55), channel_id=1, source_target_pairs={{0,16},{1,17},{2,18},{3,19},{4,20},{5,21},{6,22},{7,23},{8,24},{9,... | collective-permute-start | bytes 1671176 | tf_op jit(solution)/shard_map/ppermute | solution.py:13
  75.8 0.6 collective-permute-start.17
  76.4 0.5 collective-permute-start.19
  76.9 12.9 %collective-permute-done.18 = bf16[17,8,2048]{2,1,0:T(8,128)(2,1)S(1)} collective-permute-done((bf16[17,8,2048]{2,1,0:T(8,128)(2,1)S(1)}, bf16[17,8,2048]{2,1,0:T(8,128)(2,1)S(1)}, u32[]{:S(2)}, u32[]{:S(2)}) %collective-permute-start.18) | collective-permute-done | bytes 557088 | tf_op jit(solution)/shard_map/ppermute | solution.py:13
  89.8 7.0 %collective-permute-done.17 = bf16[17,8,2048]{2,1,0:T(8,128)(2,1)S(1)} collective-permute-done((bf16[17,8,2048]{2,1,0:T(8,128)(2,1)S(1)}, bf16[17,8,2048]{2,1,0:T(8,128)(2,1)S(1)}, u32[]{:S(2)}, u32[]{:S(2)}) %collective-permute-start.17) | collective-permute-done | bytes 557088 | tf_op jit(solution)/shard_map/ppermute | solution.py:13
  96.8 0.3 pad_maximum_fusion
  97.3 0.6 slice_reduce_fusion
  98.6 0.6 slice_reduce_fusion.2
  99.9 7.4 %fusion.5 = f32[2,2,17,8,2048]{4,3,2,1,0:T(8,128)S(1)} fusion(bf16[2,2,17,8,2048]{4,3,2,1,0:T(8,128)(2,1)S(1)} %bitcast.161, bf16[2048,2048]{1,0:T(8,128)(2,1)} %param.3, f32[2048]{0:T(1024)S(1)} %bitcast.174), kind=kOutput, calls=%fused_computation.7 | convolution fusion | flops 4575985664 | bytes 15081472 | tf_op jit(solution)/shard_map/dot_general | solution.py:97
  107.3 1.8 fusion.9
  109.1 1.3 collective-permute-start.20
  110.3 2.2 %collective-permute-start.22 = (f16[2,8,8,2048]{3,2,1,0:T(8,128)(2,1)}, f16[2,8,8,2048]{3,2,1,0:T(8,128)(2,1)S(1)}, u32[]{:S(2)}, u32[]{:S(2)}) collective-permute-start(f16[2,8,8,2048]{3,2,1,0:T(8,128)(2,1)} %get-tuple-element.43), channel_id=1, source_target_pairs={{0,192},{32,224},{64,128},{96,160},{128,64},{160,96},{192,0},{224,... | collective-permute-start | bytes 1572872 | tf_op jit(solution)/shard_map/ppermute | solution.py:13
  112.5 0.7 collective-permute-start.21
  113.2 11.0 %fusion.3 = f32[2,2,17,8,2048]{4,3,2,1,0:T(8,128)} fusion(bf16[2,2,17,8,2048]{4,3,2,1,0:T(8,128)(2,1)} %bitcast.49, bf16[2048,2048]{1,0:T(8,128)(2,1)} %param.3, f32[2048]{0:T(1024)S(1)} %bitcast.175), kind=kOutput, calls=%fused_computation.6 | convolution fusion | flops 4575985664 | bytes 15081472 | tf_op jit(solution)/shard_map/dot_general | solution.py:97
  124.3 1.3 slice_reduce_fusion.1
  126.3 3.3 %fusion.12 = (f16[2,8,8,2048]{3,2,1,0:T(8,128)(2,1)}, f16[2,8,8,2048]{3,2,1,0:T(8,128)(2,1)}, f16[2,8,8,2048]{3,2,1,0:T(8,128)(2,1)S(1)}) fusion(f32[2,2,17,8,2048]{4,3,2,1,0:T(8,128)} %fusion.3, s32[]{:T(128)S(6)} %select_n.408, s32[]{:T(128)S(6)} %select_n.409, f32[]{:T(128)S(6)} %div.32, f32[]{:T(128)S(6)} %div.28, s32[]{:T(128)S(6)} %select_n.412, ...), kind=kLoop, calls=%fused_computation.33 | loop fusion | flops 2359296 | bytes 4718624 | tf_op jit(solution)/shard_map/convert_element_type | solution.py:111
  129.6 1.2 collective-permute-start.25
  130.8 2.2 %collective-permute-start.27 = (f16[2,8,8,2048]{3,2,1,0:T(8,128)(2,1)}, f16[2,8,8,2048]{3,2,1,0:T(8,128)(2,1)S(1)}, u32[]{:S(2)}, u32[]{:S(2)}) collective-permute-start(f16[2,8,8,2048]{3,2,1,0:T(8,128)(2,1)} %get-tuple-element.46), channel_id=1, source_target_pairs={{0,192},{32,224},{64,128},{96,160},{128,64},{160,96},{192,0},{224,... | collective-permute-start | bytes 1572872 | tf_op jit(solution)/shard_map/ppermute | solution.py:13
  133.0 0.7 collective-permute-start.26
  133.7 2.7 %collective-permute-done.22 = f16[2,8,8,2048]{3,2,1,0:T(8,128)(2,1)S(1)} collective-permute-done((f16[2,8,8,2048]{3,2,1,0:T(8,128)(2,1)}, f16[2,8,8,2048]{3,2,1,0:T(8,128)(2,1)S(1)}, u32[]{:S(2)}, u32[]{:S(2)}) %collective-permute-start.22) | collective-permute-done | bytes 524320 | tf_op jit(solution)/shard_map/ppermute | solution.py:13
  136.4 1.2 collective-permute-done.21
  137.5 2.1 %fusion.22 = f16[8,8,2048]{2,1,0:T(8,128)(2,1)} fusion(f32[2,2,17,8,2048]{4,3,2,1,0:T(8,128)} %copy-done, s32[]{:T(128)S(6)} %select_n.403, s32[]{:T(128)S(6)} %select_n.415, s32[]{:T(128)S(6)} %select_n.407, f32[]{:T(128)S(6)} %div.29, f32[]{:T(128)S(6)} %div.28, f16[2,8,8,2048]{3,2,1,0:T(8,128)(2,1)S(1)} %collective-permute-done.22, s32[]{:T(128)S(6)} %select_n.414, ...), kind=kLoop, calls=%fused_computation.52 | loop fusion | flops 1966080 | bytes 1572896 | tf_op jit(solution)/shard_map/convert_element_type | solution.py:121
  139.6 7.1 %collective-permute-start.23 = (f16[8,8,2048]{2,1,0:T(8,128)(2,1)}, f16[8,8,2048]{2,1,0:T(8,128)(2,1)S(1)}, u32[]{:S(2)}, u32[]{:S(2)}) collective-permute-start(f16[8,8,2048]{2,1,0:T(8,128)(2,1)} %fusion.22), channel_id=1, source_target_pairs={{0,32},{32,0},{64,96},{96,64},{128,160},{160,128},{192,224},{224,1... | collective-permute-start | bytes 786440 | tf_op jit(solution)/shard_map/ppermute | solution.py:13
  146.8 11.3 %collective-permute-done.27 = f16[2,8,8,2048]{3,2,1,0:T(8,128)(2,1)S(1)} collective-permute-done((f16[2,8,8,2048]{3,2,1,0:T(8,128)(2,1)}, f16[2,8,8,2048]{3,2,1,0:T(8,128)(2,1)S(1)}, u32[]{:S(2)}, u32[]{:S(2)}) %collective-permute-start.27) | collective-permute-done | bytes 524320 | tf_op jit(solution)/shard_map/ppermute | solution.py:13
  158.0 1.4 collective-permute-done.26
  159.5 1.3 fusion.17
  160.8 7.2 %collective-permute-start.28 = (f16[8,8,2048]{2,1,0:T(8,128)(2,1)S(1)}, f16[8,8,2048]{2,1,0:T(8,128)(2,1)S(1)}, u32[]{:S(2)}, u32[]{:S(2)}) collective-permute-start(f16[8,8,2048]{2,1,0:T(8,128)(2,1)S(1)} %fusion.17), channel_id=1, source_target_pairs={{0,32},{32,0},{64,96},{96,64},{128,160},{160,128},{192,224},{224,1... | collective-permute-start | bytes 786440 | tf_op jit(solution)/shard_map/ppermute | solution.py:13
  168.0 12.0 %collective-permute-done.28 = f16[8,8,2048]{2,1,0:T(8,128)(2,1)S(1)} collective-permute-done((f16[8,8,2048]{2,1,0:T(8,128)(2,1)S(1)}, f16[8,8,2048]{2,1,0:T(8,128)(2,1)S(1)}, u32[]{:S(2)}, u32[]{:S(2)}) %collective-permute-start.28) | collective-permute-done | bytes 262176 | tf_op jit(solution)/shard_map/ppermute | solution.py:13
  180.0 1.9 %select_bitcast_fusion.1 = (f32[1,8,8,2048]{3,2,1,0:T(8,128)S(1)}, f32[8,8,2048]{2,1,0:T(8,128)S(1)}, f32[8,8,2048]{2,1,0:T(8,128)S(1)}) fusion(pred[]{:T(512)S(6)} %eq.90, f32[]{:T(128)S(6)} %div.30, f32[]{:T(128)S(6)} %max.27, f16[8,8,2048]{2,1,0:T(8,128)(2,1)S(1)} %collective-permute-done.28, f16[2,8,8,2048]{3,2,1,0:T(8,128)(2,1)S(1)} %collective-permute-done.27, ...), kind=kLoop, calls=%fused_computation.61 | loop fusion | flops 4587520 | bytes 4724224 | tf_op jit(solution)/shard_map/stack | solution.py:124
  181.9 1.1 pad_maximum_fusion.1
  (51 shorter events, 1.6 us)
Async XLA Ops:
  2.5 10.1 %copy-start.1 = (s32[2]{0:T(128)S(1)}, s32[2]{0:T(128)}, u32[]{:S(2)}) copy-start(s32[2]{0:T(128)} %param.5) | copy-start | bytes 28
  2.5 26.3 %collective-permute-start.2 = (bf16[128,2048]{1,0:T(8,128)(2,1)}, bf16[128,2048]{1,0:T(8,128)(2,1)S(1)}, u32[]{:S(2)}, u32[]{:S(2)}) collective-permute-start(bf16[128,2048]{1,0:T(8,128)(2,1)} %get-tuple-element.50), channel_id=1, source_target_pairs={{0,24},{1,25},{2,26},{3,27},{4,28},{5,29},{6,30},{7,31},{8,16},{9,... | collective-permute-start | bytes 1572872 | tf_op jit(solution)/shard_map/ppermute | solution.py:13
  5.2 23.6 %collective-permute-start.1 = (bf16[128,2048]{1,0:T(8,128)(2,1)S(1)}, bf16[128,2048]{1,0:T(8,128)(2,1)S(1)}, u32[]{:S(2)}, u32[]{:S(2)}) collective-permute-start(bf16[128,2048]{1,0:T(8,128)(2,1)S(1)} %get-tuple-element.51), channel_id=1, source_target_pairs={{0,16},{1,17},{2,18},{3,19},{4,20},{5,21},{6,22},{7,23},{8,24},{9,... | collective-permute-start | bytes 1572872 | tf_op jit(solution)/shard_map/ppermute | solution.py:13
  6.0 23.2 %collective-permute-start = (bf16[128,2048]{1,0:T(8,128)(2,1)S(1)}, bf16[128,2048]{1,0:T(8,128)(2,1)S(1)}, u32[]{:S(2)}, u32[]{:S(2)}) collective-permute-start(bf16[128,2048]{1,0:T(8,128)(2,1)S(1)} %get-tuple-element.52), channel_id=1, source_target_pairs={{0,8},{1,9},{2,10},{3,11},{4,12},{5,13},{6,14},{7,15},{8,0},{9,1},... | collective-permute-start | bytes 1572872 | tf_op jit(solution)/shard_map/ppermute | solution.py:13
  29.5 3.3 %collective-permute-start.3 = (bf16[2,4,2,8,2048]{4,3,2,1,0:T(8,128)(2,1)S(1)}, bf16[2,4,2,8,2048]{4,3,2,1,0:T(8,128)(2,1)S(1)}, u32[]{:S(2)}, u32[]{:S(2)}) collective-permute-start(bf16[2,4,2,8,2048]{4,3,2,1,0:T(8,128)(2,1)S(1)} %pad_maximum_fusion.3), channel_id=1, source_target_pairs={{0,1},{1,0},{2,3},{3,2},{4,5},{5,4},{6,7},{7,6},{8,9},{9,8},{10,11... | collective-permute-start | bytes 1572872 | tf_op jit(solution)/shard_map/ppermute | solution.py:13
  33.5 7.7 %collective-permute-start.12 = (f32[3,2176]{1,0:T(4,128)S(1)}, f32[3,2176]{1,0:T(4,128)S(1)}, u32[]{:S(2)}, u32[]{:S(2)}) collective-permute-start(f32[3,2176]{1,0:T(4,128)S(1)} %maximum_maximum_fusion), channel_id=1, source_target_pairs={{0,192},{32,224},{64,128},{96,160},{128,64},{160,96},{192,0},{224,... | collective-permute-start | bytes 78344 | tf_op jit(solution)/shard_map/ppermute | solution.py:13
  36.6 5.5 %collective-permute-start.11 = (f32[3,2176]{1,0:T(4,128)S(1)}, f32[3,2176]{1,0:T(4,128)S(1)}, u32[]{:S(2)}, u32[]{:S(2)}) collective-permute-start(f32[3,2176]{1,0:T(4,128)S(1)} %maximum_maximum_fusion), channel_id=1, source_target_pairs={{0,128},{32,160},{64,192},{96,224},{128,0},{160,32},{192,64},{224,... | collective-permute-start | bytes 78344 | tf_op jit(solution)/shard_map/ppermute | solution.py:13
  37.3 4.8 %collective-permute-start.10 = (f32[3,2176]{1,0:T(4,128)S(1)}, f32[3,2176]{1,0:T(4,128)S(1)}, u32[]{:S(2)}, u32[]{:S(2)}) collective-permute-start(f32[3,2176]{1,0:T(4,128)S(1)} %maximum_maximum_fusion), channel_id=1, source_target_pairs={{0,64},{32,96},{64,0},{96,32},{128,192},{160,224},{192,128},{224,1... | collective-permute-start | bytes 78344 | tf_op jit(solution)/shard_map/ppermute | solution.py:13
  37.8 5.3 %collective-permute-start.4 = (bf16[2,2,8,2048]{3,2,1,0:T(8,128)(2,1)S(1)}, bf16[2,2,8,2048]{3,2,1,0:T(8,128)(2,1)S(1)}, u32[]{:S(2)}, u32[]{:S(2)}) collective-permute-start(bf16[2,2,8,2048]{3,2,1,0:T(8,128)(2,1)S(1)} %get-tuple-element.62), channel_id=1, source_target_pairs={{0,2},{1,3},{2,0},{3,1},{4,6},{5,7},{6,4},{7,5},{8,10},{9,11},{10,... | collective-permute-start | bytes 393224 | tf_op jit(solution)/shard_map/ppermute | solution.py:13
  37.9 13.5 %collective-permute-start.5 = (bf16[2,2,8,2048]{3,2,1,0:T(8,128)(2,1)S(1)}, bf16[2,2,8,2048]{3,2,1,0:T(8,128)(2,1)S(1)}, u32[]{:S(2)}, u32[]{:S(2)}) collective-permute-start(bf16[2,2,8,2048]{3,2,1,0:T(8,128)(2,1)S(1)} %get-tuple-element.63), channel_id=1, source_target_pairs={{0,4},{1,5},{2,6},{3,7},{4,0},{5,1},{6,2},{7,3},{8,12},{9,13},{10,... | collective-permute-start | bytes 393224 | tf_op jit(solution)/shard_map/ppermute | solution.py:13
  41.2 15.0 %collective-permute-start.6 = (bf16[2,2,8,2048]{3,2,1,0:T(8,128)(2,1)S(1)}, bf16[2,2,8,2048]{3,2,1,0:T(8,128)(2,1)S(1)}, u32[]{:S(2)}, u32[]{:S(2)}) collective-permute-start(bf16[2,2,8,2048]{3,2,1,0:T(8,128)(2,1)S(1)} %get-tuple-element.64), channel_id=1, source_target_pairs={{0,6},{1,7},{2,4},{3,5},{4,2},{5,3},{6,0},{7,1},{8,14},{9,15},{10,... | collective-permute-start | bytes 393224 | tf_op jit(solution)/shard_map/ppermute | solution.py:13
  43.0 16.9 %collective-permute-start.13 = (f32[3,2176]{1,0:T(4,128)S(1)}, f32[3,2176]{1,0:T(4,128)S(1)}, u32[]{:S(2)}, u32[]{:S(2)}) collective-permute-start(f32[3,2176]{1,0:T(4,128)S(1)} %pad_maximum_fusion.6), channel_id=1, source_target_pairs={{0,32},{32,0},{64,96},{96,64},{128,160},{160,128},{192,224},{224,1... | collective-permute-start | bytes 78344 | tf_op jit(solution)/shard_map/ppermute | solution.py:13
  56.3 11.8 %collective-permute-start.9 = (bf16[2,2,8,2048]{3,2,1,0:T(8,128)(2,1)S(1)}, bf16[2,2,8,2048]{3,2,1,0:T(8,128)(2,1)S(1)}, u32[]{:S(2)}, u32[]{:S(2)}) collective-permute-start(bf16[2,2,8,2048]{3,2,1,0:T(8,128)(2,1)S(1)} %pad_maximum_fusion.5), channel_id=1, source_target_pairs={{0,6},{1,7},{2,4},{3,5},{4,2},{5,3},{6,0},{7,1},{8,14},{9,15},{10,... | collective-permute-start | bytes 393224 | tf_op jit(solution)/shard_map/ppermute | solution.py:13
  57.9 10.1 %collective-permute-start.8 = (bf16[2,2,8,2048]{3,2,1,0:T(8,128)(2,1)S(1)}, bf16[2,2,8,2048]{3,2,1,0:T(8,128)(2,1)S(1)}, u32[]{:S(2)}, u32[]{:S(2)}) collective-permute-start(bf16[2,2,8,2048]{3,2,1,0:T(8,128)(2,1)S(1)} %pad_maximum_fusion.5), channel_id=1, source_target_pairs={{0,4},{1,5},{2,6},{3,7},{4,0},{5,1},{6,2},{7,3},{8,12},{9,13},{10,... | collective-permute-start | bytes 393224 | tf_op jit(solution)/shard_map/ppermute | solution.py:13
  57.9 6.6 %collective-permute-start.7 = (bf16[2,2,8,2048]{3,2,1,0:T(8,128)(2,1)S(1)}, bf16[2,2,8,2048]{3,2,1,0:T(8,128)(2,1)S(1)}, u32[]{:S(2)}, u32[]{:S(2)}) collective-permute-start(bf16[2,2,8,2048]{3,2,1,0:T(8,128)(2,1)S(1)} %pad_maximum_fusion.5), channel_id=1, source_target_pairs={{0,2},{1,3},{2,0},{3,1},{4,6},{5,7},{6,4},{7,5},{8,10},{9,11},{10,... | collective-permute-start | bytes 393224 | tf_op jit(solution)/shard_map/ppermute | solution.py:13
  64.6 3.7 %collective-permute-start.16 = (f32[2,2,4,2,8]{4,3,2,1,0:T(2,128)S(1)}, f32[2,2,4,2,8]{4,3,2,1,0:T(2,128)S(1)}, u32[]{:S(2)}, u32[]{:S(2)}) collective-permute-start(f32[2,2,4,2,8]{4,3,2,1,0:T(2,128)S(1)} %pad_maximum_fusion.8), channel_id=1, source_target_pairs={{0,6},{1,7},{2,4},{3,5},{4,2},{5,3},{6,0},{7,1},{8,14},{9,15},{10,... | collective-permute-start | bytes 3080 | tf_op jit(solution)/shard_map/ppermute | solution.py:13
  66.0 4.6 %collective-permute-start.15 = (f32[2,2,4,2,8]{4,3,2,1,0:T(2,128)S(1)}, f32[2,2,4,2,8]{4,3,2,1,0:T(2,128)S(1)}, u32[]{:S(2)}, u32[]{:S(2)}) collective-permute-start(f32[2,2,4,2,8]{4,3,2,1,0:T(2,128)S(1)} %pad_maximum_fusion.8), channel_id=1, source_target_pairs={{0,4},{1,5},{2,6},{3,7},{4,0},{5,1},{6,2},{7,3},{8,12},{9,13},{10,... | collective-permute-start | bytes 3080 | tf_op jit(solution)/shard_map/ppermute | solution.py:13
  67.4 3.7 %collective-permute-start.14 = (f32[2,2,4,2,8]{4,3,2,1,0:T(2,128)S(1)}, f32[2,2,4,2,8]{4,3,2,1,0:T(2,128)S(1)}, u32[]{:S(2)}, u32[]{:S(2)}) collective-permute-start(f32[2,2,4,2,8]{4,3,2,1,0:T(2,128)S(1)} %pad_maximum_fusion.8), channel_id=1, source_target_pairs={{0,2},{1,3},{2,0},{3,1},{4,6},{5,7},{6,4},{7,5},{8,10},{9,11},{10,... | collective-permute-start | bytes 3080 | tf_op jit(solution)/shard_map/ppermute | solution.py:13
  72.7 17.2 %collective-permute-start.18 = (bf16[17,8,2048]{2,1,0:T(8,128)(2,1)S(1)}, bf16[17,8,2048]{2,1,0:T(8,128)(2,1)S(1)}, u32[]{:S(2)}, u32[]{:S(2)}) collective-permute-start(bf16[17,8,2048]{2,1,0:T(8,128)(2,1)S(1)} %get-tuple-element.55), channel_id=1, source_target_pairs={{0,16},{1,17},{2,18},{3,19},{4,20},{5,21},{6,22},{7,23},{8,24},{9,... | collective-permute-start | bytes 1671176 | tf_op jit(solution)/shard_map/ppermute | solution.py:13
  75.8 21.0 %collective-permute-start.17 = (bf16[17,8,2048]{2,1,0:T(8,128)(2,1)S(1)}, bf16[17,8,2048]{2,1,0:T(8,128)(2,1)S(1)}, u32[]{:S(2)}, u32[]{:S(2)}) collective-permute-start(bf16[17,8,2048]{2,1,0:T(8,128)(2,1)S(1)} %get-tuple-element.55), channel_id=1, source_target_pairs={{0,8},{1,9},{2,10},{3,11},{4,12},{5,13},{6,14},{7,15},{8,0},{9,1},... | collective-permute-start | bytes 1671176 | tf_op jit(solution)/shard_map/ppermute | solution.py:13
  76.4 20.5 %collective-permute-start.19 = (bf16[17,8,2048]{2,1,0:T(8,128)(2,1)S(1)}, bf16[17,8,2048]{2,1,0:T(8,128)(2,1)S(1)}, u32[]{:S(2)}, u32[]{:S(2)}) collective-permute-start(bf16[17,8,2048]{2,1,0:T(8,128)(2,1)S(1)} %get-tuple-element.55), channel_id=1, source_target_pairs={{0,24},{1,25},{2,26},{3,27},{4,28},{5,29},{6,30},{7,31},{8,16},{9,... | collective-permute-start | bytes 1671176 | tf_op jit(solution)/shard_map/ppermute | solution.py:13
  97.1 16.2 %collective-permute-start.24 = (bf16[4,17,8,2048]{3,2,1,0:T(8,128)(2,1)S(1)}, bf16[4,17,8,2048]{3,2,1,0:T(8,128)(2,1)}, u32[]{:S(2)}, u32[]{:S(2)}) collective-permute-start(bf16[4,17,8,2048]{3,2,1,0:T(8,128)(2,1)S(1)} %pad_maximum_fusion), channel_id=1, source_target_pairs={{0,1},{1,0},{2,3},{3,2},{4,5},{5,4},{6,7},{7,6},{8,9},{9,8},{10,11... | collective-permute-start | bytes 6684680 | tf_op jit(solution)/shard_map/ppermute | solution.py:13
  107.3 17.0 %copy-start = (f32[2,2,17,8,2048]{4,3,2,1,0:T(8,128)}, f32[2,2,17,8,2048]{4,3,2,1,0:T(8,128)S(1)}, u32[]{:S(2)}) copy-start(f32[2,2,17,8,2048]{4,3,2,1,0:T(8,128)S(1)} %fusion.5) | copy-start | bytes 13369348
  109.1 23.9 %collective-permute-start.20 = (f16[2,8,8,2048]{3,2,1,0:T(8,128)(2,1)}, f16[2,8,8,2048]{3,2,1,0:T(8,128)(2,1)S(1)}, u32[]{:S(2)}, u32[]{:S(2)}) collective-permute-start(f16[2,8,8,2048]{3,2,1,0:T(8,128)(2,1)} %get-tuple-element.42), channel_id=1, source_target_pairs={{0,64},{32,96},{64,0},{96,32},{128,192},{160,224},{192,128},{224,1... | collective-permute-start | bytes 1572872 | tf_op jit(solution)/shard_map/ppermute | solution.py:13
  110.3 26.0 %collective-permute-start.22 = (f16[2,8,8,2048]{3,2,1,0:T(8,128)(2,1)}, f16[2,8,8,2048]{3,2,1,0:T(8,128)(2,1)S(1)}, u32[]{:S(2)}, u32[]{:S(2)}) collective-permute-start(f16[2,8,8,2048]{3,2,1,0:T(8,128)(2,1)} %get-tuple-element.43), channel_id=1, source_target_pairs={{0,192},{32,224},{64,128},{96,160},{128,64},{160,96},{192,0},{224,... | collective-permute-start | bytes 1572872 | tf_op jit(solution)/shard_map/ppermute | solution.py:13
  112.5 25.0 %collective-permute-start.21 = (f16[2,8,8,2048]{3,2,1,0:T(8,128)(2,1)}, f16[2,8,8,2048]{3,2,1,0:T(8,128)(2,1)}, u32[]{:S(2)}, u32[]{:S(2)}) collective-permute-start(f16[2,8,8,2048]{3,2,1,0:T(8,128)(2,1)} %get-tuple-element.44), channel_id=1, source_target_pairs={{0,128},{32,160},{64,192},{96,224},{128,0},{160,32},{192,64},{224,... | collective-permute-start | bytes 1572872 | tf_op jit(solution)/shard_map/ppermute | solution.py:13
  129.6 17.2 %collective-permute-start.25 = (f16[2,8,8,2048]{3,2,1,0:T(8,128)(2,1)}, f16[2,8,8,2048]{3,2,1,0:T(8,128)(2,1)S(1)}, u32[]{:S(2)}, u32[]{:S(2)}) collective-permute-start(f16[2,8,8,2048]{3,2,1,0:T(8,128)(2,1)} %get-tuple-element.45), channel_id=1, source_target_pairs={{0,64},{32,96},{64,0},{96,32},{128,192},{160,224},{192,128},{224,1... | collective-permute-start | bytes 1572872 | tf_op jit(solution)/shard_map/ppermute | solution.py:13
  130.8 27.3 %collective-permute-start.27 = (f16[2,8,8,2048]{3,2,1,0:T(8,128)(2,1)}, f16[2,8,8,2048]{3,2,1,0:T(8,128)(2,1)S(1)}, u32[]{:S(2)}, u32[]{:S(2)}) collective-permute-start(f16[2,8,8,2048]{3,2,1,0:T(8,128)(2,1)} %get-tuple-element.46), channel_id=1, source_target_pairs={{0,192},{32,224},{64,128},{96,160},{128,64},{160,96},{192,0},{224,... | collective-permute-start | bytes 1572872 | tf_op jit(solution)/shard_map/ppermute | solution.py:13
  133.0 26.5 %collective-permute-start.26 = (f16[2,8,8,2048]{3,2,1,0:T(8,128)(2,1)S(1)}, f16[2,8,8,2048]{3,2,1,0:T(8,128)(2,1)S(1)}, u32[]{:S(2)}, u32[]{:S(2)}) collective-permute-start(f16[2,8,8,2048]{3,2,1,0:T(8,128)(2,1)S(1)} %get-tuple-element.47), channel_id=1, source_target_pairs={{0,128},{32,160},{64,192},{96,224},{128,0},{160,32},{192,64},{224,... | collective-permute-start | bytes 1572872 | tf_op jit(solution)/shard_map/ppermute | solution.py:13
  139.6 28.4 %collective-permute-start.23 = (f16[8,8,2048]{2,1,0:T(8,128)(2,1)}, f16[8,8,2048]{2,1,0:T(8,128)(2,1)S(1)}, u32[]{:S(2)}, u32[]{:S(2)}) collective-permute-start(f16[8,8,2048]{2,1,0:T(8,128)(2,1)} %fusion.22), channel_id=1, source_target_pairs={{0,32},{32,0},{64,96},{96,64},{128,160},{160,128},{192,224},{224,1... | collective-permute-start | bytes 786440 | tf_op jit(solution)/shard_map/ppermute | solution.py:13
  160.8 19.2 %collective-permute-start.28 = (f16[8,8,2048]{2,1,0:T(8,128)(2,1)S(1)}, f16[8,8,2048]{2,1,0:T(8,128)(2,1)S(1)}, u32[]{:S(2)}, u32[]{:S(2)}) collective-permute-start(f16[8,8,2048]{2,1,0:T(8,128)(2,1)S(1)} %fusion.17), channel_id=1, source_target_pairs={{0,32},{32,0},{64,96},{96,64},{128,160},{160,128},{192,224},{224,1... | collective-permute-start | bytes 786440 | tf_op jit(solution)/shard_map/ppermute | solution.py:13

commit v4 on v3

--- a/solution.py
+++ b/solution.py
@@ -75,31 +75,30 @@
 
     mine = jnp.stack([pick(my_z ^ own_z[p], [f[p] for f in from_z]) for p in range(2)])
     parts = [mine] + [swap(mine, "samp", 2 * bits) for bits in (1, 2, 3)]
-    facts, parts[1] = after(facts, parts[1])
     facts_z = [facts] + [swap(facts, "samp", 2 * bits) for bits in (1, 2, 3)]
     facts = jnp.stack([pick(my_z ^ own_z[p], [f[:, p] for f in facts_z]) for p in range(2)], 1)
     line = jnp.stack([pick(my_z ^ place, parts) for place in range(4)], 1)
-    line = (line.astype(F32) - facts[0][..., None]).astype(BF16)
-    tiles = 16
-    bound = jnp.max(facts[1]) * 1.02
-    mark = jnp.broadcast_to(bound, (1, 8, shard)).astype(BF16)
-    sent = jnp.concatenate([line.reshape(tiles, 8, shard), mark])
+    sent = line.reshape(16, 8, shard)
     near = jnp.stack([sent] + [swap(sent, "samp", 8 * bits) for bits in (1, 2, 3)])
     far = swap(near, "samp", 1)
+    near_facts = jnp.stack([facts] + [swap(facts, "samp", 8 * bits) for bits in (1, 2, 3)])
+    far_facts = swap(near_facts, "samp", 1)
 
     first_anom = (first_plane.astype(F32) - first_mean[:, None]).astype(BF16)
     shrink_first = 4.0 / jnp.maximum(jnp.max(span[:samples]), 1e-30)
     grow_first = 1.0 / shrink_first
-    results = []
-    for anom in (near, far):
-        shrink_panel = 1.0 / jnp.maximum(jnp.max(anom[:, tiles, 0, :128].astype(F32)), 1e-30)
+    out = jnp.zeros((2, 8, 8, samples), F32)
+    for place, rows, its_facts in ((my_core, near, near_facts), (1 - my_core, far, far_facts)):
+        shrink_panel = 1.0 / jnp.maximum(jnp.max(its_facts[:, 1]), 1e-30)
         grow_panel = 1.0 / shrink_panel
+        means = its_facts[:, 0].reshape(4, 16, 8, 1)
+        anom = (rows.astype(F32) - means).astype(BF16)
         shares = lax.dot_general(
             anom.reshape(-1, shard),
             first_anom,
             (((1,), (1,)), ((), ())),
             preferred_element_type=F32,
-        ).reshape(2, 2, tiles + 1, 8, samples)
+        ).reshape(2, 2, 16, 8, samples)
 
         def for_y(dest):
             start = ((dest & 1) ^ (my_x >> 1), 0, 8 * (dest >> 1), 0, 0)
@@ -120,8 +119,8 @@
 
         other = (for_z(1 - my_zh) * shrink_first * shrink_panel).astype(WIRE)
         total = for_z(my_zh) + swap(other, "mem", 1).astype(F32) * grow_panel * grow_first
-        results.append(total / (members - 1))
-    return jnp.stack([pick(my_core ^ core, results) for core in range(2)]).reshape(-1, samples)
+        out = lax.dynamic_update_index_in_dim(out, total / (members - 1), place, 0)
+    return out.reshape(-1, samples)
 
 
 def solution(mesh):

time: 183 us -> 188 us (1.027)
  waiting for transfers between devices: 72.8 us -> 79.5 us
  matrix products: 18.4 us -> 12.7 us
  local copies, waits for them, and re-layouts: 4.39 us -> 8.38 us
    ppermute x29 -> x33, waiting for transfers between devices: 72.8 us -> 79.5 us  [swap(): return lax.ppermute(value, axis, [(i, i ^ bits) for i in range(size)])]
    dot_general x2, matrix products: 18.4 us -> 12.7 us  [per_device(): lax.dot_general(anom.reshape(-1, shard), first_anom, (((1,), (1,)), ((),...]
    unnamed x4 -> x17, local copies, waits for them, and re-layouts: 0.01 us -> 3.97 us
    another operation x4 -> x2, other arithmetic: 3.03 us -> 0.05 us  [per_device(): jnp.stack([facts] + [swap(facts, 'samp', 8 * bits) for bits in (1, 2, 3)])]
    dynamic_update_slice x0 -> x2, other arithmetic: none -> 2.78 us  [per_device(): out = lax.dynamic_update_index_in_dim(out, total / (members - 1), place, 0)]
    convert_element_type x2, other arithmetic: 5.11 us -> 3.07 us  [per_device(): sent = (for_y(my_y ^ bits) * shrink_first * shrink_panel).astype(WIRE)]
    ppermute x29 -> x33, starting transfers between devices: 53.8 us -> 54.2 us  [swap(): return lax.ppermute(value, axis, [(i, i ^ bits) for i in range(size)])]
  transfers between devices with their start and end apart: 29 -> 33, of which waited for: 17 -> 14; matrix products, arithmetic and copies ran while one was open for 23% -> 21% of each run, Pallas kernels for 0% -> 0%
where the time goes in v4:
time: 188 us
  waiting for transfers between devices  79.5 us (42%)
  starting transfers between devices  54.2 us (29%)
  other arithmetic  26.3 us (14%)
  matrix products  12.7 us (7%)
  local copies, waits for them, and re-layouts  8.38 us (4%)
  between operations  6.51 us (3%)
    ppermute x33, waiting for transfers between devices, swap(): return lax.ppermute(value, axis, [(i, i ^ bits) for i in range(size)])  79.5 us
    ppermute x33, starting transfers between devices, swap(): return lax.ppermute(value, axis, [(i, i ^ bits) for i in range(size)])  54.2 us
    dot_general x2, matrix products, per_device(): lax.dot_general(anom.reshape(-1, shard), first_anom, (((1,), (1,)), ((),...  12.7 us
    reduce_sum x2, other arithmetic, row_stats(): return jnp.stack([jnp.sum(wide, -1), jnp.max(wide, -1), jnp.max(-wide, -1)])  6.29 us
    reduce_max x3, other arithmetic, row_stats(): return jnp.stack([jnp.sum(wide, -1), jnp.max(wide, -1), jnp.max(-wide, -1)])  4.75 us
    unnamed x17, local copies, waits for them, and re-layouts  3.97 us
  transfers between devices with their start and end apart: 33, of which 14 were waited for; matrix products, arithmetic and copies ran while one was open for 21% of the time, Pallas kernels for 0%

profile of v4, /device:TPU:32, one launch (start us, length us, event | category | flops | bytes accessed | tf_op | source)
XLA Modules:
  0.0 187.6 jit_solution(4834867270520275197)
XLA Ops:
  0.0 2.5 %dynamic-slice_bitcast_fusion = (bf16[128,2048]{1,0:T(8,128)(2,1)S(1)}, bf16[128,2048]{1,0:T(8,128)(2,1)S(1)}, bf16[128,2048]{1,0:T(8,128)(2,1)}, bf16[128,2048]{1,0:T(8,128)(2,1)S(1)}) fusion(bf16[4,128,2048]{2,1,0:T(8,128)(2,1)} %bitcast.168, s32[]{:T(128)S(6)} %select_n.323, s32[]{:T(128)S(6)} %select_n.322, s32[]{:T(128)S(6)} %select_n.321, s32[]{:T(128)S(6)} %select_n.320), kind=kLoop, calls=%fused_computation.65 | loop fusion | bytes 4194320 | tf_op jit(solution)/shard_map/jit(dynamic_index_in_dim)/squeeze | solution.py:49
  2.5 1.5 collective-permute-start
  4.0 2.7 %collective-permute-start.1 = (bf16[128,2048]{1,0:T(8,128)(2,1)S(1)}, bf16[128,2048]{1,0:T(8,128)(2,1)S(1)}, u32[]{:S(2)}, u32[]{:S(2)}) collective-permute-start(bf16[128,2048]{1,0:T(8,128)(2,1)S(1)} %get-tuple-element.42), channel_id=1, source_target_pairs={{0,16},{1,17},{2,18},{3,19},{4,20},{5,21},{6,22},{7,23},{8,24},{9,... | collective-permute-start | bytes 1572872 | tf_op jit(solution)/shard_map/ppermute | solution.py:13
  6.7 0.5 collective-permute-start.2
  7.2 6.0 %convert_reduce_fusion = (f32[2048]{0:T(1024)S(1)}, f32[2048]{0:T(1024)S(1)}) fusion(bf16[2048,2048]{1,0:T(8,128)(2,1)} %param.3), kind=kLoop, calls=%fused_computation.2 | loop fusion | flops 16773120 | bytes 8404992 | tf_op jit(solution)/shard_map/reduce_sum | solution.py:25
  13.3 0.6 fusion.47
  15.2 4.6 %reduce_max.77 = bf16[2048]{0:T(1024)(128)(2,1)S(1)} reduce(bf16[2048,2048]{1,0:T(8,128)(2,1)} %param.3, bf16[]{:T(256)} %constant.207.clone.1), dimensions={1}, to_apply=%region_1.2 | reduce | flops 4192256 | bytes 8392706 | tf_op jit(solution)/shard_map/reduce_max | solution.py:25
  19.8 10.1 %collective-permute-done.1 = bf16[128,2048]{1,0:T(8,128)(2,1)S(1)} collective-permute-done((bf16[128,2048]{1,0:T(8,128)(2,1)S(1)}, bf16[128,2048]{1,0:T(8,128)(2,1)S(1)}, u32[]{:S(2)}, u32[]{:S(2)}) %collective-permute-start.1) | collective-permute-done | bytes 524320 | tf_op jit(solution)/shard_map/ppermute | solution.py:13
  29.9 2.4 %collective-permute-done.2 = bf16[128,2048]{1,0:T(8,128)(2,1)S(1)} collective-permute-done((bf16[128,2048]{1,0:T(8,128)(2,1)S(1)}, bf16[128,2048]{1,0:T(8,128)(2,1)S(1)}, u32[]{:S(2)}, u32[]{:S(2)}) %collective-permute-start.2) | collective-permute-done | bytes 524320 | tf_op jit(solution)/shard_map/ppermute | solution.py:13
  32.6 0.7 fusion.45
  36.0 0.2 convert_reduce_fusion.1
  36.7 3.1 %collective-permute-start.15 = (f32[3,2176]{1,0:T(4,128)S(1)}, f32[3,2176]{1,0:T(4,128)S(1)}, u32[]{:S(2)}, u32[]{:S(2)}) collective-permute-start(f32[3,2176]{1,0:T(4,128)S(1)} %maximum_maximum_fusion), channel_id=1, source_target_pairs={{0,192},{32,224},{64,128},{96,160},{128,64},{160,96},{192,0},{224,... | collective-permute-start | bytes 78344 | tf_op jit(solution)/shard_map/ppermute | solution.py:13
  39.8 0.6 collective-permute-start.14
  40.5 0.5 collective-permute-start.13
  41.2 3.7 %collective-permute-start.6 = (bf16[2,2,8,2048]{3,2,1,0:T(8,128)(2,1)S(1)}, bf16[2,2,8,2048]{3,2,1,0:T(8,128)(2,1)S(1)}, u32[]{:S(2)}, u32[]{:S(2)}) collective-permute-start(bf16[2,2,8,2048]{3,2,1,0:T(8,128)(2,1)S(1)} %get-tuple-element.53), channel_id=1, source_target_pairs={{0,6},{1,7},{2,4},{3,5},{4,2},{5,3},{6,0},{7,1},{8,14},{9,15},{10,... | collective-permute-start | bytes 393224 | tf_op jit(solution)/shard_map/ppermute | solution.py:13
  44.9 0.6 collective-permute-start.5
  45.6 0.7 collective-permute-done.4
  46.3 7.5 %collective-permute-start.16 = (f32[3,2176]{1,0:T(4,128)S(1)}, f32[3,2176]{1,0:T(4,128)S(1)}, u32[]{:S(2)}, u32[]{:S(2)}) collective-permute-start(f32[3,2176]{1,0:T(4,128)S(1)} %pad_maximum_fusion.6), channel_id=1, source_target_pairs={{0,32},{32,0},{64,96},{96,64},{128,160},{160,128},{192,224},{224,1... | collective-permute-start | bytes 78344 | tf_op jit(solution)/shard_map/ppermute | solution.py:13
  53.7 1.8 collective-permute-done.6
  55.5 1.7 collective-permute-done.5
  57.3 2.3 %collective-permute-start.7 = (bf16[2,2,8,2048]{3,2,1,0:T(8,128)(2,1)S(1)}, bf16[2,2,8,2048]{3,2,1,0:T(8,128)(2,1)S(1)}, u32[]{:S(2)}, u32[]{:S(2)}) collective-permute-start(bf16[2,2,8,2048]{3,2,1,0:T(8,128)(2,1)S(1)} %pad_maximum_fusion.4), channel_id=1, source_target_pairs={{0,2},{1,3},{2,0},{3,1},{4,6},{5,7},{6,4},{7,5},{8,10},{9,11},{10,... | collective-permute-start | bytes 393224 | tf_op jit(solution)/shard_map/ppermute | solution.py:13
  59.6 1.4 collective-permute-start.8
  61.1 0.3 collective-permute-start.9
  61.7 1.8 collective-permute-start.19
  63.5 3.3 %collective-permute-start.18 = (f32[2,2,4,2,8]{4,3,2,1,0:T(2,128)S(1)}, f32[2,2,4,2,8]{4,3,2,1,0:T(2,128)S(1)}, u32[]{:S(2)}, u32[]{:S(2)}) collective-permute-start(f32[2,2,4,2,8]{4,3,2,1,0:T(2,128)S(1)} %constant_dynamic-update-slice_fusion), channel_id=1, source_target_pairs={{0,4},{1,5},{2,6},{3,7},{4,0},{5,1},{6,2},{7,3},{8,12},{9,13},{10,... | collective-permute-start | bytes 3080 | tf_op jit(solution)/shard_map/ppermute | solution.py:13
  66.8 0.3 collective-permute-start.17
  67.0 3.7 %collective-permute-done.8 = bf16[2,2,8,2048]{3,2,1,0:T(8,128)(2,1)S(1)} collective-permute-done((bf16[2,2,8,2048]{3,2,1,0:T(8,128)(2,1)S(1)}, bf16[2,2,8,2048]{3,2,1,0:T(8,128)(2,1)S(1)}, u32[]{:S(2)}, u32[]{:S(2)}) %collective-permute-start.8) | collective-permute-done | bytes 131104 | tf_op jit(solution)/shard_map/ppermute | solution.py:13
  70.7 2.8 %collective-permute-done.9 = bf16[2,2,8,2048]{3,2,1,0:T(8,128)(2,1)S(1)} collective-permute-done((bf16[2,2,8,2048]{3,2,1,0:T(8,128)(2,1)S(1)}, bf16[2,2,8,2048]{3,2,1,0:T(8,128)(2,1)S(1)}, u32[]{:S(2)}, u32[]{:S(2)}) %collective-permute-start.9) | collective-permute-done | bytes 131104 | tf_op jit(solution)/shard_map/ppermute | solution.py:13
  73.6 0.6 collective-permute-start.12
  74.2 0.6 collective-permute-start.11
  74.8 3.0 %collective-permute-start.10 = (bf16[16,8,2048]{2,1,0:T(8,128)(2,1)S(1)}, bf16[16,8,2048]{2,1,0:T(8,128)(2,1)S(1)}, u32[]{:S(2)}, u32[]{:S(2)}) collective-permute-start(bf16[16,8,2048]{2,1,0:T(8,128)(2,1)S(1)} %bitcast.171), channel_id=1, source_target_pairs={{0,8},{1,9},{2,10},{3,11},{4,12},{5,13},{6,14},{7,15},{8,0},{9,1},... | collective-permute-start | bytes 1572872 | tf_op jit(solution)/shard_map/ppermute | solution.py:13
  77.9 0.6 collective-permute-start.22
  78.5 1.6 collective-permute-start.21
  80.1 18.5 %collective-permute-done.22 = f32[2,2,4,2,8]{4,3,2,1,0:T(2,128)S(1)} collective-permute-done((f32[2,2,4,2,8]{4,3,2,1,0:T(2,128)S(1)}, f32[2,2,4,2,8]{4,3,2,1,0:T(2,128)S(1)}, u32[]{:S(2)}, u32[]{:S(2)}) %collective-permute-start.22) | collective-permute-done | bytes 1056 | tf_op jit(solution)/shard_map/ppermute | solution.py:13
  98.6 0.6 slice_reduce_fusion.2
  99.9 2.4 %collective-permute-done.20 = f32[2,2,4,2,8]{4,3,2,1,0:T(2,128)S(1)} collective-permute-done((f32[2,2,4,2,8]{4,3,2,1,0:T(2,128)S(1)}, f32[2,2,4,2,8]{4,3,2,1,0:T(2,128)S(1)}, u32[]{:S(2)}, u32[]{:S(2)}) %collective-permute-start.20) | collective-permute-done | bytes 1056 | tf_op jit(solution)/shard_map/ppermute | solution.py:13
  102.5 0.8 copy-done.3
  103.5 1.5 pad_maximum_fusion
  105.0 0.6 collective-permute-start.27
  105.5 0.6 slice_reduce_fusion.1
  106.9 0.6 slice_reduce_fusion
  108.2 8.0 %fusion.5 = f32[2,2,16,8,2048]{4,3,2,1,0:T(8,128)S(1)} fusion(bf16[2048,2048]{1,0:T(8,128)(2,1)} %param.3, f32[2048]{0:T(1024)S(1)} %bitcast.184, bf16[2,2,16,8,2048]{4,3,2,1,0:T(8,128)(2,1)S(1)} %bitcast.166, f32[2,2,16,8]{3,2,1,0:T(8,128)S(1)} %bitcast.177), kind=kOutput, calls=%fused_computation.7 | convolution fusion | flops 4310695936 | bytes 14690304 | tf_op jit(solution)/shard_map/dot_general | solution.py:96
  116.2 1.7 fusion.11
  117.9 2.8 %collective-permute-start.25 = (f16[2,8,8,2048]{3,2,1,0:T(8,128)(2,1)S(1)}, f16[2,8,8,2048]{3,2,1,0:T(8,128)(2,1)S(1)}, u32[]{:S(2)}, u32[]{:S(2)}) collective-permute-start(f16[2,8,8,2048]{3,2,1,0:T(8,128)(2,1)S(1)} %get-tuple-element.37), channel_id=1, source_target_pairs={{0,192},{32,224},{64,128},{96,160},{128,64},{160,96},{192,0},{224,... | collective-permute-start | bytes 1572872 | tf_op jit(solution)/shard_map/ppermute | solution.py:13
  120.6 0.6 collective-permute-start.24
  121.3 0.7 collective-permute-start.23
  122.0 2.0 %subtract_convert_fusion = bf16[4,16,8,2048]{3,2,1,0:T(8,128)(2,1)S(1)} fusion(bf16[4,16,8,2048]{3,2,1,0:T(8,128)(2,1)} %collective-permute-done.27, f32[4,16,8]{2,1,0:T(8,128)S(1)} %bitcast.176), kind=kLoop, calls=%fused_computation.10 | loop fusion | flops 3145728 | bytes 4196352 | tf_op jit(solution)/shard_map/convert_element_type | solution.py:95
  124.0 4.7 %fusion.3 = f32[2,2,16,8,2048]{4,3,2,1,0:T(8,128)S(1)} fusion(bf16[2,2,16,8,2048]{4,3,2,1,0:T(8,128)(2,1)S(1)} %bitcast.167, bf16[2048,2048]{1,0:T(8,128)(2,1)S(1)} %bitcast.161, f32[2048]{0:T(1024)S(1)} %bitcast.185), kind=kOutput, calls=%fused_computation.6 | convolution fusion | flops 4307550208 | bytes 14688256 | tf_op jit(solution)/shard_map/dot_general | solution.py:96
  128.7 2.0 %copy-done.1 = f32[2,2,16,8,2048]{4,3,2,1,0:T(8,128)} copy-done((f32[2,2,16,8,2048]{4,3,2,1,0:T(8,128)}, f32[2,2,16,8,2048]{4,3,2,1,0:T(8,128)S(1)}, u32[]{:S(2)}) %copy-start.1) | copy-done | bytes 4194328
  130.8 1.4 fusion.14
  132.2 2.8 %collective-permute-start.31 = (f16[2,8,8,2048]{3,2,1,0:T(8,128)(2,1)}, f16[2,8,8,2048]{3,2,1,0:T(8,128)(2,1)S(1)}, u32[]{:S(2)}, u32[]{:S(2)}) collective-permute-start(f16[2,8,8,2048]{3,2,1,0:T(8,128)(2,1)} %get-tuple-element.34), channel_id=1, source_target_pairs={{0,192},{32,224},{64,128},{96,160},{128,64},{160,96},{192,0},{224,... | collective-permute-start | bytes 1572872 | tf_op jit(solution)/shard_map/ppermute | solution.py:13
  134.9 0.6 collective-permute-start.30
  135.6 9.5 %collective-permute-done.25 = f16[2,8,8,2048]{3,2,1,0:T(8,128)(2,1)S(1)} collective-permute-done((f16[2,8,8,2048]{3,2,1,0:T(8,128)(2,1)S(1)}, f16[2,8,8,2048]{3,2,1,0:T(8,128)(2,1)S(1)}, u32[]{:S(2)}, u32[]{:S(2)}) %collective-permute-start.25) | collective-permute-done | bytes 524320 | tf_op jit(solution)/shard_map/ppermute | solution.py:13
  145.2 1.1 collective-permute-done.23
  146.3 2.1 %fusion.24 = f16[8,8,2048]{2,1,0:T(8,128)(2,1)} fusion(f32[2,2,16,8,2048]{4,3,2,1,0:T(8,128)} %copy-done, s32[]{:T(128)S(6)} %select_n.391, s32[]{:T(128)S(6)} %select_n.403, s32[]{:T(128)S(6)} %select_n.395, f32[]{:T(128)S(6)} %div.29, f32[]{:T(128)S(6)} %div.28, f16[2,8,8,2048]{3,2,1,0:T(8,128)(2,1)S(1)} %collective-permute-done.25, s32[]{:T(128)S(6)} %select_n.402, ...), kind=kLoop, calls=%fused_computation.55 | loop fusion | flops 1966080 | bytes 1572896 | tf_op jit(solution)/shard_map/convert_element_type | solution.py:120
  148.4 4.6 %collective-permute-start.26 = (f16[8,8,2048]{2,1,0:T(8,128)(2,1)}, f16[8,8,2048]{2,1,0:T(8,128)(2,1)S(1)}, u32[]{:S(2)}, u32[]{:S(2)}) collective-permute-start(f16[8,8,2048]{2,1,0:T(8,128)(2,1)} %fusion.24), channel_id=1, source_target_pairs={{0,32},{32,0},{64,96},{96,64},{128,160},{160,128},{192,224},{224,1... | collective-permute-start | bytes 786440 | tf_op jit(solution)/shard_map/ppermute | solution.py:13
  153.0 13.6 %collective-permute-done.31 = f16[2,8,8,2048]{3,2,1,0:T(8,128)(2,1)S(1)} collective-permute-done((f16[2,8,8,2048]{3,2,1,0:T(8,128)(2,1)}, f16[2,8,8,2048]{3,2,1,0:T(8,128)(2,1)S(1)}, u32[]{:S(2)}, u32[]{:S(2)}) %collective-permute-start.31) | collective-permute-done | bytes 524320 | tf_op jit(solution)/shard_map/ppermute | solution.py:13
  166.6 0.9 collective-permute-done.29
  167.5 1.3 fusion.19
  168.8 4.7 %collective-permute-start.32 = (f16[8,8,2048]{2,1,0:T(8,128)(2,1)S(1)}, f16[8,8,2048]{2,1,0:T(8,128)(2,1)S(1)}, u32[]{:S(2)}, u32[]{:S(2)}) collective-permute-start(f16[8,8,2048]{2,1,0:T(8,128)(2,1)S(1)} %fusion.19), channel_id=1, source_target_pairs={{0,32},{32,0},{64,96},{96,64},{128,160},{160,128},{192,224},{224,1... | collective-permute-start | bytes 786440 | tf_op jit(solution)/shard_map/ppermute | solution.py:13
  173.6 1.4 bitcast_dynamic-update-slice_fusion.1
  175.1 10.2 %collective-permute-done.32 = f16[8,8,2048]{2,1,0:T(8,128)(2,1)S(1)} collective-permute-done((f16[8,8,2048]{2,1,0:T(8,128)(2,1)S(1)}, f16[8,8,2048]{2,1,0:T(8,128)(2,1)S(1)}, u32[]{:S(2)}, u32[]{:S(2)}) %collective-permute-start.32) | collective-permute-done | bytes 262176 | tf_op jit(solution)/shard_map/ppermute | solution.py:13
  185.3 1.3 bitcast_dynamic-update-slice_fusion
  186.6 1.0 copy-done.2
  (73 shorter events, 2.3 us)
Async XLA Ops:
  2.5 17.3 %collective-permute-start = (bf16[128,2048]{1,0:T(8,128)(2,1)}, bf16[128,2048]{1,0:T(8,128)(2,1)S(1)}, u32[]{:S(2)}, u32[]{:S(2)}) collective-permute-start(bf16[128,2048]{1,0:T(8,128)(2,1)} %get-tuple-element.43), channel_id=1, source_target_pairs={{0,8},{1,9},{2,10},{3,11},{4,12},{5,13},{6,14},{7,15},{8,0},{9,1},... | collective-permute-start | bytes 1572872 | tf_op jit(solution)/shard_map/ppermute | solution.py:13
  4.0 25.9 %collective-permute-start.1 = (bf16[128,2048]{1,0:T(8,128)(2,1)S(1)}, bf16[128,2048]{1,0:T(8,128)(2,1)S(1)}, u32[]{:S(2)}, u32[]{:S(2)}) collective-permute-start(bf16[128,2048]{1,0:T(8,128)(2,1)S(1)} %get-tuple-element.42), channel_id=1, source_target_pairs={{0,16},{1,17},{2,18},{3,19},{4,20},{5,21},{6,22},{7,23},{8,24},{9,... | collective-permute-start | bytes 1572872 | tf_op jit(solution)/shard_map/ppermute | solution.py:13
  6.7 25.5 %collective-permute-start.2 = (bf16[128,2048]{1,0:T(8,128)(2,1)S(1)}, bf16[128,2048]{1,0:T(8,128)(2,1)S(1)}, u32[]{:S(2)}, u32[]{:S(2)}) collective-permute-start(bf16[128,2048]{1,0:T(8,128)(2,1)S(1)} %get-tuple-element.41), channel_id=1, source_target_pairs={{0,24},{1,25},{2,26},{3,27},{4,28},{5,29},{6,30},{7,31},{8,16},{9,... | collective-permute-start | bytes 1572872 | tf_op jit(solution)/shard_map/ppermute | solution.py:13
  7.2 6.1 %copy-start.5 = (s32[2]{0:T(128)S(1)}, s32[2]{0:T(128)}, u32[]{:S(2)}) copy-start(s32[2]{0:T(128)} %param.5) | copy-start | bytes 28
  32.5 3.5 %collective-permute-start.3 = (bf16[2,4,2,8,2048]{4,3,2,1,0:T(8,128)(2,1)S(1)}, bf16[2,4,2,8,2048]{4,3,2,1,0:T(8,128)(2,1)S(1)}, u32[]{:S(2)}, u32[]{:S(2)}) collective-permute-start(bf16[2,4,2,8,2048]{4,3,2,1,0:T(8,128)(2,1)S(1)} %pad_maximum_fusion.2), channel_id=1, source_target_pairs={{0,1},{1,0},{2,3},{3,2},{4,5},{5,4},{6,7},{7,6},{8,9},{9,8},{10,11... | collective-permute-start | bytes 1572872 | tf_op jit(solution)/shard_map/ppermute | solution.py:13
  36.7 8.2 %collective-permute-start.15 = (f32[3,2176]{1,0:T(4,128)S(1)}, f32[3,2176]{1,0:T(4,128)S(1)}, u32[]{:S(2)}, u32[]{:S(2)}) collective-permute-start(f32[3,2176]{1,0:T(4,128)S(1)} %maximum_maximum_fusion), channel_id=1, source_target_pairs={{0,192},{32,224},{64,128},{96,160},{128,64},{160,96},{192,0},{224,... | collective-permute-start | bytes 78344 | tf_op jit(solution)/shard_map/ppermute | solution.py:13
  39.8 5.6 %collective-permute-start.14 = (f32[3,2176]{1,0:T(4,128)S(1)}, f32[3,2176]{1,0:T(4,128)S(1)}, u32[]{:S(2)}, u32[]{:S(2)}) collective-permute-start(f32[3,2176]{1,0:T(4,128)S(1)} %maximum_maximum_fusion), channel_id=1, source_target_pairs={{0,128},{32,160},{64,192},{96,224},{128,0},{160,32},{192,64},{224,... | collective-permute-start | bytes 78344 | tf_op jit(solution)/shard_map/ppermute | solution.py:13
  40.5 5.0 %collective-permute-start.13 = (f32[3,2176]{1,0:T(4,128)S(1)}, f32[3,2176]{1,0:T(4,128)S(1)}, u32[]{:S(2)}, u32[]{:S(2)}) collective-permute-start(f32[3,2176]{1,0:T(4,128)S(1)} %maximum_maximum_fusion), channel_id=1, source_target_pairs={{0,64},{32,96},{64,0},{96,32},{128,192},{160,224},{192,128},{224,1... | collective-permute-start | bytes 78344 | tf_op jit(solution)/shard_map/ppermute | solution.py:13
  41.0 5.3 %collective-permute-start.4 = (bf16[2,2,8,2048]{3,2,1,0:T(8,128)(2,1)S(1)}, bf16[2,2,8,2048]{3,2,1,0:T(8,128)(2,1)S(1)}, u32[]{:S(2)}, u32[]{:S(2)}) collective-permute-start(bf16[2,2,8,2048]{3,2,1,0:T(8,128)(2,1)S(1)} %get-tuple-element.51), channel_id=1, source_target_pairs={{0,2},{1,3},{2,0},{3,1},{4,6},{5,7},{6,4},{7,5},{8,10},{9,11},{10,... | collective-permute-start | bytes 393224 | tf_op jit(solution)/shard_map/ppermute | solution.py:13
  41.2 14.3 %collective-permute-start.6 = (bf16[2,2,8,2048]{3,2,1,0:T(8,128)(2,1)S(1)}, bf16[2,2,8,2048]{3,2,1,0:T(8,128)(2,1)S(1)}, u32[]{:S(2)}, u32[]{:S(2)}) collective-permute-start(bf16[2,2,8,2048]{3,2,1,0:T(8,128)(2,1)S(1)} %get-tuple-element.53), channel_id=1, source_target_pairs={{0,6},{1,7},{2,4},{3,5},{4,2},{5,3},{6,0},{7,1},{8,14},{9,15},{10,... | collective-permute-start | bytes 393224 | tf_op jit(solution)/shard_map/ppermute | solution.py:13
  44.9 12.4 %collective-permute-start.5 = (bf16[2,2,8,2048]{3,2,1,0:T(8,128)(2,1)S(1)}, bf16[2,2,8,2048]{3,2,1,0:T(8,128)(2,1)S(1)}, u32[]{:S(2)}, u32[]{:S(2)}) collective-permute-start(bf16[2,2,8,2048]{3,2,1,0:T(8,128)(2,1)S(1)} %get-tuple-element.52), channel_id=1, source_target_pairs={{0,4},{1,5},{2,6},{3,7},{4,0},{5,1},{6,2},{7,3},{8,12},{9,13},{10,... | collective-permute-start | bytes 393224 | tf_op jit(solution)/shard_map/ppermute | solution.py:13
  46.3 15.1 %collective-permute-start.16 = (f32[3,2176]{1,0:T(4,128)S(1)}, f32[3,2176]{1,0:T(4,128)S(1)}, u32[]{:S(2)}, u32[]{:S(2)}) collective-permute-start(f32[3,2176]{1,0:T(4,128)S(1)} %pad_maximum_fusion.6), channel_id=1, source_target_pairs={{0,32},{32,0},{64,96},{96,64},{128,160},{160,128},{192,224},{224,1... | collective-permute-start | bytes 78344 | tf_op jit(solution)/shard_map/ppermute | solution.py:13
  57.3 9.5 %collective-permute-start.7 = (bf16[2,2,8,2048]{3,2,1,0:T(8,128)(2,1)S(1)}, bf16[2,2,8,2048]{3,2,1,0:T(8,128)(2,1)S(1)}, u32[]{:S(2)}, u32[]{:S(2)}) collective-permute-start(bf16[2,2,8,2048]{3,2,1,0:T(8,128)(2,1)S(1)} %pad_maximum_fusion.4), channel_id=1, source_target_pairs={{0,2},{1,3},{2,0},{3,1},{4,6},{5,7},{6,4},{7,5},{8,10},{9,11},{10,... | collective-permute-start | bytes 393224 | tf_op jit(solution)/shard_map/ppermute | solution.py:13
  59.6 11.1 %collective-permute-start.8 = (bf16[2,2,8,2048]{3,2,1,0:T(8,128)(2,1)S(1)}, bf16[2,2,8,2048]{3,2,1,0:T(8,128)(2,1)S(1)}, u32[]{:S(2)}, u32[]{:S(2)}) collective-permute-start(bf16[2,2,8,2048]{3,2,1,0:T(8,128)(2,1)S(1)} %pad_maximum_fusion.4), channel_id=1, source_target_pairs={{0,4},{1,5},{2,6},{3,7},{4,0},{5,1},{6,2},{7,3},{8,12},{9,13},{10,... | collective-permute-start | bytes 393224 | tf_op jit(solution)/shard_map/ppermute | solution.py:13
  61.1 12.4 %collective-permute-start.9 = (bf16[2,2,8,2048]{3,2,1,0:T(8,128)(2,1)S(1)}, bf16[2,2,8,2048]{3,2,1,0:T(8,128)(2,1)S(1)}, u32[]{:S(2)}, u32[]{:S(2)}) collective-permute-start(bf16[2,2,8,2048]{3,2,1,0:T(8,128)(2,1)S(1)} %pad_maximum_fusion.4), channel_id=1, source_target_pairs={{0,6},{1,7},{2,4},{3,5},{4,2},{5,3},{6,0},{7,1},{8,14},{9,15},{10,... | collective-permute-start | bytes 393224 | tf_op jit(solution)/shard_map/ppermute | solution.py:13
  61.7 13.1 %collective-permute-start.19 = (f32[2,2,4,2,8]{4,3,2,1,0:T(2,128)S(1)}, f32[2,2,4,2,8]{4,3,2,1,0:T(2,128)S(1)}, u32[]{:S(2)}, u32[]{:S(2)}) collective-permute-start(f32[2,2,4,2,8]{4,3,2,1,0:T(2,128)S(1)} %constant_dynamic-update-slice_fusion), channel_id=1, source_target_pairs={{0,6},{1,7},{2,4},{3,5},{4,2},{5,3},{6,0},{7,1},{8,14},{9,15},{10,... | collective-permute-start | bytes 3080 | tf_op jit(solution)/shard_map/ppermute | solution.py:13
  63.5 14.3 %collective-permute-start.18 = (f32[2,2,4,2,8]{4,3,2,1,0:T(2,128)S(1)}, f32[2,2,4,2,8]{4,3,2,1,0:T(2,128)S(1)}, u32[]{:S(2)}, u32[]{:S(2)}) collective-permute-start(f32[2,2,4,2,8]{4,3,2,1,0:T(2,128)S(1)} %constant_dynamic-update-slice_fusion), channel_id=1, source_target_pairs={{0,4},{1,5},{2,6},{3,7},{4,0},{5,1},{6,2},{7,3},{8,12},{9,13},{10,... | collective-permute-start | bytes 3080 | tf_op jit(solution)/shard_map/ppermute | solution.py:13
  66.8 11.1 %collective-permute-start.17 = (f32[2,2,4,2,8]{4,3,2,1,0:T(2,128)S(1)}, f32[2,2,4,2,8]{4,3,2,1,0:T(2,128)S(1)}, u32[]{:S(2)}, u32[]{:S(2)}) collective-permute-start(f32[2,2,4,2,8]{4,3,2,1,0:T(2,128)S(1)} %constant_dynamic-update-slice_fusion), channel_id=1, source_target_pairs={{0,2},{1,3},{2,0},{3,1},{4,6},{5,7},{6,4},{7,5},{8,10},{9,11},{10,... | collective-permute-start | bytes 3080 | tf_op jit(solution)/shard_map/ppermute | solution.py:13
  73.6 28.8 %collective-permute-start.12 = (bf16[16,8,2048]{2,1,0:T(8,128)(2,1)S(1)}, bf16[16,8,2048]{2,1,0:T(8,128)(2,1)S(1)}, u32[]{:S(2)}, u32[]{:S(2)}) collective-permute-start(bf16[16,8,2048]{2,1,0:T(8,128)(2,1)S(1)} %bitcast.169), channel_id=1, source_target_pairs={{0,24},{1,25},{2,26},{3,27},{4,28},{5,29},{6,30},{7,31},{8,16},{9,... | collective-permute-start | bytes 1572872 | tf_op jit(solution)/shard_map/ppermute | solution.py:13
  74.2 28.3 %collective-permute-start.11 = (bf16[16,8,2048]{2,1,0:T(8,128)(2,1)S(1)}, bf16[16,8,2048]{2,1,0:T(8,128)(2,1)S(1)}, u32[]{:S(2)}, u32[]{:S(2)}) collective-permute-start(bf16[16,8,2048]{2,1,0:T(8,128)(2,1)S(1)} %bitcast.170), channel_id=1, source_target_pairs={{0,16},{1,17},{2,18},{3,19},{4,20},{5,21},{6,22},{7,23},{8,24},{9,... | collective-permute-start | bytes 1572872 | tf_op jit(solution)/shard_map/ppermute | solution.py:13
  74.8 27.7 %collective-permute-start.10 = (bf16[16,8,2048]{2,1,0:T(8,128)(2,1)S(1)}, bf16[16,8,2048]{2,1,0:T(8,128)(2,1)S(1)}, u32[]{:S(2)}, u32[]{:S(2)}) collective-permute-start(bf16[16,8,2048]{2,1,0:T(8,128)(2,1)S(1)} %bitcast.171), channel_id=1, source_target_pairs={{0,8},{1,9},{2,10},{3,11},{4,12},{5,13},{6,14},{7,15},{8,0},{9,1},... | collective-permute-start | bytes 1572872 | tf_op jit(solution)/shard_map/ppermute | solution.py:13
  77.9 20.7 %collective-permute-start.22 = (f32[2,2,4,2,8]{4,3,2,1,0:T(2,128)S(1)}, f32[2,2,4,2,8]{4,3,2,1,0:T(2,128)S(1)}, u32[]{:S(2)}, u32[]{:S(2)}) collective-permute-start(f32[2,2,4,2,8]{4,3,2,1,0:T(2,128)S(1)} %get-tuple-element.63), channel_id=1, source_target_pairs={{0,24},{1,25},{2,26},{3,27},{4,28},{5,29},{6,30},{7,31},{8,16},{9,... | collective-permute-start | bytes 3080 | tf_op jit(solution)/shard_map/ppermute | solution.py:13
  78.5 21.5 %collective-permute-start.21 = (f32[2,2,4,2,8]{4,3,2,1,0:T(2,128)S(1)}, f32[2,2,4,2,8]{4,3,2,1,0:T(2,128)S(1)}, u32[]{:S(2)}, u32[]{:S(2)}) collective-permute-start(f32[2,2,4,2,8]{4,3,2,1,0:T(2,128)S(1)} %get-tuple-element.63), channel_id=1, source_target_pairs={{0,16},{1,17},{2,18},{3,19},{4,20},{5,21},{6,22},{7,23},{8,24},{9,... | collective-permute-start | bytes 3080 | tf_op jit(solution)/shard_map/ppermute | solution.py:13
  98.6 3.7 %collective-permute-start.20 = (f32[2,2,4,2,8]{4,3,2,1,0:T(2,128)S(1)}, f32[2,2,4,2,8]{4,3,2,1,0:T(2,128)S(1)}, u32[]{:S(2)}, u32[]{:S(2)}) collective-permute-start(f32[2,2,4,2,8]{4,3,2,1,0:T(2,128)S(1)} %get-tuple-element.63), channel_id=1, source_target_pairs={{0,8},{1,9},{2,10},{3,11},{4,12},{5,13},{6,14},{7,15},{8,0},{9,1},... | collective-permute-start | bytes 3080 | tf_op jit(solution)/shard_map/ppermute | solution.py:13
  102.4 4.5 %collective-permute-start.28 = (f32[4,2,2,4,2,8]{5,4,3,2,1,0:T(2,128)S(1)}, f32[4,2,2,4,2,8]{5,4,3,2,1,0:T(2,128)S(1)}, u32[]{:S(2)}, u32[]{:S(2)}) collective-permute-start(f32[4,2,2,4,2,8]{5,4,3,2,1,0:T(2,128)S(1)} %pad_maximum_fusion.5), channel_id=1, source_target_pairs={{0,1},{1,0},{2,3},{3,2},{4,5},{5,4},{6,7},{7,6},{8,9},{9,8},{10,11... | collective-permute-start | bytes 12296 | tf_op jit(solution)/shard_map/ppermute | solution.py:13
  102.5 0.8 copy-start.3
  102.5 1.0 copy-start.4
  105.0 17.0 %collective-permute-start.27 = (bf16[4,16,8,2048]{3,2,1,0:T(8,128)(2,1)S(1)}, bf16[4,16,8,2048]{3,2,1,0:T(8,128)(2,1)}, u32[]{:S(2)}, u32[]{:S(2)}) collective-permute-start(bf16[4,16,8,2048]{3,2,1,0:T(8,128)(2,1)S(1)} %pad_maximum_fusion), channel_id=1, source_target_pairs={{0,1},{1,0},{2,3},{3,2},{4,5},{5,4},{6,7},{7,6},{8,9},{9,8},{10,11... | collective-permute-start | bytes 6291464 | tf_op jit(solution)/shard_map/ppermute | solution.py:13
  108.2 15.8 %slice-start = ((s8[8388608]{0:T(1024)(128)(4,1)}), s8[4194304]{0:T(1024)(128)(4,1)S(1)}, s32[]{:S(2)}) async-start(s8[8388608]{0:T(1024)(128)(4,1)} %bitcast.160), calls=%async_computation | async-start | bytes 8388608
  108.2 15.8 %slice-start.1 = ((s8[8388608]{0:T(1024)(128)(4,1)}), s8[4194304]{0:T(1024)(128)(4,1)S(1)}, s32[]{:S(2)}) async-start(s8[8388608]{0:T(1024)(128)(4,1)} %bitcast.160), calls=%async_computation.1 | async-start | bytes 8388608
  116.2 7.8 %copy-start = (f32[2,2,16,8,2048]{4,3,2,1,0:T(8,128)}, f32[2,2,16,8,2048]{4,3,2,1,0:T(8,128)S(1)}, u32[]{:S(2)}) copy-start(f32[2,2,16,8,2048]{4,3,2,1,0:T(8,128)S(1)} %fusion.5) | copy-start | bytes 12582916
  117.9 27.2 %collective-permute-start.25 = (f16[2,8,8,2048]{3,2,1,0:T(8,128)(2,1)S(1)}, f16[2,8,8,2048]{3,2,1,0:T(8,128)(2,1)S(1)}, u32[]{:S(2)}, u32[]{:S(2)}) collective-permute-start(f16[2,8,8,2048]{3,2,1,0:T(8,128)(2,1)S(1)} %get-tuple-element.37), channel_id=1, source_target_pairs={{0,192},{32,224},{64,128},{96,160},{128,64},{160,96},{192,0},{224,... | collective-permute-start | bytes 1572872 | tf_op jit(solution)/shard_map/ppermute | solution.py:13
  120.6 24.6 %collective-permute-start.24 = (f16[2,8,8,2048]{3,2,1,0:T(8,128)(2,1)}, f16[2,8,8,2048]{3,2,1,0:T(8,128)(2,1)S(1)}, u32[]{:S(2)}, u32[]{:S(2)}) collective-permute-start(f16[2,8,8,2048]{3,2,1,0:T(8,128)(2,1)} %get-tuple-element.38), channel_id=1, source_target_pairs={{0,128},{32,160},{64,192},{96,224},{128,0},{160,32},{192,64},{224,... | collective-permute-start | bytes 1572872 | tf_op jit(solution)/shard_map/ppermute | solution.py:13
  121.3 25.1 %collective-permute-start.23 = (f16[2,8,8,2048]{3,2,1,0:T(8,128)(2,1)}, f16[2,8,8,2048]{3,2,1,0:T(8,128)(2,1)}, u32[]{:S(2)}, u32[]{:S(2)}) collective-permute-start(f16[2,8,8,2048]{3,2,1,0:T(8,128)(2,1)} %get-tuple-element.36), channel_id=1, source_target_pairs={{0,64},{32,96},{64,0},{96,32},{128,192},{160,224},{192,128},{224,1... | collective-permute-start | bytes 1572872 | tf_op jit(solution)/shard_map/ppermute | solution.py:13
  128.7 2.0 %copy-start.1 = (f32[2,2,16,8,2048]{4,3,2,1,0:T(8,128)}, f32[2,2,16,8,2048]{4,3,2,1,0:T(8,128)S(1)}, u32[]{:S(2)}) copy-start(f32[2,2,16,8,2048]{4,3,2,1,0:T(8,128)S(1)} %fusion.3) | copy-start | bytes 12582916
  132.2 34.5 %collective-permute-start.31 = (f16[2,8,8,2048]{3,2,1,0:T(8,128)(2,1)}, f16[2,8,8,2048]{3,2,1,0:T(8,128)(2,1)S(1)}, u32[]{:S(2)}, u32[]{:S(2)}) collective-permute-start(f16[2,8,8,2048]{3,2,1,0:T(8,128)(2,1)} %get-tuple-element.34), channel_id=1, source_target_pairs={{0,192},{32,224},{64,128},{96,160},{128,64},{160,96},{192,0},{224,... | collective-permute-start | bytes 1572872 | tf_op jit(solution)/shard_map/ppermute | solution.py:13
  134.9 31.7 %collective-permute-start.30 = (f16[2,8,8,2048]{3,2,1,0:T(8,128)(2,1)}, f16[2,8,8,2048]{3,2,1,0:T(8,128)(2,1)S(1)}, u32[]{:S(2)}, u32[]{:S(2)}) collective-permute-start(f16[2,8,8,2048]{3,2,1,0:T(8,128)(2,1)} %get-tuple-element.35), channel_id=1, source_target_pairs={{0,128},{32,160},{64,192},{96,224},{128,0},{160,32},{192,64},{224,... | collective-permute-start | bytes 1572872 | tf_op jit(solution)/shard_map/ppermute | solution.py:13
  145.1 22.4 %collective-permute-start.29 = (f16[2,8,8,2048]{3,2,1,0:T(8,128)(2,1)S(1)}, f16[2,8,8,2048]{3,2,1,0:T(8,128)(2,1)S(1)}, u32[]{:S(2)}, u32[]{:S(2)}) collective-permute-start(f16[2,8,8,2048]{3,2,1,0:T(8,128)(2,1)S(1)} %get-tuple-element.33), channel_id=1, source_target_pairs={{0,64},{32,96},{64,0},{96,32},{128,192},{160,224},{192,128},{224,1... | collective-permute-start | bytes 1572872 | tf_op jit(solution)/shard_map/ppermute | solution.py:13
  148.4 25.1 %collective-permute-start.26 = (f16[8,8,2048]{2,1,0:T(8,128)(2,1)}, f16[8,8,2048]{2,1,0:T(8,128)(2,1)S(1)}, u32[]{:S(2)}, u32[]{:S(2)}) collective-permute-start(f16[8,8,2048]{2,1,0:T(8,128)(2,1)} %fusion.24), channel_id=1, source_target_pairs={{0,32},{32,0},{64,96},{96,64},{128,160},{160,128},{192,224},{224,1... | collective-permute-start | bytes 786440 | tf_op jit(solution)/shard_map/ppermute | solution.py:13
  168.8 16.5 %collective-permute-start.32 = (f16[8,8,2048]{2,1,0:T(8,128)(2,1)S(1)}, f16[8,8,2048]{2,1,0:T(8,128)(2,1)S(1)}, u32[]{:S(2)}, u32[]{:S(2)}) collective-permute-start(f16[8,8,2048]{2,1,0:T(8,128)(2,1)S(1)} %fusion.19), channel_id=1, source_target_pairs={{0,32},{32,0},{64,96},{96,64},{128,160},{160,128},{192,224},{224,1... | collective-permute-start | bytes 786440 | tf_op jit(solution)/shard_map/ppermute | solution.py:13
  186.6 1.0 copy-start.2

commit v5 on v3

--- a/solution.py
+++ b/solution.py
@@ -77,6 +77,8 @@
     parts = [mine] + [swap(mine, "samp", 2 * bits) for bits in (1, 2, 3)]
     facts, parts[1] = after(facts, parts[1])
     facts_z = [facts] + [swap(facts, "samp", 2 * bits) for bits in (1, 2, 3)]
+    shrink_first = 4.0 / jnp.maximum(jnp.max(span[:samples]), 1e-30)
+    facts_z[1], shrink_first = after(facts_z[1], shrink_first)
     facts = jnp.stack([pick(my_z ^ own_z[p], [f[:, p] for f in facts_z]) for p in range(2)], 1)
     line = jnp.stack([pick(my_z ^ place, parts) for place in range(4)], 1)
     line = (line.astype(F32) - facts[0][..., None]).astype(BF16)
@@ -88,10 +90,10 @@
     far = swap(near, "samp", 1)
 
     first_anom = (first_plane.astype(F32) - first_mean[:, None]).astype(BF16)
-    shrink_first = 4.0 / jnp.maximum(jnp.max(span[:samples]), 1e-30)
     grow_first = 1.0 / shrink_first
-    results = []
-    for anom in (near, far):
+    give, keep = (1 - my_zh) ^ (my_x & 1), my_zh ^ (my_x & 1)
+    out = jnp.zeros((2, 8, 8, samples), F32)
+    for place, anom in ((my_core, near), (1 - my_core, far)):
         shrink_panel = 1.0 / jnp.maximum(jnp.max(anom[:, tiles, 0, :128].astype(F32)), 1e-30)
         grow_panel = 1.0 / shrink_panel
         shares = lax.dot_general(
@@ -101,27 +103,35 @@
             preferred_element_type=F32,
         ).reshape(2, 2, tiles + 1, 8, samples)
 
-        def for_y(dest):
-            start = ((dest & 1) ^ (my_x >> 1), 0, 8 * (dest >> 1), 0, 0)
-            block = lax.dynamic_slice(shares, start, (1, 2, 8, 8, samples))
-            return block.reshape(2, 8, 8, samples)
+        def block(dest, low, lows):
+            start = ((dest & 1) ^ (my_x >> 1), low, 8 * (dest >> 1), 0, 0)
+            return lax.dynamic_slice(shares, start, (1, lows, 8, 8, samples))[0]
 
-        blocks = [for_y(my_y)]
-        for bits in (1, 2, 3):
-            sent = (for_y(my_y ^ bits) * shrink_first * shrink_panel).astype(WIRE)
-            blocks.append(swap(sent, "mem", 2 * bits))
+        def over_y(low, lows):
+            parts = [block(my_y, low, lows)]
+            for bits in (1, 2, 3):
+                sent = block(my_y ^ bits, low, lows) * shrink_first * shrink_panel
+                parts.append(swap(sent.astype(WIRE), "mem", 2 * bits))
+            return parts
 
-        def for_z(dest):
-            part = lambda v: lax.dynamic_index_in_dim(v, dest ^ (my_x & 1), 0, keepdims=False)
-            total = part(blocks[0])
-            for value in blocks[1:]:
-                total += part(value).astype(F32) * grow_panel * grow_first
-            return total
+        def total(parts):
+            result = parts[0]
+            for value in parts[1:]:
+                result += value.astype(F32) * grow_panel * grow_first
+            return result
 
-        other = (for_z(1 - my_zh) * shrink_first * shrink_panel).astype(WIRE)
-        total = for_z(my_zh) + swap(other, "mem", 1).astype(F32) * grow_panel * grow_first
-        results.append(total / (members - 1))
-    return jnp.stack([pick(my_core ^ core, results) for core in range(2)]).reshape(-1, samples)
+        if anom is far:
+            given, kept = [[v[0] for v in over_y(low, 1)] for low in (give, keep)]
+        else:
+            both = over_y(0, 2)
+            given, kept = [
+                [lax.dynamic_index_in_dim(v, low, 0, keepdims=False) for v in both]
+                for low in (give, keep)
+            ]
+        given = (total(given) * shrink_first * shrink_panel).astype(WIRE)
+        result = total(kept + [swap(given, "mem", 1)]) / (members - 1)
+        out = lax.dynamic_update_index_in_dim(out, result, place, 0)
+    return out.reshape(-1, samples)
 
 
 def solution(mesh):

time: 183 us -> 178 us (0.973)
  the two profiles are of different devices: /device:TPU:32 before, /device:TPU:1 now
where the time goes in v5:
time: 178 us
  waiting for transfers between devices  73.8 us (41%)
  starting transfers between devices  48.7 us (27%)
  other arithmetic  24.8 us (14%)
  matrix products  18.4 us (10%)
  between operations  6.82 us (4%)
  local copies, waits for them, and re-layouts  5.4 us (3%)
    ppermute x32, waiting for transfers between devices, swap(): return lax.ppermute(value, axis, [(i, i ^ bits) for i in range(size)])  73.8 us
    ppermute x32, starting transfers between devices, swap(): return lax.ppermute(value, axis, [(i, i ^ bits) for i in range(size)])  48.7 us
    dot_general x2, matrix products, per_device(): lax.dot_general(anom.reshape(-1, shard), first_anom, (((1,), (1,)), ((),...  18.4 us
    reduce_sum x2, other arithmetic, row_stats(): return jnp.stack([jnp.sum(wide, -1), jnp.max(wide, -1), jnp.max(-wide, -1)])  6.28 us
    reduce_max x3, other arithmetic, row_stats(): return jnp.stack([jnp.sum(wide, -1), jnp.max(wide, -1), jnp.max(-wide, -1)])  4.75 us
    convert_element_type x2, other arithmetic, over_y(): parts.append(swap(sent.astype(WIRE), 'mem', 2 * bits))  4 us
  transfers between devices with their start and end apart: 32, of which 16 were waited for; matrix products, arithmetic and copies ran while one was open for 23% of the time, Pallas kernels for 0%

profile of v5, /device:TPU:1, one launch (start us, length us, event | category | flops | bytes accessed | tf_op | source)
XLA Modules:
  0.0 177.9 jit_solution(2048858200454779166)
XLA Ops:
  0.0 2.5 %dynamic-slice_bitcast_fusion = (bf16[128,2048]{1,0:T(8,128)(2,1)S(1)}, bf16[128,2048]{1,0:T(8,128)(2,1)S(1)}, bf16[128,2048]{1,0:T(8,128)(2,1)}, bf16[128,2048]{1,0:T(8,128)(2,1)S(1)}) fusion(bf16[4,128,2048]{2,1,0:T(8,128)(2,1)} %bitcast.168, s32[]{:T(128)S(6)} %select_n.331, s32[]{:T(128)S(6)} %select_n.330, s32[]{:T(128)S(6)} %select_n.329, s32[]{:T(128)S(6)} %select_n.328), kind=kLoop, calls=%fused_computation.63 | loop fusion | bytes 4194320 | tf_op jit(solution)/shard_map/jit(dynamic_index_in_dim)/squeeze | solution.py:49
  2.5 2.0 %collective-permute-start = (bf16[128,2048]{1,0:T(8,128)(2,1)}, bf16[128,2048]{1,0:T(8,128)(2,1)S(1)}, u32[]{:S(2)}, u32[]{:S(2)}) collective-permute-start(bf16[128,2048]{1,0:T(8,128)(2,1)} %get-tuple-element.58), channel_id=1, source_target_pairs={{0,8},{1,9},{2,10},{3,11},{4,12},{5,13},{6,14},{7,15},{8,0},{9,1},... | collective-permute-start | bytes 1572872 | tf_op jit(solution)/shard_map/ppermute | solution.py:13
  4.5 2.5 %collective-permute-start.1 = (bf16[128,2048]{1,0:T(8,128)(2,1)S(1)}, bf16[128,2048]{1,0:T(8,128)(2,1)S(1)}, u32[]{:S(2)}, u32[]{:S(2)}) collective-permute-start(bf16[128,2048]{1,0:T(8,128)(2,1)S(1)} %get-tuple-element.57), channel_id=1, source_target_pairs={{0,16},{1,17},{2,18},{3,19},{4,20},{5,21},{6,22},{7,23},{8,24},{9,... | collective-permute-start | bytes 1572872 | tf_op jit(solution)/shard_map/ppermute | solution.py:13
  7.0 6.0 %convert_reduce_fusion = (f32[2048]{0:T(1024)S(1)}, f32[2048]{0:T(1024)S(1)}) fusion(bf16[2048,2048]{1,0:T(8,128)(2,1)} %param.3), kind=kLoop, calls=%fused_computation.2 | loop fusion | flops 16773120 | bytes 8404992 | tf_op jit(solution)/shard_map/reduce_sum | solution.py:25
  13.0 0.6 fusion.49
  14.8 4.6 %reduce_max.96 = bf16[2048]{0:T(1024)(128)(2,1)S(1)} reduce(bf16[2048,2048]{1,0:T(8,128)(2,1)} %param.3, bf16[]{:T(256)} %constant.143.clone.1), dimensions={1}, to_apply=%region_1.2 | reduce | flops 4192256 | bytes 8392706 | tf_op jit(solution)/shard_map/reduce_max | solution.py:25
  19.4 10.4 %collective-permute-done.1 = bf16[128,2048]{1,0:T(8,128)(2,1)S(1)} collective-permute-done((bf16[128,2048]{1,0:T(8,128)(2,1)S(1)}, bf16[128,2048]{1,0:T(8,128)(2,1)S(1)}, u32[]{:S(2)}, u32[]{:S(2)}) %collective-permute-start.1) | collective-permute-done | bytes 524320 | tf_op jit(solution)/shard_map/ppermute | solution.py:13
  29.8 1.8 %collective-permute-done.2 = bf16[128,2048]{1,0:T(8,128)(2,1)S(1)} collective-permute-done((bf16[128,2048]{1,0:T(8,128)(2,1)S(1)}, bf16[128,2048]{1,0:T(8,128)(2,1)S(1)}, u32[]{:S(2)}, u32[]{:S(2)}) %collective-permute-start.2) | collective-permute-done | bytes 524320 | tf_op jit(solution)/shard_map/ppermute | solution.py:13
  31.8 2.2 %collective-permute-start.3 = (bf16[2,4,2,8,2048]{4,3,2,1,0:T(8,128)(2,1)S(1)}, bf16[2,4,2,8,2048]{4,3,2,1,0:T(8,128)(2,1)S(1)}, u32[]{:S(2)}, u32[]{:S(2)}) collective-permute-start(bf16[2,4,2,8,2048]{4,3,2,1,0:T(8,128)(2,1)S(1)} %pad_maximum_fusion.2), channel_id=1, source_target_pairs={{0,1},{1,0},{2,3},{3,2},{4,5},{5,4},{6,7},{7,6},{8,9},{9,8},{10,11... | collective-permute-start | bytes 1572872 | tf_op jit(solution)/shard_map/ppermute | solution.py:13
  34.1 0.7 fusion.47
  37.4 0.2 convert_reduce_fusion.1
  37.7 0.2 fusion.28
  38.1 2.8 %collective-permute-start.12 = (f32[3,2176]{1,0:T(4,128)S(1)}, f32[3,2176]{1,0:T(4,128)S(1)}, u32[]{:S(2)}, u32[]{:S(2)}) collective-permute-start(f32[3,2176]{1,0:T(4,128)S(1)} %maximum_maximum_fusion), channel_id=1, source_target_pairs={{0,192},{32,224},{64,128},{96,160},{128,64},{160,96},{192,0},{224,... | collective-permute-start | bytes 78344 | tf_op jit(solution)/shard_map/ppermute | solution.py:13
  41.0 0.3 collective-permute-start.11
  41.3 0.3 collective-permute-start.10
  41.7 4.4 %collective-permute-start.6 = (bf16[2,2,8,2048]{3,2,1,0:T(8,128)(2,1)S(1)}, bf16[2,2,8,2048]{3,2,1,0:T(8,128)(2,1)S(1)}, u32[]{:S(2)}, u32[]{:S(2)}) collective-permute-start(bf16[2,2,8,2048]{3,2,1,0:T(8,128)(2,1)S(1)} %get-tuple-element.70), channel_id=1, source_target_pairs={{0,6},{1,7},{2,4},{3,5},{4,2},{5,3},{6,0},{7,1},{8,14},{9,15},{10,... | collective-permute-start | bytes 393224 | tf_op jit(solution)/shard_map/ppermute | solution.py:13
  46.1 0.4 collective-permute-start.4
  46.6 7.3 %collective-permute-done.4 = bf16[2,2,8,2048]{3,2,1,0:T(8,128)(2,1)S(1)} collective-permute-done((bf16[2,2,8,2048]{3,2,1,0:T(8,128)(2,1)S(1)}, bf16[2,2,8,2048]{3,2,1,0:T(8,128)(2,1)S(1)}, u32[]{:S(2)}, u32[]{:S(2)}) %collective-permute-start.4) | collective-permute-done | bytes 131104 | tf_op jit(solution)/shard_map/ppermute | solution.py:13
  53.9 5.1 %collective-permute-start.13 = (f32[3,2176]{1,0:T(4,128)S(1)}, f32[3,2176]{1,0:T(4,128)S(1)}, u32[]{:S(2)}, u32[]{:S(2)}) collective-permute-start(f32[3,2176]{1,0:T(4,128)S(1)} %pad_maximum_fusion.5), channel_id=1, source_target_pairs={{0,32},{32,0},{64,96},{96,64},{128,160},{160,128},{192,224},{224,1... | collective-permute-start | bytes 78344 | tf_op jit(solution)/shard_map/ppermute | solution.py:13
  59.1 1.4 collective-permute-start.7
  60.5 0.7 collective-permute-start.8
  61.2 1.6 collective-permute-start.9
  62.9 0.6 slice_reduce_fusion
  64.5 1.1 collective-permute-done.7
  65.6 2.0 %collective-permute-start.16 = (f32[2,2,4,2,8]{4,3,2,1,0:T(2,128)S(1)}, f32[2,2,4,2,8]{4,3,2,1,0:T(2,128)S(1)}, u32[]{:S(2)}, u32[]{:S(2)}) collective-permute-start(f32[2,2,4,2,8]{4,3,2,1,0:T(2,128)S(1)} %pad_maximum_fusion.7), channel_id=1, source_target_pairs={{0,6},{1,7},{2,4},{3,5},{4,2},{5,3},{6,0},{7,1},{8,14},{9,15},{10,... | collective-permute-start | bytes 3080 | tf_op jit(solution)/shard_map/ppermute | solution.py:13
  67.6 1.6 collective-permute-start.14
  69.1 1.3 collective-permute-done.9
  70.8 4.5 %collective-permute-done.15 = f32[2,2,4,2,8]{4,3,2,1,0:T(2,128)S(1)} collective-permute-done((f32[2,2,4,2,8]{4,3,2,1,0:T(2,128)S(1)}, f32[2,2,4,2,8]{4,3,2,1,0:T(2,128)S(1)}, u32[]{:S(2)}, u32[]{:S(2)}) %collective-permute-start.15) | collective-permute-done | bytes 1056 | tf_op jit(solution)/shard_map/ppermute | solution.py:13
  75.4 0.6 fusion.42
  76.0 0.2 fusion.8
  76.9 0.3 collective-permute-start.19
  77.2 0.3 collective-permute-start.18
  77.5 2.7 %collective-permute-start.17 = (bf16[17,8,2048]{2,1,0:T(8,128)(2,1)S(1)}, bf16[17,8,2048]{2,1,0:T(8,128)(2,1)S(1)}, u32[]{:S(2)}, u32[]{:S(2)}) collective-permute-start(bf16[17,8,2048]{2,1,0:T(8,128)(2,1)S(1)} %get-tuple-element.61), channel_id=1, source_target_pairs={{0,8},{1,9},{2,10},{3,11},{4,12},{5,13},{6,14},{7,15},{8,0},{9,1},... | collective-permute-start | bytes 1671176 | tf_op jit(solution)/shard_map/ppermute | solution.py:13
  80.2 23.9 %collective-permute-done.19 = bf16[17,8,2048]{2,1,0:T(8,128)(2,1)S(1)} collective-permute-done((bf16[17,8,2048]{2,1,0:T(8,128)(2,1)S(1)}, bf16[17,8,2048]{2,1,0:T(8,128)(2,1)S(1)}, u32[]{:S(2)}, u32[]{:S(2)}) %collective-permute-start.19) | collective-permute-done | bytes 557088 | tf_op jit(solution)/shard_map/ppermute | solution.py:13
  104.1 0.3 pad_maximum_fusion
  104.4 1.8 collective-permute-start.24
  106.1 0.6 slice_reduce_fusion.2
  107.4 7.4 %fusion.5 = f32[2,2,17,8,2048]{4,3,2,1,0:T(8,128)S(1)} fusion(bf16[2,2,17,8,2048]{4,3,2,1,0:T(8,128)(2,1)S(1)} %bitcast.163, bf16[2048,2048]{1,0:T(8,128)(2,1)} %param.3, f32[2048]{0:T(1024)S(1)} %bitcast.176), kind=kOutput, calls=%fused_computation.7 | convolution fusion | flops 4575985664 | bytes 15081472 | tf_op jit(solution)/shard_map/dot_general | solution.py:99
  114.8 1.7 fusion.9
  116.6 2.4 %collective-permute-start.22 = (f16[2,8,8,2048]{3,2,1,0:T(8,128)(2,1)}, f16[2,8,8,2048]{3,2,1,0:T(8,128)(2,1)S(1)}, u32[]{:S(2)}, u32[]{:S(2)}) collective-permute-start(f16[2,8,8,2048]{3,2,1,0:T(8,128)(2,1)} %get-tuple-element.52), channel_id=1, source_target_pairs={{0,192},{32,224},{64,128},{96,160},{128,64},{160,96},{192,0},{224,... | collective-permute-start | bytes 1572872 | tf_op jit(solution)/shard_map/ppermute | solution.py:13
  119.0 0.4 collective-permute-start.21
  119.3 0.5 collective-permute-start.20
  119.8 11.0 %fusion.3 = f32[2,2,17,8,2048]{4,3,2,1,0:T(8,128)} fusion(bf16[2,2,17,8,2048]{4,3,2,1,0:T(8,128)(2,1)} %bitcast.50, bf16[2048,2048]{1,0:T(8,128)(2,1)} %param.3, f32[2048]{0:T(1024)S(1)} %bitcast.177), kind=kOutput, calls=%fused_computation.6 | convolution fusion | flops 4575985664 | bytes 15081472 | tf_op jit(solution)/shard_map/dot_general | solution.py:99
  130.9 1.3 slice_reduce_fusion.1
  132.9 2.3 %fusion.22 = (f16[1,8,8,2048]{3,2,1,0:T(8,128)(2,1)S(1)}, f16[1,8,8,2048]{3,2,1,0:T(8,128)(2,1)S(1)}, f16[1,8,8,2048]{3,2,1,0:T(8,128)(2,1)S(1)}, f16[1,8,8,2048...) fusion(f32[2,2,17,8,2048]{4,3,2,1,0:T(8,128)} %fusion.3, ...), kind=kLoop, calls=%fused_computation.67 | loop fusion | flops 2359296 | bytes 4718632 | tf_op jit(solution)/shard_map/convert_element_type | solution.py:114
  135.2 2.5 %collective-permute-start.30 = (f16[1,8,8,2048]{3,2,1,0:T(8,128)(2,1)S(1)}, f16[1,8,8,2048]{3,2,1,0:T(8,128)(2,1)S(1)}, u32[]{:S(2)}, u32[]{:S(2)}) collective-permute-start(f16[1,8,8,2048]{3,2,1,0:T(8,128)(2,1)S(1)} %get-tuple-element.46), channel_id=1, source_target_pairs={{0,192},{32,224},{64,128},{96,160},{128,64},{160,96},{192,0},{224,... | collective-permute-start | bytes 786440 | tf_op jit(solution)/shard_map/ppermute | solution.py:13
  137.7 0.3 collective-permute-start.29
  138.0 4.7 %collective-permute-done.22 = f16[2,8,8,2048]{3,2,1,0:T(8,128)(2,1)S(1)} collective-permute-done((f16[2,8,8,2048]{3,2,1,0:T(8,128)(2,1)}, f16[2,8,8,2048]{3,2,1,0:T(8,128)(2,1)S(1)}, u32[]{:S(2)}, u32[]{:S(2)}) %collective-permute-start.22) | collective-permute-done | bytes 524320 | tf_op jit(solution)/shard_map/ppermute | solution.py:13
  142.8 0.3 collective-permute-done.20
  143.1 1.4 fusion.19
  144.5 2.3 %collective-permute-start.23 = (f16[8,8,2048]{2,1,0:T(8,128)(2,1)S(1)}, f16[8,8,2048]{2,1,0:T(8,128)(2,1)S(1)}, u32[]{:S(2)}, u32[]{:S(2)}) collective-permute-start(f16[8,8,2048]{2,1,0:T(8,128)(2,1)S(1)} %fusion.19), channel_id=1, source_target_pairs={{0,32},{32,0},{64,96},{96,64},{128,160},{160,128},{192,224},{224,1... | collective-permute-start | bytes 786440 | tf_op jit(solution)/shard_map/ppermute | solution.py:13
  146.8 2.4 %collective-permute-start.27 = (f16[1,8,8,2048]{3,2,1,0:T(8,128)(2,1)S(1)}, f16[1,8,8,2048]{3,2,1,0:T(8,128)(2,1)S(1)}, u32[]{:S(2)}, u32[]{:S(2)}) collective-permute-start(f16[1,8,8,2048]{3,2,1,0:T(8,128)(2,1)S(1)} %get-tuple-element.49), channel_id=1, source_target_pairs={{0,192},{32,224},{64,128},{96,160},{128,64},{160,96},{192,0},{224,... | collective-permute-start | bytes 786440 | tf_op jit(solution)/shard_map/ppermute | solution.py:13
  149.2 4.7 %collective-permute-done.30 = f16[1,8,8,2048]{3,2,1,0:T(8,128)(2,1)S(1)} collective-permute-done((f16[1,8,8,2048]{3,2,1,0:T(8,128)(2,1)S(1)}, f16[1,8,8,2048]{3,2,1,0:T(8,128)(2,1)S(1)}, u32[]{:S(2)}, u32[]{:S(2)}) %collective-permute-start.30) | collective-permute-done | bytes 262176 | tf_op jit(solution)/shard_map/ppermute | solution.py:13
  153.9 1.4 collective-permute-start.26
  155.3 1.6 collective-permute-start.25
  156.9 1.3 fusion.14
  158.3 2.3 %collective-permute-start.31 = (f16[8,8,2048]{2,1,0:T(8,128)(2,1)S(1)}, f16[8,8,2048]{2,1,0:T(8,128)(2,1)S(1)}, u32[]{:S(2)}, u32[]{:S(2)}) collective-permute-start(f16[8,8,2048]{2,1,0:T(8,128)(2,1)S(1)} %fusion.14), channel_id=1, source_target_pairs={{0,32},{32,0},{64,96},{96,64},{128,160},{160,128},{192,224},{224,1... | collective-permute-start | bytes 786440 | tf_op jit(solution)/shard_map/ppermute | solution.py:13
  160.6 1.1 collective-permute-done.23
  161.8 1.4 bitcast_dynamic-update-slice_fusion.1
  163.2 1.5 collective-permute-done.27
  164.7 2.9 %collective-permute-done.25 = f16[1,8,8,2048]{3,2,1,0:T(8,128)(2,1)S(1)} collective-permute-done((f16[1,8,8,2048]{3,2,1,0:T(8,128)(2,1)S(1)}, f16[1,8,8,2048]{3,2,1,0:T(8,128)(2,1)S(1)}, u32[]{:S(2)}, u32[]{:S(2)}) %collective-permute-start.25) | collective-permute-done | bytes 262176 | tf_op jit(solution)/shard_map/ppermute | solution.py:13
  167.7 7.9 %collective-permute-done.31 = f16[8,8,2048]{2,1,0:T(8,128)(2,1)S(1)} collective-permute-done((f16[8,8,2048]{2,1,0:T(8,128)(2,1)S(1)}, f16[8,8,2048]{2,1,0:T(8,128)(2,1)S(1)}, u32[]{:S(2)}, u32[]{:S(2)}) %collective-permute-start.31) | collective-permute-done | bytes 262176 | tf_op jit(solution)/shard_map/ppermute | solution.py:13
  175.5 1.4 bitcast_dynamic-update-slice_fusion
  176.9 1.0 copy-done.1
  (59 shorter events, 1.6 us)
Async XLA Ops:
  2.5 10.5 %copy-start.2 = (s32[2]{0:T(128)S(1)}, s32[2]{0:T(128)}, u32[]{:S(2)}) copy-start(s32[2]{0:T(128)} %param.5) | copy-start | bytes 28
  2.5 16.9 %collective-permute-start = (bf16[128,2048]{1,0:T(8,128)(2,1)}, bf16[128,2048]{1,0:T(8,128)(2,1)S(1)}, u32[]{:S(2)}, u32[]{:S(2)}) collective-permute-start(bf16[128,2048]{1,0:T(8,128)(2,1)} %get-tuple-element.58), channel_id=1, source_target_pairs={{0,8},{1,9},{2,10},{3,11},{4,12},{5,13},{6,14},{7,15},{8,0},{9,1},... | collective-permute-start | bytes 1572872 | tf_op jit(solution)/shard_map/ppermute | solution.py:13
  4.5 25.3 %collective-permute-start.1 = (bf16[128,2048]{1,0:T(8,128)(2,1)S(1)}, bf16[128,2048]{1,0:T(8,128)(2,1)S(1)}, u32[]{:S(2)}, u32[]{:S(2)}) collective-permute-start(bf16[128,2048]{1,0:T(8,128)(2,1)S(1)} %get-tuple-element.57), channel_id=1, source_target_pairs={{0,16},{1,17},{2,18},{3,19},{4,20},{5,21},{6,22},{7,23},{8,24},{9,... | collective-permute-start | bytes 1572872 | tf_op jit(solution)/shard_map/ppermute | solution.py:13
  7.0 24.6 %collective-permute-start.2 = (bf16[128,2048]{1,0:T(8,128)(2,1)S(1)}, bf16[128,2048]{1,0:T(8,128)(2,1)S(1)}, u32[]{:S(2)}, u32[]{:S(2)}) collective-permute-start(bf16[128,2048]{1,0:T(8,128)(2,1)S(1)} %get-tuple-element.56), channel_id=1, source_target_pairs={{0,24},{1,25},{2,26},{3,27},{4,28},{5,29},{6,30},{7,31},{8,16},{9,... | collective-permute-start | bytes 1572872 | tf_op jit(solution)/shard_map/ppermute | solution.py:13
  31.8 5.5 %collective-permute-start.3 = (bf16[2,4,2,8,2048]{4,3,2,1,0:T(8,128)(2,1)S(1)}, bf16[2,4,2,8,2048]{4,3,2,1,0:T(8,128)(2,1)S(1)}, u32[]{:S(2)}, u32[]{:S(2)}) collective-permute-start(bf16[2,4,2,8,2048]{4,3,2,1,0:T(8,128)(2,1)S(1)} %pad_maximum_fusion.2), channel_id=1, source_target_pairs={{0,1},{1,0},{2,3},{3,2},{4,5},{5,4},{6,7},{7,6},{8,9},{9,8},{10,11... | collective-permute-start | bytes 1572872 | tf_op jit(solution)/shard_map/ppermute | solution.py:13
  38.1 8.0 %collective-permute-start.12 = (f32[3,2176]{1,0:T(4,128)S(1)}, f32[3,2176]{1,0:T(4,128)S(1)}, u32[]{:S(2)}, u32[]{:S(2)}) collective-permute-start(f32[3,2176]{1,0:T(4,128)S(1)} %maximum_maximum_fusion), channel_id=1, source_target_pairs={{0,192},{32,224},{64,128},{96,160},{128,64},{160,96},{192,0},{224,... | collective-permute-start | bytes 78344 | tf_op jit(solution)/shard_map/ppermute | solution.py:13
  41.0 5.5 %collective-permute-start.11 = (f32[3,2176]{1,0:T(4,128)S(1)}, f32[3,2176]{1,0:T(4,128)S(1)}, u32[]{:S(2)}, u32[]{:S(2)}) collective-permute-start(f32[3,2176]{1,0:T(4,128)S(1)} %maximum_maximum_fusion), channel_id=1, source_target_pairs={{0,128},{32,160},{64,192},{96,224},{128,0},{160,32},{192,64},{224,... | collective-permute-start | bytes 78344 | tf_op jit(solution)/shard_map/ppermute | solution.py:13
  41.3 5.2 %collective-permute-start.10 = (f32[3,2176]{1,0:T(4,128)S(1)}, f32[3,2176]{1,0:T(4,128)S(1)}, u32[]{:S(2)}, u32[]{:S(2)}) collective-permute-start(f32[3,2176]{1,0:T(4,128)S(1)} %maximum_maximum_fusion), channel_id=1, source_target_pairs={{0,64},{32,96},{64,0},{96,32},{128,192},{160,224},{192,128},{224,1... | collective-permute-start | bytes 78344 | tf_op jit(solution)/shard_map/ppermute | solution.py:13
  41.7 17.4 %collective-permute-start.6 = (bf16[2,2,8,2048]{3,2,1,0:T(8,128)(2,1)S(1)}, bf16[2,2,8,2048]{3,2,1,0:T(8,128)(2,1)S(1)}, u32[]{:S(2)}, u32[]{:S(2)}) collective-permute-start(bf16[2,2,8,2048]{3,2,1,0:T(8,128)(2,1)S(1)} %get-tuple-element.70), channel_id=1, source_target_pairs={{0,6},{1,7},{2,4},{3,5},{4,2},{5,3},{6,0},{7,1},{8,14},{9,15},{10,... | collective-permute-start | bytes 393224 | tf_op jit(solution)/shard_map/ppermute | solution.py:13
  46.1 12.9 %collective-permute-start.5 = (bf16[2,2,8,2048]{3,2,1,0:T(8,128)(2,1)S(1)}, bf16[2,2,8,2048]{3,2,1,0:T(8,128)(2,1)S(1)}, u32[]{:S(2)}, u32[]{:S(2)}) collective-permute-start(bf16[2,2,8,2048]{3,2,1,0:T(8,128)(2,1)S(1)} %get-tuple-element.69), channel_id=1, source_target_pairs={{0,4},{1,5},{2,6},{3,7},{4,0},{5,1},{6,2},{7,3},{8,12},{9,13},{10,... | collective-permute-start | bytes 393224 | tf_op jit(solution)/shard_map/ppermute | solution.py:13
  46.1 7.8 %collective-permute-start.4 = (bf16[2,2,8,2048]{3,2,1,0:T(8,128)(2,1)S(1)}, bf16[2,2,8,2048]{3,2,1,0:T(8,128)(2,1)S(1)}, u32[]{:S(2)}, u32[]{:S(2)}) collective-permute-start(bf16[2,2,8,2048]{3,2,1,0:T(8,128)(2,1)S(1)} %get-tuple-element.67), channel_id=1, source_target_pairs={{0,2},{1,3},{2,0},{3,1},{4,6},{5,7},{6,4},{7,5},{8,10},{9,11},{10,... | collective-permute-start | bytes 393224 | tf_op jit(solution)/shard_map/ppermute | solution.py:13
  53.9 8.9 %collective-permute-start.13 = (f32[3,2176]{1,0:T(4,128)S(1)}, f32[3,2176]{1,0:T(4,128)S(1)}, u32[]{:S(2)}, u32[]{:S(2)}) collective-permute-start(f32[3,2176]{1,0:T(4,128)S(1)} %pad_maximum_fusion.5), channel_id=1, source_target_pairs={{0,32},{32,0},{64,96},{96,64},{128,160},{160,128},{192,224},{224,1... | collective-permute-start | bytes 78344 | tf_op jit(solution)/shard_map/ppermute | solution.py:13
  59.1 6.5 %collective-permute-start.7 = (bf16[2,2,8,2048]{3,2,1,0:T(8,128)(2,1)S(1)}, bf16[2,2,8,2048]{3,2,1,0:T(8,128)(2,1)S(1)}, u32[]{:S(2)}, u32[]{:S(2)}) collective-permute-start(bf16[2,2,8,2048]{3,2,1,0:T(8,128)(2,1)S(1)} %pad_maximum_fusion.4), channel_id=1, source_target_pairs={{0,2},{1,3},{2,0},{3,1},{4,6},{5,7},{6,4},{7,5},{8,10},{9,11},{10,... | collective-permute-start | bytes 393224 | tf_op jit(solution)/shard_map/ppermute | solution.py:13
  60.5 8.6 %collective-permute-start.8 = (bf16[2,2,8,2048]{3,2,1,0:T(8,128)(2,1)S(1)}, bf16[2,2,8,2048]{3,2,1,0:T(8,128)(2,1)S(1)}, u32[]{:S(2)}, u32[]{:S(2)}) collective-permute-start(bf16[2,2,8,2048]{3,2,1,0:T(8,128)(2,1)S(1)} %pad_maximum_fusion.4), channel_id=1, source_target_pairs={{0,4},{1,5},{2,6},{3,7},{4,0},{5,1},{6,2},{7,3},{8,12},{9,13},{10,... | collective-permute-start | bytes 393224 | tf_op jit(solution)/shard_map/ppermute | solution.py:13
  61.2 9.3 %collective-permute-start.9 = (bf16[2,2,8,2048]{3,2,1,0:T(8,128)(2,1)S(1)}, bf16[2,2,8,2048]{3,2,1,0:T(8,128)(2,1)S(1)}, u32[]{:S(2)}, u32[]{:S(2)}) collective-permute-start(bf16[2,2,8,2048]{3,2,1,0:T(8,128)(2,1)S(1)} %pad_maximum_fusion.4), channel_id=1, source_target_pairs={{0,6},{1,7},{2,4},{3,5},{4,2},{5,3},{6,0},{7,1},{8,14},{9,15},{10,... | collective-permute-start | bytes 393224 | tf_op jit(solution)/shard_map/ppermute | solution.py:13
  65.6 5.2 %collective-permute-start.16 = (f32[2,2,4,2,8]{4,3,2,1,0:T(2,128)S(1)}, f32[2,2,4,2,8]{4,3,2,1,0:T(2,128)S(1)}, u32[]{:S(2)}, u32[]{:S(2)}) collective-permute-start(f32[2,2,4,2,8]{4,3,2,1,0:T(2,128)S(1)} %pad_maximum_fusion.7), channel_id=1, source_target_pairs={{0,6},{1,7},{2,4},{3,5},{4,2},{5,3},{6,0},{7,1},{8,14},{9,15},{10,... | collective-permute-start | bytes 3080 | tf_op jit(solution)/shard_map/ppermute | solution.py:13
  67.6 7.8 %collective-permute-start.15 = (f32[2,2,4,2,8]{4,3,2,1,0:T(2,128)S(1)}, f32[2,2,4,2,8]{4,3,2,1,0:T(2,128)S(1)}, u32[]{:S(2)}, u32[]{:S(2)}) collective-permute-start(f32[2,2,4,2,8]{4,3,2,1,0:T(2,128)S(1)} %pad_maximum_fusion.7), channel_id=1, source_target_pairs={{0,4},{1,5},{2,6},{3,7},{4,0},{5,1},{6,2},{7,3},{8,12},{9,13},{10,... | collective-permute-start | bytes 3080 | tf_op jit(solution)/shard_map/ppermute | solution.py:13
  67.6 3.2 %collective-permute-start.14 = (f32[2,2,4,2,8]{4,3,2,1,0:T(2,128)S(1)}, f32[2,2,4,2,8]{4,3,2,1,0:T(2,128)S(1)}, u32[]{:S(2)}, u32[]{:S(2)}) collective-permute-start(f32[2,2,4,2,8]{4,3,2,1,0:T(2,128)S(1)} %pad_maximum_fusion.7), channel_id=1, source_target_pairs={{0,2},{1,3},{2,0},{3,1},{4,6},{5,7},{6,4},{7,5},{8,10},{9,11},{10,... | collective-permute-start | bytes 3080 | tf_op jit(solution)/shard_map/ppermute | solution.py:13
  76.9 27.2 %collective-permute-start.19 = (bf16[17,8,2048]{2,1,0:T(8,128)(2,1)S(1)}, bf16[17,8,2048]{2,1,0:T(8,128)(2,1)S(1)}, u32[]{:S(2)}, u32[]{:S(2)}) collective-permute-start(bf16[17,8,2048]{2,1,0:T(8,128)(2,1)S(1)} %get-tuple-element.61), channel_id=1, source_target_pairs={{0,24},{1,25},{2,26},{3,27},{4,28},{5,29},{6,30},{7,31},{8,16},{9,... | collective-permute-start | bytes 1671176 | tf_op jit(solution)/shard_map/ppermute | solution.py:13
  77.2 26.9 %collective-permute-start.18 = (bf16[17,8,2048]{2,1,0:T(8,128)(2,1)S(1)}, bf16[17,8,2048]{2,1,0:T(8,128)(2,1)S(1)}, u32[]{:S(2)}, u32[]{:S(2)}) collective-permute-start(bf16[17,8,2048]{2,1,0:T(8,128)(2,1)S(1)} %get-tuple-element.61), channel_id=1, source_target_pairs={{0,16},{1,17},{2,18},{3,19},{4,20},{5,21},{6,22},{7,23},{8,24},{9,... | collective-permute-start | bytes 1671176 | tf_op jit(solution)/shard_map/ppermute | solution.py:13
  77.5 26.6 %collective-permute-start.17 = (bf16[17,8,2048]{2,1,0:T(8,128)(2,1)S(1)}, bf16[17,8,2048]{2,1,0:T(8,128)(2,1)S(1)}, u32[]{:S(2)}, u32[]{:S(2)}) collective-permute-start(bf16[17,8,2048]{2,1,0:T(8,128)(2,1)S(1)} %get-tuple-element.61), channel_id=1, source_target_pairs={{0,8},{1,9},{2,10},{3,11},{4,12},{5,13},{6,14},{7,15},{8,0},{9,1},... | collective-permute-start | bytes 1671176 | tf_op jit(solution)/shard_map/ppermute | solution.py:13
  104.4 15.4 %collective-permute-start.24 = (bf16[4,17,8,2048]{3,2,1,0:T(8,128)(2,1)S(1)}, bf16[4,17,8,2048]{3,2,1,0:T(8,128)(2,1)}, u32[]{:S(2)}, u32[]{:S(2)}) collective-permute-start(bf16[4,17,8,2048]{3,2,1,0:T(8,128)(2,1)S(1)} %pad_maximum_fusion), channel_id=1, source_target_pairs={{0,1},{1,0},{2,3},{3,2},{4,5},{5,4},{6,7},{7,6},{8,9},{9,8},{10,11... | collective-permute-start | bytes 6684680 | tf_op jit(solution)/shard_map/ppermute | solution.py:13
  114.8 16.0 %copy-start = (f32[2,2,17,8,2048]{4,3,2,1,0:T(8,128)}, f32[2,2,17,8,2048]{4,3,2,1,0:T(8,128)S(1)}, u32[]{:S(2)}) copy-start(f32[2,2,17,8,2048]{4,3,2,1,0:T(8,128)S(1)} %fusion.5) | copy-start | bytes 13369348
  116.6 26.1 %collective-permute-start.22 = (f16[2,8,8,2048]{3,2,1,0:T(8,128)(2,1)}, f16[2,8,8,2048]{3,2,1,0:T(8,128)(2,1)S(1)}, u32[]{:S(2)}, u32[]{:S(2)}) collective-permute-start(f16[2,8,8,2048]{3,2,1,0:T(8,128)(2,1)} %get-tuple-element.52), channel_id=1, source_target_pairs={{0,192},{32,224},{64,128},{96,160},{128,64},{160,96},{192,0},{224,... | collective-permute-start | bytes 1572872 | tf_op jit(solution)/shard_map/ppermute | solution.py:13
  119.0 23.8 %collective-permute-start.21 = (f16[2,8,8,2048]{3,2,1,0:T(8,128)(2,1)}, f16[2,8,8,2048]{3,2,1,0:T(8,128)(2,1)S(1)}, u32[]{:S(2)}, u32[]{:S(2)}) collective-permute-start(f16[2,8,8,2048]{3,2,1,0:T(8,128)(2,1)} %get-tuple-element.53), channel_id=1, source_target_pairs={{0,128},{32,160},{64,192},{96,224},{128,0},{160,32},{192,64},{224,... | collective-permute-start | bytes 1572872 | tf_op jit(solution)/shard_map/ppermute | solution.py:13
  119.3 23.8 %collective-permute-start.20 = (f16[2,8,8,2048]{3,2,1,0:T(8,128)(2,1)}, f16[2,8,8,2048]{3,2,1,0:T(8,128)(2,1)}, u32[]{:S(2)}, u32[]{:S(2)}) collective-permute-start(f16[2,8,8,2048]{3,2,1,0:T(8,128)(2,1)} %get-tuple-element.51), channel_id=1, source_target_pairs={{0,64},{32,96},{64,0},{96,32},{128,192},{160,224},{192,128},{224,1... | collective-permute-start | bytes 1572872 | tf_op jit(solution)/shard_map/ppermute | solution.py:13
  135.2 18.8 %collective-permute-start.30 = (f16[1,8,8,2048]{3,2,1,0:T(8,128)(2,1)S(1)}, f16[1,8,8,2048]{3,2,1,0:T(8,128)(2,1)S(1)}, u32[]{:S(2)}, u32[]{:S(2)}) collective-permute-start(f16[1,8,8,2048]{3,2,1,0:T(8,128)(2,1)S(1)} %get-tuple-element.46), channel_id=1, source_target_pairs={{0,192},{32,224},{64,128},{96,160},{128,64},{160,96},{192,0},{224,... | collective-permute-start | bytes 786440 | tf_op jit(solution)/shard_map/ppermute | solution.py:13
  137.7 17.7 %collective-permute-start.29 = (f16[1,8,8,2048]{3,2,1,0:T(8,128)(2,1)S(1)}, f16[1,8,8,2048]{3,2,1,0:T(8,128)(2,1)S(1)}, u32[]{:S(2)}, u32[]{:S(2)}) collective-permute-start(f16[1,8,8,2048]{3,2,1,0:T(8,128)(2,1)S(1)} %get-tuple-element.47), channel_id=1, source_target_pairs={{0,128},{32,160},{64,192},{96,224},{128,0},{160,32},{192,64},{224,... | collective-permute-start | bytes 786440 | tf_op jit(solution)/shard_map/ppermute | solution.py:13
  142.7 14.2 %collective-permute-start.28 = (f16[1,8,8,2048]{3,2,1,0:T(8,128)(2,1)S(1)}, f16[1,8,8,2048]{3,2,1,0:T(8,128)(2,1)S(1)}, u32[]{:S(2)}, u32[]{:S(2)}) collective-permute-start(f16[1,8,8,2048]{3,2,1,0:T(8,128)(2,1)S(1)} %get-tuple-element.48), channel_id=1, source_target_pairs={{0,64},{32,96},{64,0},{96,32},{128,192},{160,224},{192,128},{224,1... | collective-permute-start | bytes 786440 | tf_op jit(solution)/shard_map/ppermute | solution.py:13
  144.5 17.2 %collective-permute-start.23 = (f16[8,8,2048]{2,1,0:T(8,128)(2,1)S(1)}, f16[8,8,2048]{2,1,0:T(8,128)(2,1)S(1)}, u32[]{:S(2)}, u32[]{:S(2)}) collective-permute-start(f16[8,8,2048]{2,1,0:T(8,128)(2,1)S(1)} %fusion.19), channel_id=1, source_target_pairs={{0,32},{32,0},{64,96},{96,64},{128,160},{160,128},{192,224},{224,1... | collective-permute-start | bytes 786440 | tf_op jit(solution)/shard_map/ppermute | solution.py:13
  146.8 17.9 %collective-permute-start.27 = (f16[1,8,8,2048]{3,2,1,0:T(8,128)(2,1)S(1)}, f16[1,8,8,2048]{3,2,1,0:T(8,128)(2,1)S(1)}, u32[]{:S(2)}, u32[]{:S(2)}) collective-permute-start(f16[1,8,8,2048]{3,2,1,0:T(8,128)(2,1)S(1)} %get-tuple-element.49), channel_id=1, source_target_pairs={{0,192},{32,224},{64,128},{96,160},{128,64},{160,96},{192,0},{224,... | collective-permute-start | bytes 786440 | tf_op jit(solution)/shard_map/ppermute | solution.py:13
  153.9 10.8 %collective-permute-start.26 = (f16[1,8,8,2048]{3,2,1,0:T(8,128)(2,1)S(1)}, f16[1,8,8,2048]{3,2,1,0:T(8,128)(2,1)S(1)}, u32[]{:S(2)}, u32[]{:S(2)}) collective-permute-start(f16[1,8,8,2048]{3,2,1,0:T(8,128)(2,1)S(1)} %get-tuple-element.50), channel_id=1, source_target_pairs={{0,128},{32,160},{64,192},{96,224},{128,0},{160,32},{192,64},{224,... | collective-permute-start | bytes 786440 | tf_op jit(solution)/shard_map/ppermute | solution.py:13
  155.3 12.3 %collective-permute-start.25 = (f16[1,8,8,2048]{3,2,1,0:T(8,128)(2,1)S(1)}, f16[1,8,8,2048]{3,2,1,0:T(8,128)(2,1)S(1)}, u32[]{:S(2)}, u32[]{:S(2)}) collective-permute-start(f16[1,8,8,2048]{3,2,1,0:T(8,128)(2,1)S(1)} %get-tuple-element.45), channel_id=1, source_target_pairs={{0,64},{32,96},{64,0},{96,32},{128,192},{160,224},{192,128},{224,1... | collective-permute-start | bytes 786440 | tf_op jit(solution)/shard_map/ppermute | solution.py:13
  158.3 17.3 %collective-permute-start.31 = (f16[8,8,2048]{2,1,0:T(8,128)(2,1)S(1)}, f16[8,8,2048]{2,1,0:T(8,128)(2,1)S(1)}, u32[]{:S(2)}, u32[]{:S(2)}) collective-permute-start(f16[8,8,2048]{2,1,0:T(8,128)(2,1)S(1)} %fusion.14), channel_id=1, source_target_pairs={{0,32},{32,0},{64,96},{96,64},{128,160},{160,128},{192,224},{224,1... | collective-permute-start | bytes 786440 | tf_op jit(solution)/shard_map/ppermute | solution.py:13
  176.9 1.0 copy-start.1

commit v6 on v5

--- a/solution.py
+++ b/solution.py
@@ -109,7 +109,7 @@
 
         def over_y(low, lows):
             parts = [block(my_y, low, lows)]
-            for bits in (1, 2, 3):
+            for bits in (2, 1, 3):
                 sent = block(my_y ^ bits, low, lows) * shrink_first * shrink_panel
                 parts.append(swap(sent.astype(WIRE), "mem", 2 * bits))
             return parts

time: 178 us -> 175 us (0.983)
  the two profiles are of different devices: /device:TPU:1 before, /device:TPU:32 now
where the time goes in v6:
time: 175 us; the launch traced here: 174 us
  waiting for transfers between devices  69.1 us (39%)
  starting transfers between devices  49.5 us (28%)
  other arithmetic  24.8 us (14%)
  matrix products  18.4 us (11%)
  between operations  6.96 us (4%)
  local copies, waits for them, and re-layouts  5.41 us (3%)
    ppermute x32, waiting for transfers between devices, swap(): return lax.ppermute(value, axis, [(i, i ^ bits) for i in range(size)])  69.1 us
    ppermute x32, starting transfers between devices, swap(): return lax.ppermute(value, axis, [(i, i ^ bits) for i in range(size)])  49.5 us
    dot_general x2, matrix products, per_device(): lax.dot_general(anom.reshape(-1, shard), first_anom, (((1,), (1,)), ((),...  18.4 us
    reduce_sum x2, other arithmetic, row_stats(): return jnp.stack([jnp.sum(wide, -1), jnp.max(wide, -1), jnp.max(-wide, -1)])  6.28 us
    reduce_max x3, other arithmetic, row_stats(): return jnp.stack([jnp.sum(wide, -1), jnp.max(wide, -1), jnp.max(-wide, -1)])  4.75 us
    convert_element_type x2, other arithmetic, over_y(): parts.append(swap(sent.astype(WIRE), 'mem', 2 * bits))  4 us
  transfers between devices with their start and end apart: 32, of which 14 were waited for; matrix products, arithmetic and copies ran while one was open for 24% of the time, Pallas kernels for 0%

profile of v6, /device:TPU:32, one launch (start us, length us, event | category | flops | bytes accessed | tf_op | source)
XLA Modules:
  0.0 174.1 jit_solution(12268130065232787336)
XLA Ops:
  0.0 2.5 %dynamic-slice_bitcast_fusion = (bf16[128,2048]{1,0:T(8,128)(2,1)S(1)}, bf16[128,2048]{1,0:T(8,128)(2,1)S(1)}, bf16[128,2048]{1,0:T(8,128)(2,1)}, bf16[128,2048]{1,0:T(8,128)(2,1)S(1)}) fusion(bf16[4,128,2048]{2,1,0:T(8,128)(2,1)} %bitcast.168, s32[]{:T(128)S(6)} %select_n.331, s32[]{:T(128)S(6)} %select_n.330, s32[]{:T(128)S(6)} %select_n.329, s32[]{:T(128)S(6)} %select_n.328), kind=kLoop, calls=%fused_computation.63 | loop fusion | bytes 4194320 | tf_op jit(solution)/shard_map/jit(dynamic_index_in_dim)/squeeze | solution.py:49
  2.5 1.5 collective-permute-start
  4.0 2.7 %collective-permute-start.1 = (bf16[128,2048]{1,0:T(8,128)(2,1)S(1)}, bf16[128,2048]{1,0:T(8,128)(2,1)S(1)}, u32[]{:S(2)}, u32[]{:S(2)}) collective-permute-start(bf16[128,2048]{1,0:T(8,128)(2,1)S(1)} %get-tuple-element.57), channel_id=1, source_target_pairs={{0,16},{1,17},{2,18},{3,19},{4,20},{5,21},{6,22},{7,23},{8,24},{9,... | collective-permute-start | bytes 1572872 | tf_op jit(solution)/shard_map/ppermute | solution.py:13
  6.7 0.5 collective-permute-start.2
  7.2 6.0 %convert_reduce_fusion = (f32[2048]{0:T(1024)S(1)}, f32[2048]{0:T(1024)S(1)}) fusion(bf16[2048,2048]{1,0:T(8,128)(2,1)} %param.3), kind=kLoop, calls=%fused_computation.2 | loop fusion | flops 16773120 | bytes 8404992 | tf_op jit(solution)/shard_map/reduce_sum | solution.py:25
  13.2 0.6 fusion.49
  15.0 4.6 %reduce_max.96 = bf16[2048]{0:T(1024)(128)(2,1)S(1)} reduce(bf16[2048,2048]{1,0:T(8,128)(2,1)} %param.3, bf16[]{:T(256)} %constant.143.clone.1), dimensions={1}, to_apply=%region_1.2 | reduce | flops 4192256 | bytes 8392706 | tf_op jit(solution)/shard_map/reduce_max | solution.py:25
  19.6 10.3 %collective-permute-done.1 = bf16[128,2048]{1,0:T(8,128)(2,1)S(1)} collective-permute-done((bf16[128,2048]{1,0:T(8,128)(2,1)S(1)}, bf16[128,2048]{1,0:T(8,128)(2,1)S(1)}, u32[]{:S(2)}, u32[]{:S(2)}) %collective-permute-start.1) | collective-permute-done | bytes 524320 | tf_op jit(solution)/shard_map/ppermute | solution.py:13
  29.9 2.4 %collective-permute-done.2 = bf16[128,2048]{1,0:T(8,128)(2,1)S(1)} collective-permute-done((bf16[128,2048]{1,0:T(8,128)(2,1)S(1)}, bf16[128,2048]{1,0:T(8,128)(2,1)S(1)}, u32[]{:S(2)}, u32[]{:S(2)}) %collective-permute-start.2) | collective-permute-done | bytes 524320 | tf_op jit(solution)/shard_map/ppermute | solution.py:13
  32.3 0.1 select_select_fusion.1
  32.6 0.7 fusion.47
  35.9 0.2 convert_reduce_fusion.1
  36.2 0.2 fusion.28
  36.4 0.1 reshape.317
  36.7 3.1 %collective-permute-start.12 = (f32[3,2176]{1,0:T(4,128)S(1)}, f32[3,2176]{1,0:T(4,128)S(1)}, u32[]{:S(2)}, u32[]{:S(2)}) collective-permute-start(f32[3,2176]{1,0:T(4,128)S(1)} %maximum_maximum_fusion), channel_id=1, source_target_pairs={{0,192},{32,224},{64,128},{96,160},{128,64},{160,96},{192,0},{224,... | collective-permute-start | bytes 78344 | tf_op jit(solution)/shard_map/ppermute | solution.py:13
  39.8 0.6 collective-permute-start.11
  40.4 0.5 collective-permute-start.10
  40.9 2.0 %collective-permute-start.6 = (bf16[2,2,8,2048]{3,2,1,0:T(8,128)(2,1)S(1)}, bf16[2,2,8,2048]{3,2,1,0:T(8,128)(2,1)S(1)}, u32[]{:S(2)}, u32[]{:S(2)}) collective-permute-start(bf16[2,2,8,2048]{3,2,1,0:T(8,128)(2,1)S(1)} %get-tuple-element.70), channel_id=1, source_target_pairs={{0,6},{1,7},{2,4},{3,5},{4,2},{5,3},{6,0},{7,1},{8,14},{9,15},{10,... | collective-permute-start | bytes 393224 | tf_op jit(solution)/shard_map/ppermute | solution.py:13
  42.9 1.5 collective-permute-start.5
  44.4 1.4 collective-permute-start.4
  45.8 8.7 %collective-permute-done.4 = bf16[2,2,8,2048]{3,2,1,0:T(8,128)(2,1)S(1)} collective-permute-done((bf16[2,2,8,2048]{3,2,1,0:T(8,128)(2,1)S(1)}, bf16[2,2,8,2048]{3,2,1,0:T(8,128)(2,1)S(1)}, u32[]{:S(2)}, u32[]{:S(2)}) %collective-permute-start.4) | collective-permute-done | bytes 131104 | tf_op jit(solution)/shard_map/ppermute | solution.py:13
  54.5 4.5 %collective-permute-start.13 = (f32[3,2176]{1,0:T(4,128)S(1)}, f32[3,2176]{1,0:T(4,128)S(1)}, u32[]{:S(2)}, u32[]{:S(2)}) collective-permute-start(f32[3,2176]{1,0:T(4,128)S(1)} %pad_maximum_fusion.5), channel_id=1, source_target_pairs={{0,32},{32,0},{64,96},{96,64},{128,160},{160,128},{192,224},{224,1... | collective-permute-start | bytes 78344 | tf_op jit(solution)/shard_map/ppermute | solution.py:13
  59.2 2.5 %collective-permute-start.8 = (bf16[2,2,8,2048]{3,2,1,0:T(8,128)(2,1)S(1)}, bf16[2,2,8,2048]{3,2,1,0:T(8,128)(2,1)S(1)}, u32[]{:S(2)}, u32[]{:S(2)}) collective-permute-start(bf16[2,2,8,2048]{3,2,1,0:T(8,128)(2,1)S(1)} %pad_maximum_fusion.4), channel_id=1, source_target_pairs={{0,4},{1,5},{2,6},{3,7},{4,0},{5,1},{6,2},{7,3},{8,12},{9,13},{10,... | collective-permute-start | bytes 393224 | tf_op jit(solution)/shard_map/ppermute | solution.py:13
  61.7 1.0 collective-permute-start.9
  62.8 0.6 slice_reduce_fusion
  64.4 1.2 collective-permute-done.7
  65.6 1.0 collective-permute-start.16
  66.6 2.2 %collective-permute-start.15 = (f32[2,2,4,2,8]{4,3,2,1,0:T(2,128)S(1)}, f32[2,2,4,2,8]{4,3,2,1,0:T(2,128)S(1)}, u32[]{:S(2)}, u32[]{:S(2)}) collective-permute-start(f32[2,2,4,2,8]{4,3,2,1,0:T(2,128)S(1)} %pad_maximum_fusion.7), channel_id=1, source_target_pairs={{0,4},{1,5},{2,6},{3,7},{4,0},{5,1},{6,2},{7,3},{8,12},{9,13},{10,... | collective-permute-start | bytes 3080 | tf_op jit(solution)/shard_map/ppermute | solution.py:13
  68.8 0.3 collective-permute-start.14
  69.1 2.0 %collective-permute-done.8 = bf16[2,2,8,2048]{3,2,1,0:T(8,128)(2,1)S(1)} collective-permute-done((bf16[2,2,8,2048]{3,2,1,0:T(8,128)(2,1)S(1)}, bf16[2,2,8,2048]{3,2,1,0:T(8,128)(2,1)S(1)}, u32[]{:S(2)}, u32[]{:S(2)}) %collective-permute-start.8) | collective-permute-done | bytes 131104 | tf_op jit(solution)/shard_map/ppermute | solution.py:13
  71.1 3.2 %collective-permute-done.9 = bf16[2,2,8,2048]{3,2,1,0:T(8,128)(2,1)S(1)} collective-permute-done((bf16[2,2,8,2048]{3,2,1,0:T(8,128)(2,1)S(1)}, bf16[2,2,8,2048]{3,2,1,0:T(8,128)(2,1)S(1)}, u32[]{:S(2)}, u32[]{:S(2)}) %collective-permute-start.9) | collective-permute-done | bytes 131104 | tf_op jit(solution)/shard_map/ppermute | solution.py:13
  74.5 0.6 fusion.42
  75.2 0.2 fusion.8
  76.1 0.6 collective-permute-start.19
  76.6 0.6 collective-permute-start.18
  77.2 3.0 %collective-permute-start.17 = (bf16[17,8,2048]{2,1,0:T(8,128)(2,1)S(1)}, bf16[17,8,2048]{2,1,0:T(8,128)(2,1)S(1)}, u32[]{:S(2)}, u32[]{:S(2)}) collective-permute-start(bf16[17,8,2048]{2,1,0:T(8,128)(2,1)S(1)} %get-tuple-element.61), channel_id=1, source_target_pairs={{0,8},{1,9},{2,10},{3,11},{4,12},{5,13},{6,14},{7,15},{8,0},{9,1},... | collective-permute-start | bytes 1671176 | tf_op jit(solution)/shard_map/ppermute | solution.py:13
  80.2 22.0 %collective-permute-done.19 = bf16[17,8,2048]{2,1,0:T(8,128)(2,1)S(1)} collective-permute-done((bf16[17,8,2048]{2,1,0:T(8,128)(2,1)S(1)}, bf16[17,8,2048]{2,1,0:T(8,128)(2,1)S(1)}, u32[]{:S(2)}, u32[]{:S(2)}) %collective-permute-start.19) | collective-permute-done | bytes 557088 | tf_op jit(solution)/shard_map/ppermute | solution.py:13
  102.2 0.6 collective-permute-done.17
  102.9 0.3 pad_maximum_fusion
  103.3 0.6 slice_reduce_fusion.2
  104.6 7.4 %fusion.5 = f32[2,2,17,8,2048]{4,3,2,1,0:T(8,128)S(1)} fusion(bf16[2,2,17,8,2048]{4,3,2,1,0:T(8,128)(2,1)S(1)} %bitcast.163, bf16[2048,2048]{1,0:T(8,128)(2,1)} %param.3, f32[2048]{0:T(1024)S(1)} %bitcast.176), kind=kOutput, calls=%fused_computation.7 | convolution fusion | flops 4575985664 | bytes 15081472 | tf_op jit(solution)/shard_map/dot_general | solution.py:99
  112.0 1.7 fusion.9
  113.7 2.5 %collective-permute-start.22 = (f16[2,8,8,2048]{3,2,1,0:T(8,128)(2,1)}, f16[2,8,8,2048]{3,2,1,0:T(8,128)(2,1)S(1)}, u32[]{:S(2)}, u32[]{:S(2)}) collective-permute-start(f16[2,8,8,2048]{3,2,1,0:T(8,128)(2,1)} %get-tuple-element.52), channel_id=1, source_target_pairs={{0,192},{32,224},{64,128},{96,160},{128,64},{160,96},{192,0},{224,... | collective-permute-start | bytes 1572872 | tf_op jit(solution)/shard_map/ppermute | solution.py:13
  116.2 0.1 collective-permute-start.21
  116.4 2.1 %collective-permute-start.20 = (f16[2,8,8,2048]{3,2,1,0:T(8,128)(2,1)}, f16[2,8,8,2048]{3,2,1,0:T(8,128)(2,1)}, u32[]{:S(2)}, u32[]{:S(2)}) collective-permute-start(f16[2,8,8,2048]{3,2,1,0:T(8,128)(2,1)} %get-tuple-element.51), channel_id=1, source_target_pairs={{0,128},{32,160},{64,192},{96,224},{128,0},{160,32},{192,64},{224,... | collective-permute-start | bytes 1572872 | tf_op jit(solution)/shard_map/ppermute | solution.py:13
  118.4 11.0 %fusion.3 = f32[2,2,17,8,2048]{4,3,2,1,0:T(8,128)} fusion(bf16[2,2,17,8,2048]{4,3,2,1,0:T(8,128)(2,1)} %bitcast.50, bf16[2048,2048]{1,0:T(8,128)(2,1)} %param.3, f32[2048]{0:T(1024)S(1)} %bitcast.177), kind=kOutput, calls=%fused_computation.6 | convolution fusion | flops 4575985664 | bytes 15081472 | tf_op jit(solution)/shard_map/dot_general | solution.py:99
  129.5 1.3 slice_reduce_fusion.1
  131.5 2.3 %fusion.22 = (f16[1,8,8,2048]{3,2,1,0:T(8,128)(2,1)S(1)}, f16[1,8,8,2048]{3,2,1,0:T(8,128)(2,1)S(1)}, f16[1,8,8,2048]{3,2,1,0:T(8,128)(2,1)S(1)}, f16[1,8,8,2048...) fusion(f32[2,2,17,8,2048]{4,3,2,1,0:T(8,128)} %fusion.3, ...), kind=kLoop, calls=%fused_computation.67 | loop fusion | flops 2359296 | bytes 4718632 | tf_op jit(solution)/shard_map/convert_element_type | solution.py:114
  133.8 2.6 %collective-permute-start.30 = (f16[1,8,8,2048]{3,2,1,0:T(8,128)(2,1)S(1)}, f16[1,8,8,2048]{3,2,1,0:T(8,128)(2,1)S(1)}, u32[]{:S(2)}, u32[]{:S(2)}) collective-permute-start(f16[1,8,8,2048]{3,2,1,0:T(8,128)(2,1)S(1)} %get-tuple-element.46), channel_id=1, source_target_pairs={{0,192},{32,224},{64,128},{96,160},{128,64},{160,96},{192,0},{224,... | collective-permute-start | bytes 786440 | tf_op jit(solution)/shard_map/ppermute | solution.py:13
  136.3 2.2 %collective-permute-start.28 = (f16[1,8,8,2048]{3,2,1,0:T(8,128)(2,1)S(1)}, f16[1,8,8,2048]{3,2,1,0:T(8,128)(2,1)S(1)}, u32[]{:S(2)}, u32[]{:S(2)}) collective-permute-start(f16[1,8,8,2048]{3,2,1,0:T(8,128)(2,1)S(1)} %get-tuple-element.48), channel_id=1, source_target_pairs={{0,128},{32,160},{64,192},{96,224},{128,0},{160,32},{192,64},{224,... | collective-permute-start | bytes 786440 | tf_op jit(solution)/shard_map/ppermute | solution.py:13
  138.6 4.2 %collective-permute-done.20 = f16[2,8,8,2048]{3,2,1,0:T(8,128)(2,1)} collective-permute-done((f16[2,8,8,2048]{3,2,1,0:T(8,128)(2,1)}, f16[2,8,8,2048]{3,2,1,0:T(8,128)(2,1)}, u32[]{:S(2)}, u32[]{:S(2)}) %collective-permute-start.20) | collective-permute-done | bytes 524320 | tf_op jit(solution)/shard_map/ppermute | solution.py:13
  142.8 1.4 fusion.19
  144.1 2.6 %collective-permute-start.23 = (f16[8,8,2048]{2,1,0:T(8,128)(2,1)S(1)}, f16[8,8,2048]{2,1,0:T(8,128)(2,1)S(1)}, u32[]{:S(2)}, u32[]{:S(2)}) collective-permute-start(f16[8,8,2048]{2,1,0:T(8,128)(2,1)S(1)} %fusion.19), channel_id=1, source_target_pairs={{0,32},{32,0},{64,96},{96,64},{128,160},{160,128},{192,224},{224,1... | collective-permute-start | bytes 786440 | tf_op jit(solution)/shard_map/ppermute | solution.py:13
  146.7 2.7 %collective-permute-start.27 = (f16[1,8,8,2048]{3,2,1,0:T(8,128)(2,1)S(1)}, f16[1,8,8,2048]{3,2,1,0:T(8,128)(2,1)S(1)}, u32[]{:S(2)}, u32[]{:S(2)}) collective-permute-start(f16[1,8,8,2048]{3,2,1,0:T(8,128)(2,1)S(1)} %get-tuple-element.49), channel_id=1, source_target_pairs={{0,192},{32,224},{64,128},{96,160},{128,64},{160,96},{192,0},{224,... | collective-permute-start | bytes 786440 | tf_op jit(solution)/shard_map/ppermute | solution.py:13
  149.4 2.7 %collective-permute-start.25 = (f16[1,8,8,2048]{3,2,1,0:T(8,128)(2,1)S(1)}, f16[1,8,8,2048]{3,2,1,0:T(8,128)(2,1)S(1)}, u32[]{:S(2)}, u32[]{:S(2)}) collective-permute-start(f16[1,8,8,2048]{3,2,1,0:T(8,128)(2,1)S(1)} %get-tuple-element.45), channel_id=1, source_target_pairs={{0,128},{32,160},{64,192},{96,224},{128,0},{160,32},{192,64},{224,... | collective-permute-start | bytes 786440 | tf_op jit(solution)/shard_map/ppermute | solution.py:13
  152.1 1.5 collective-permute-done.28
  153.6 1.3 fusion.14
  154.9 2.4 %collective-permute-start.31 = (f16[8,8,2048]{2,1,0:T(8,128)(2,1)S(1)}, f16[8,8,2048]{2,1,0:T(8,128)(2,1)S(1)}, u32[]{:S(2)}, u32[]{:S(2)}) collective-permute-start(f16[8,8,2048]{2,1,0:T(8,128)(2,1)S(1)} %fusion.14), channel_id=1, source_target_pairs={{0,32},{32,0},{64,96},{96,64},{128,160},{160,128},{192,224},{224,1... | collective-permute-start | bytes 786440 | tf_op jit(solution)/shard_map/ppermute | solution.py:13
  157.3 3.0 %collective-permute-done.23 = f16[8,8,2048]{2,1,0:T(8,128)(2,1)S(1)} collective-permute-done((f16[8,8,2048]{2,1,0:T(8,128)(2,1)S(1)}, f16[8,8,2048]{2,1,0:T(8,128)(2,1)S(1)}, u32[]{:S(2)}, u32[]{:S(2)}) %collective-permute-start.23) | collective-permute-done | bytes 262176 | tf_op jit(solution)/shard_map/ppermute | solution.py:13
  160.4 1.4 bitcast_dynamic-update-slice_fusion.1
  161.8 2.5 %collective-permute-done.25 = f16[1,8,8,2048]{3,2,1,0:T(8,128)(2,1)S(1)} collective-permute-done((f16[1,8,8,2048]{3,2,1,0:T(8,128)(2,1)S(1)}, f16[1,8,8,2048]{3,2,1,0:T(8,128)(2,1)S(1)}, u32[]{:S(2)}, u32[]{:S(2)}) %collective-permute-start.25) | collective-permute-done | bytes 262176 | tf_op jit(solution)/shard_map/ppermute | solution.py:13
  164.4 7.4 %collective-permute-done.31 = f16[8,8,2048]{2,1,0:T(8,128)(2,1)S(1)} collective-permute-done((f16[8,8,2048]{2,1,0:T(8,128)(2,1)S(1)}, f16[8,8,2048]{2,1,0:T(8,128)(2,1)S(1)}, u32[]{:S(2)}, u32[]{:S(2)}) %collective-permute-start.31) | collective-permute-done | bytes 262176 | tf_op jit(solution)/shard_map/ppermute | solution.py:13
  171.8 1.4 bitcast_dynamic-update-slice_fusion
  173.2 1.0 copy-done.1
  (59 shorter events, 1.6 us)
Async XLA Ops:
  2.5 10.7 %copy-start.2 = (s32[2]{0:T(128)S(1)}, s32[2]{0:T(128)}, u32[]{:S(2)}) copy-start(s32[2]{0:T(128)} %param.5) | copy-start | bytes 28
  2.5 17.1 %collective-permute-start = (bf16[128,2048]{1,0:T(8,128)(2,1)}, bf16[128,2048]{1,0:T(8,128)(2,1)S(1)}, u32[]{:S(2)}, u32[]{:S(2)}) collective-permute-start(bf16[128,2048]{1,0:T(8,128)(2,1)} %get-tuple-element.58), channel_id=1, source_target_pairs={{0,8},{1,9},{2,10},{3,11},{4,12},{5,13},{6,14},{7,15},{8,0},{9,1},... | collective-permute-start | bytes 1572872 | tf_op jit(solution)/shard_map/ppermute | solution.py:13
  4.0 25.9 %collective-permute-start.1 = (bf16[128,2048]{1,0:T(8,128)(2,1)S(1)}, bf16[128,2048]{1,0:T(8,128)(2,1)S(1)}, u32[]{:S(2)}, u32[]{:S(2)}) collective-permute-start(bf16[128,2048]{1,0:T(8,128)(2,1)S(1)} %get-tuple-element.57), channel_id=1, source_target_pairs={{0,16},{1,17},{2,18},{3,19},{4,20},{5,21},{6,22},{7,23},{8,24},{9,... | collective-permute-start | bytes 1572872 | tf_op jit(solution)/shard_map/ppermute | solution.py:13
  6.7 25.5 %collective-permute-start.2 = (bf16[128,2048]{1,0:T(8,128)(2,1)S(1)}, bf16[128,2048]{1,0:T(8,128)(2,1)S(1)}, u32[]{:S(2)}, u32[]{:S(2)}) collective-permute-start(bf16[128,2048]{1,0:T(8,128)(2,1)S(1)} %get-tuple-element.56), channel_id=1, source_target_pairs={{0,24},{1,25},{2,26},{3,27},{4,28},{5,29},{6,30},{7,31},{8,16},{9,... | collective-permute-start | bytes 1572872 | tf_op jit(solution)/shard_map/ppermute | solution.py:13
  32.5 3.4 %collective-permute-start.3 = (bf16[2,4,2,8,2048]{4,3,2,1,0:T(8,128)(2,1)S(1)}, bf16[2,4,2,8,2048]{4,3,2,1,0:T(8,128)(2,1)S(1)}, u32[]{:S(2)}, u32[]{:S(2)}) collective-permute-start(bf16[2,4,2,8,2048]{4,3,2,1,0:T(8,128)(2,1)S(1)} %pad_maximum_fusion.2), channel_id=1, source_target_pairs={{0,1},{1,0},{2,3},{3,2},{4,5},{5,4},{6,7},{7,6},{8,9},{9,8},{10,11... | collective-permute-start | bytes 1572872 | tf_op jit(solution)/shard_map/ppermute | solution.py:13
  36.7 7.7 %collective-permute-start.12 = (f32[3,2176]{1,0:T(4,128)S(1)}, f32[3,2176]{1,0:T(4,128)S(1)}, u32[]{:S(2)}, u32[]{:S(2)}) collective-permute-start(f32[3,2176]{1,0:T(4,128)S(1)} %maximum_maximum_fusion), channel_id=1, source_target_pairs={{0,192},{32,224},{64,128},{96,160},{128,64},{160,96},{192,0},{224,... | collective-permute-start | bytes 78344 | tf_op jit(solution)/shard_map/ppermute | solution.py:13
  39.8 6.0 %collective-permute-start.11 = (f32[3,2176]{1,0:T(4,128)S(1)}, f32[3,2176]{1,0:T(4,128)S(1)}, u32[]{:S(2)}, u32[]{:S(2)}) collective-permute-start(f32[3,2176]{1,0:T(4,128)S(1)} %maximum_maximum_fusion), channel_id=1, source_target_pairs={{0,128},{32,160},{64,192},{96,224},{128,0},{160,32},{192,64},{224,... | collective-permute-start | bytes 78344 | tf_op jit(solution)/shard_map/ppermute | solution.py:13
  40.4 5.3 %collective-permute-start.10 = (f32[3,2176]{1,0:T(4,128)S(1)}, f32[3,2176]{1,0:T(4,128)S(1)}, u32[]{:S(2)}, u32[]{:S(2)}) collective-permute-start(f32[3,2176]{1,0:T(4,128)S(1)} %maximum_maximum_fusion), channel_id=1, source_target_pairs={{0,64},{32,96},{64,0},{96,32},{128,192},{160,224},{192,128},{224,1... | collective-permute-start | bytes 78344 | tf_op jit(solution)/shard_map/ppermute | solution.py:13
  40.9 18.1 %collective-permute-start.6 = (bf16[2,2,8,2048]{3,2,1,0:T(8,128)(2,1)S(1)}, bf16[2,2,8,2048]{3,2,1,0:T(8,128)(2,1)S(1)}, u32[]{:S(2)}, u32[]{:S(2)}) collective-permute-start(bf16[2,2,8,2048]{3,2,1,0:T(8,128)(2,1)S(1)} %get-tuple-element.70), channel_id=1, source_target_pairs={{0,6},{1,7},{2,4},{3,5},{4,2},{5,3},{6,0},{7,1},{8,14},{9,15},{10,... | collective-permute-start | bytes 393224 | tf_op jit(solution)/shard_map/ppermute | solution.py:13
  42.9 16.1 %collective-permute-start.5 = (bf16[2,2,8,2048]{3,2,1,0:T(8,128)(2,1)S(1)}, bf16[2,2,8,2048]{3,2,1,0:T(8,128)(2,1)S(1)}, u32[]{:S(2)}, u32[]{:S(2)}) collective-permute-start(bf16[2,2,8,2048]{3,2,1,0:T(8,128)(2,1)S(1)} %get-tuple-element.69), channel_id=1, source_target_pairs={{0,4},{1,5},{2,6},{3,7},{4,0},{5,1},{6,2},{7,3},{8,12},{9,13},{10,... | collective-permute-start | bytes 393224 | tf_op jit(solution)/shard_map/ppermute | solution.py:13
  44.4 10.2 %collective-permute-start.4 = (bf16[2,2,8,2048]{3,2,1,0:T(8,128)(2,1)S(1)}, bf16[2,2,8,2048]{3,2,1,0:T(8,128)(2,1)S(1)}, u32[]{:S(2)}, u32[]{:S(2)}) collective-permute-start(bf16[2,2,8,2048]{3,2,1,0:T(8,128)(2,1)S(1)} %get-tuple-element.67), channel_id=1, source_target_pairs={{0,2},{1,3},{2,0},{3,1},{4,6},{5,7},{6,4},{7,5},{8,10},{9,11},{10,... | collective-permute-start | bytes 393224 | tf_op jit(solution)/shard_map/ppermute | solution.py:13
  54.5 8.2 %collective-permute-start.13 = (f32[3,2176]{1,0:T(4,128)S(1)}, f32[3,2176]{1,0:T(4,128)S(1)}, u32[]{:S(2)}, u32[]{:S(2)}) collective-permute-start(f32[3,2176]{1,0:T(4,128)S(1)} %pad_maximum_fusion.5), channel_id=1, source_target_pairs={{0,32},{32,0},{64,96},{96,64},{128,160},{160,128},{192,224},{224,1... | collective-permute-start | bytes 78344 | tf_op jit(solution)/shard_map/ppermute | solution.py:13
  59.1 6.5 %collective-permute-start.7 = (bf16[2,2,8,2048]{3,2,1,0:T(8,128)(2,1)S(1)}, bf16[2,2,8,2048]{3,2,1,0:T(8,128)(2,1)S(1)}, u32[]{:S(2)}, u32[]{:S(2)}) collective-permute-start(bf16[2,2,8,2048]{3,2,1,0:T(8,128)(2,1)S(1)} %pad_maximum_fusion.4), channel_id=1, source_target_pairs={{0,2},{1,3},{2,0},{3,1},{4,6},{5,7},{6,4},{7,5},{8,10},{9,11},{10,... | collective-permute-start | bytes 393224 | tf_op jit(solution)/shard_map/ppermute | solution.py:13
  59.2 11.9 %collective-permute-start.8 = (bf16[2,2,8,2048]{3,2,1,0:T(8,128)(2,1)S(1)}, bf16[2,2,8,2048]{3,2,1,0:T(8,128)(2,1)S(1)}, u32[]{:S(2)}, u32[]{:S(2)}) collective-permute-start(bf16[2,2,8,2048]{3,2,1,0:T(8,128)(2,1)S(1)} %pad_maximum_fusion.4), channel_id=1, source_target_pairs={{0,4},{1,5},{2,6},{3,7},{4,0},{5,1},{6,2},{7,3},{8,12},{9,13},{10,... | collective-permute-start | bytes 393224 | tf_op jit(solution)/shard_map/ppermute | solution.py:13
  61.7 12.7 %collective-permute-start.9 = (bf16[2,2,8,2048]{3,2,1,0:T(8,128)(2,1)S(1)}, bf16[2,2,8,2048]{3,2,1,0:T(8,128)(2,1)S(1)}, u32[]{:S(2)}, u32[]{:S(2)}) collective-permute-start(bf16[2,2,8,2048]{3,2,1,0:T(8,128)(2,1)S(1)} %pad_maximum_fusion.4), channel_id=1, source_target_pairs={{0,6},{1,7},{2,4},{3,5},{4,2},{5,3},{6,0},{7,1},{8,14},{9,15},{10,... | collective-permute-start | bytes 393224 | tf_op jit(solution)/shard_map/ppermute | solution.py:13
  65.6 8.9 %collective-permute-start.16 = (f32[2,2,4,2,8]{4,3,2,1,0:T(2,128)S(1)}, f32[2,2,4,2,8]{4,3,2,1,0:T(2,128)S(1)}, u32[]{:S(2)}, u32[]{:S(2)}) collective-permute-start(f32[2,2,4,2,8]{4,3,2,1,0:T(2,128)S(1)} %pad_maximum_fusion.7), channel_id=1, source_target_pairs={{0,6},{1,7},{2,4},{3,5},{4,2},{5,3},{6,0},{7,1},{8,14},{9,15},{10,... | collective-permute-start | bytes 3080 | tf_op jit(solution)/shard_map/ppermute | solution.py:13
  66.6 7.9 %collective-permute-start.15 = (f32[2,2,4,2,8]{4,3,2,1,0:T(2,128)S(1)}, f32[2,2,4,2,8]{4,3,2,1,0:T(2,128)S(1)}, u32[]{:S(2)}, u32[]{:S(2)}) collective-permute-start(f32[2,2,4,2,8]{4,3,2,1,0:T(2,128)S(1)} %pad_maximum_fusion.7), channel_id=1, source_target_pairs={{0,4},{1,5},{2,6},{3,7},{4,0},{5,1},{6,2},{7,3},{8,12},{9,13},{10,... | collective-permute-start | bytes 3080 | tf_op jit(solution)/shard_map/ppermute | solution.py:13
  68.8 5.7 %collective-permute-start.14 = (f32[2,2,4,2,8]{4,3,2,1,0:T(2,128)S(1)}, f32[2,2,4,2,8]{4,3,2,1,0:T(2,128)S(1)}, u32[]{:S(2)}, u32[]{:S(2)}) collective-permute-start(f32[2,2,4,2,8]{4,3,2,1,0:T(2,128)S(1)} %pad_maximum_fusion.7), channel_id=1, source_target_pairs={{0,2},{1,3},{2,0},{3,1},{4,6},{5,7},{6,4},{7,5},{8,10},{9,11},{10,... | collective-permute-start | bytes 3080 | tf_op jit(solution)/shard_map/ppermute | solution.py:13
  76.1 26.2 %collective-permute-start.19 = (bf16[17,8,2048]{2,1,0:T(8,128)(2,1)S(1)}, bf16[17,8,2048]{2,1,0:T(8,128)(2,1)S(1)}, u32[]{:S(2)}, u32[]{:S(2)}) collective-permute-start(bf16[17,8,2048]{2,1,0:T(8,128)(2,1)S(1)} %get-tuple-element.61), channel_id=1, source_target_pairs={{0,24},{1,25},{2,26},{3,27},{4,28},{5,29},{6,30},{7,31},{8,16},{9,... | collective-permute-start | bytes 1671176 | tf_op jit(solution)/shard_map/ppermute | solution.py:13
  76.6 25.6 %collective-permute-start.18 = (bf16[17,8,2048]{2,1,0:T(8,128)(2,1)S(1)}, bf16[17,8,2048]{2,1,0:T(8,128)(2,1)S(1)}, u32[]{:S(2)}, u32[]{:S(2)}) collective-permute-start(bf16[17,8,2048]{2,1,0:T(8,128)(2,1)S(1)} %get-tuple-element.61), channel_id=1, source_target_pairs={{0,16},{1,17},{2,18},{3,19},{4,20},{5,21},{6,22},{7,23},{8,24},{9,... | collective-permute-start | bytes 1671176 | tf_op jit(solution)/shard_map/ppermute | solution.py:13
  77.2 25.6 %collective-permute-start.17 = (bf16[17,8,2048]{2,1,0:T(8,128)(2,1)S(1)}, bf16[17,8,2048]{2,1,0:T(8,128)(2,1)S(1)}, u32[]{:S(2)}, u32[]{:S(2)}) collective-permute-start(bf16[17,8,2048]{2,1,0:T(8,128)(2,1)S(1)} %get-tuple-element.61), channel_id=1, source_target_pairs={{0,8},{1,9},{2,10},{3,11},{4,12},{5,13},{6,14},{7,15},{8,0},{9,1},... | collective-permute-start | bytes 1671176 | tf_op jit(solution)/shard_map/ppermute | solution.py:13
  103.1 15.3 %collective-permute-start.24 = (bf16[4,17,8,2048]{3,2,1,0:T(8,128)(2,1)S(1)}, bf16[4,17,8,2048]{3,2,1,0:T(8,128)(2,1)}, u32[]{:S(2)}, u32[]{:S(2)}) collective-permute-start(bf16[4,17,8,2048]{3,2,1,0:T(8,128)(2,1)S(1)} %pad_maximum_fusion), channel_id=1, source_target_pairs={{0,1},{1,0},{2,3},{3,2},{4,5},{5,4},{6,7},{7,6},{8,9},{9,8},{10,11... | collective-permute-start | bytes 6684680 | tf_op jit(solution)/shard_map/ppermute | solution.py:13
  112.0 17.5 %copy-start = (f32[2,2,17,8,2048]{4,3,2,1,0:T(8,128)}, f32[2,2,17,8,2048]{4,3,2,1,0:T(8,128)S(1)}, u32[]{:S(2)}) copy-start(f32[2,2,17,8,2048]{4,3,2,1,0:T(8,128)S(1)} %fusion.5) | copy-start | bytes 13369348
  113.7 22.6 %collective-permute-start.22 = (f16[2,8,8,2048]{3,2,1,0:T(8,128)(2,1)}, f16[2,8,8,2048]{3,2,1,0:T(8,128)(2,1)S(1)}, u32[]{:S(2)}, u32[]{:S(2)}) collective-permute-start(f16[2,8,8,2048]{3,2,1,0:T(8,128)(2,1)} %get-tuple-element.52), channel_id=1, source_target_pairs={{0,192},{32,224},{64,128},{96,160},{128,64},{160,96},{192,0},{224,... | collective-permute-start | bytes 1572872 | tf_op jit(solution)/shard_map/ppermute | solution.py:13
  116.2 22.4 %collective-permute-start.21 = (f16[2,8,8,2048]{3,2,1,0:T(8,128)(2,1)}, f16[2,8,8,2048]{3,2,1,0:T(8,128)(2,1)S(1)}, u32[]{:S(2)}, u32[]{:S(2)}) collective-permute-start(f16[2,8,8,2048]{3,2,1,0:T(8,128)(2,1)} %get-tuple-element.53), channel_id=1, source_target_pairs={{0,64},{32,96},{64,0},{96,32},{128,192},{160,224},{192,128},{224,1... | collective-permute-start | bytes 1572872 | tf_op jit(solution)/shard_map/ppermute | solution.py:13
  116.4 26.4 %collective-permute-start.20 = (f16[2,8,8,2048]{3,2,1,0:T(8,128)(2,1)}, f16[2,8,8,2048]{3,2,1,0:T(8,128)(2,1)}, u32[]{:S(2)}, u32[]{:S(2)}) collective-permute-start(f16[2,8,8,2048]{3,2,1,0:T(8,128)(2,1)} %get-tuple-element.51), channel_id=1, source_target_pairs={{0,128},{32,160},{64,192},{96,224},{128,0},{160,32},{192,64},{224,... | collective-permute-start | bytes 1572872 | tf_op jit(solution)/shard_map/ppermute | solution.py:13
  133.8 15.6 %collective-permute-start.30 = (f16[1,8,8,2048]{3,2,1,0:T(8,128)(2,1)S(1)}, f16[1,8,8,2048]{3,2,1,0:T(8,128)(2,1)S(1)}, u32[]{:S(2)}, u32[]{:S(2)}) collective-permute-start(f16[1,8,8,2048]{3,2,1,0:T(8,128)(2,1)S(1)} %get-tuple-element.46), channel_id=1, source_target_pairs={{0,192},{32,224},{64,128},{96,160},{128,64},{160,96},{192,0},{224,... | collective-permute-start | bytes 786440 | tf_op jit(solution)/shard_map/ppermute | solution.py:13
  136.3 13.1 %collective-permute-start.29 = (f16[1,8,8,2048]{3,2,1,0:T(8,128)(2,1)S(1)}, f16[1,8,8,2048]{3,2,1,0:T(8,128)(2,1)S(1)}, u32[]{:S(2)}, u32[]{:S(2)}) collective-permute-start(f16[1,8,8,2048]{3,2,1,0:T(8,128)(2,1)S(1)} %get-tuple-element.47), channel_id=1, source_target_pairs={{0,64},{32,96},{64,0},{96,32},{128,192},{160,224},{192,128},{224,1... | collective-permute-start | bytes 786440 | tf_op jit(solution)/shard_map/ppermute | solution.py:13
  136.3 17.3 %collective-permute-start.28 = (f16[1,8,8,2048]{3,2,1,0:T(8,128)(2,1)S(1)}, f16[1,8,8,2048]{3,2,1,0:T(8,128)(2,1)S(1)}, u32[]{:S(2)}, u32[]{:S(2)}) collective-permute-start(f16[1,8,8,2048]{3,2,1,0:T(8,128)(2,1)S(1)} %get-tuple-element.48), channel_id=1, source_target_pairs={{0,128},{32,160},{64,192},{96,224},{128,0},{160,32},{192,64},{224,... | collective-permute-start | bytes 786440 | tf_op jit(solution)/shard_map/ppermute | solution.py:13
  144.1 16.1 %collective-permute-start.23 = (f16[8,8,2048]{2,1,0:T(8,128)(2,1)S(1)}, f16[8,8,2048]{2,1,0:T(8,128)(2,1)S(1)}, u32[]{:S(2)}, u32[]{:S(2)}) collective-permute-start(f16[8,8,2048]{2,1,0:T(8,128)(2,1)S(1)} %fusion.19), channel_id=1, source_target_pairs={{0,32},{32,0},{64,96},{96,64},{128,160},{160,128},{192,224},{224,1... | collective-permute-start | bytes 786440 | tf_op jit(solution)/shard_map/ppermute | solution.py:13
  146.7 15.1 %collective-permute-start.27 = (f16[1,8,8,2048]{3,2,1,0:T(8,128)(2,1)S(1)}, f16[1,8,8,2048]{3,2,1,0:T(8,128)(2,1)S(1)}, u32[]{:S(2)}, u32[]{:S(2)}) collective-permute-start(f16[1,8,8,2048]{3,2,1,0:T(8,128)(2,1)S(1)} %get-tuple-element.49), channel_id=1, source_target_pairs={{0,192},{32,224},{64,128},{96,160},{128,64},{160,96},{192,0},{224,... | collective-permute-start | bytes 786440 | tf_op jit(solution)/shard_map/ppermute | solution.py:13
  149.4 12.4 %collective-permute-start.26 = (f16[1,8,8,2048]{3,2,1,0:T(8,128)(2,1)S(1)}, f16[1,8,8,2048]{3,2,1,0:T(8,128)(2,1)S(1)}, u32[]{:S(2)}, u32[]{:S(2)}) collective-permute-start(f16[1,8,8,2048]{3,2,1,0:T(8,128)(2,1)S(1)} %get-tuple-element.50), channel_id=1, source_target_pairs={{0,64},{32,96},{64,0},{96,32},{128,192},{160,224},{192,128},{224,1... | collective-permute-start | bytes 786440 | tf_op jit(solution)/shard_map/ppermute | solution.py:13
  149.4 15.0 %collective-permute-start.25 = (f16[1,8,8,2048]{3,2,1,0:T(8,128)(2,1)S(1)}, f16[1,8,8,2048]{3,2,1,0:T(8,128)(2,1)S(1)}, u32[]{:S(2)}, u32[]{:S(2)}) collective-permute-start(f16[1,8,8,2048]{3,2,1,0:T(8,128)(2,1)S(1)} %get-tuple-element.45), channel_id=1, source_target_pairs={{0,128},{32,160},{64,192},{96,224},{128,0},{160,32},{192,64},{224,... | collective-permute-start | bytes 786440 | tf_op jit(solution)/shard_map/ppermute | solution.py:13
  154.9 16.9 %collective-permute-start.31 = (f16[8,8,2048]{2,1,0:T(8,128)(2,1)S(1)}, f16[8,8,2048]{2,1,0:T(8,128)(2,1)S(1)}, u32[]{:S(2)}, u32[]{:S(2)}) collective-permute-start(f16[8,8,2048]{2,1,0:T(8,128)(2,1)S(1)} %fusion.14), channel_id=1, source_target_pairs={{0,32},{32,0},{64,96},{96,64},{128,160},{160,128},{192,224},{224,1... | collective-permute-start | bytes 786440 | tf_op jit(solution)/shard_map/ppermute | solution.py:13
  173.2 1.0 copy-start.1
